TPU v7x, 32 devices: a whole 2x2x4 slice. The times are simulated.
32 devices in a mesh: tp: 4 (over y, x), dp: 8 (over z, core).
Axes of the slice: x: 2, y: 2, z: 4, core: 2. Of those that a mesh axis runs over, the one named last changes fastest.
Arguments:
- tokens: bfloat16 [8, 1024, 2048], P('dp', 'tp'), may hold values from -6 to 6
- seq_lengths: int32 [8, 3], P('dp'), may hold values from 64 to 896, as said below
- out_cotangent: bfloat16 [8, 1024, 2048], P('dp', 'tp'), may hold values from -6 to 6
- attn_norm_gain: float32 [2048], replicated, may hold values from 0.5 to 1.5
- query_weight: bfloat16 [2048, 2048], P(None, 'tp'), may hold values from -0.125 to 0.125
- key_weight: bfloat16 [2048, 2048], P(None, 'tp'), may hold values from -0.125 to 0.125
- value_weight: bfloat16 [2048, 2048], P(None, 'tp'), may hold values from -0.125 to 0.125
- out_gate_weight: bfloat16 [2048, 2048], P(None, 'tp'), may hold values from -0.125 to 0.125
- head_scalar_weight: bfloat16 [2048, 16, 2], P(None, 'tp'), may hold values from -0.125 to 0.125
- conv_weight: float32 [3, 4, 2048], P(None, None, 'tp'), may hold values from -3 to 3
- decay_log: float32 [16], P('tp'), may hold values from -6 to 1
- decay_bias: float32 [16], P('tp'), may hold values from -4 to -1
- head_norm_gain: float32 [128], replicated, may hold values from 0.5 to 1.5
- output_weight: bfloat16 [2048, 2048], P('tp'), may hold values from -0.1875 to 0.1875
- mlp_norm_gain: float32 [2048], replicated, may hold values from 0.5 to 1.5
- mlp_gate_weight: bfloat16 [2048, 5632], P(None, 'tp'), may hold values from -0.125 to 0.125
- mlp_up_weight: bfloat16 [2048, 5632], P(None, 'tp'), may hold values from -0.125 to 0.125
- mlp_down_weight: bfloat16 [5632, 2048], P('tp'), may hold values from -0.109375 to 0.109375
Outputs:
- block_output: bfloat16 [8, 1024, 2048], P('dp', 'tp')
- input_grad: bfloat16 [8, 1024, 2048], P('dp', 'tp')
- grad_attn_norm_gain: float32 [2048], replicated
- grad_query_weight: float32 [2048, 2048], P(None, 'tp')
- grad_key_weight: float32 [2048, 2048], P(None, 'tp')
- grad_value_weight: float32 [2048, 2048], P(None, 'tp')
- grad_out_gate_weight: float32 [2048, 2048], P(None, 'tp')
- grad_head_scalar_weight: float32 [2048, 16, 2], P(None, 'tp')
- grad_conv_weight: float32 [3, 4, 2048], P(None, None, 'tp')
- grad_decay_log: float32 [16], P('tp')
- grad_decay_bias: float32 [16], P('tp')
- grad_head_norm_gain: float32 [128], replicated
- grad_output_weight: float32 [2048, 2048], P('tp')
- grad_mlp_norm_gain: float32 [2048], replicated
- grad_mlp_gate_weight: float32 [2048, 5632], P(None, 'tp')
- grad_mlp_up_weight: float32 [2048, 5632], P(None, 'tp')
- grad_mlp_down_weight: float32 [5632, 2048], P('tp')
Inputs may be any that keep to these rules, and one draw needn't show every extreme that they name: `seq_lengths`: every document length is a multiple of 64; the 3 lengths of a group sum to 1024, and one of them is at least 512.
All inputs are finite; a program needn't handle non-finite values.
Results may differ from a plain program's by a relative error of at most 0.02.
Values may be sent and summed in bfloat16 or wider, within the bound.
No kernel may reach another device: no remote copies, remote signals or barrier semaphores. Data moves between devices by JAX's collectives and lax.ppermute only.
A program may use at most 320 MiB of HBM per device.

v0:
```python
from functools import partial

import jax
import jax.numpy as jnp
from jax import lax
from jax.sharding import PartitionSpec as P

HEAD_DIM = 128
CONV = 4
SPAN = 64


epsilon = 1e-06
head_epsilon = 0.001
maximum_level = lax.Precision.HIGHEST


def rms_scale(values):
    return lax.rsqrt(jnp.mean(values * values, axis=-1, keepdims=True) + epsilon)


def head_scale(values):
    return lax.rsqrt(jnp.mean(values * values, axis=-1, keepdims=True) + head_epsilon)


def doc_layout(lengths, length_sum):
    ends = jnp.cumsum(lengths)
    starts = ends - lengths
    places = jnp.arange(length_sum, dtype=jnp.int32)
    begins = jnp.sum(jnp.where(ends[None, :] <= places[:, None], lengths[None, :], 0), axis=1)
    positions = places - begins
    firsts = jnp.arange(length_sum // SPAN, dtype=jnp.int32) * SPAN
    carried = 1.0 - jnp.sum((starts[None, :] == firsts[:, None]).astype(jnp.float32), axis=1)
    return (positions, carried)


def conv_silu(values, taps, positions):
    summed = values * taps[0]
    for offset in range(1, CONV):
        moved = jnp.concatenate(
            [jnp.zeros((offset, values.shape[1]), jnp.float32), values[:-offset]], axis=0
        )
        summed = summed + moved * taps[offset] * (positions >= offset).astype(jnp.float32)[:, None]
    return jax.nn.silu(summed)


def unit_inverse(strict):
    size_here = strict.shape[-1]
    identity = jnp.eye(size_here, dtype=jnp.float32)
    result = identity - strict
    powered = strict
    for depth_level in range(1, size_here.bit_length() - 1):
        powered = jnp.einsum("hij,hjk->hik", powered, powered, precision=maximum_level)
        result = jnp.einsum("hij,hjk->hik", result, identity + powered, precision=maximum_level)
    return result


def span_rule(queries, keys_all, values_all, log_decay, writes, carried):
    rows_here, heads_here, head_width = queries.shape
    blocks = rows_here // SPAN

    def to_blocks(source):
        shaped = source.reshape((blocks, SPAN) + source.shape[1:])
        return jnp.moveaxis(shaped, 2, 1)

    places = jnp.arange(SPAN)
    lower_incl = places[:, None] >= places[None, :]
    lower_strict = places[:, None] > places[None, :]

    def block_step(current_state, inputs):
        query_tile_rows, key_block, value_block, decay_block, write_block, carry_flag = inputs
        current_state = current_state * carry_flag
        cumulative = jnp.cumsum(decay_block, axis=-1)
        gaps = cumulative[:, :, None] - cumulative[:, None, :]
        fading = jnp.where(lower_incl, jnp.exp(jnp.where(lower_incl, gaps, 0.0)), 0.0)
        key_gram = jnp.einsum("hik,hjk->hij", key_block, key_block, precision=maximum_level)
        strict = jnp.where(lower_strict, write_block[:, :, None] * key_gram * fading, 0.0)
        inverse = unit_inverse(strict)
        enlarged_state = jnp.exp(cumulative)
        weighted_rows = jnp.einsum(
            "hij,hjk->hik",
            inverse,
            (write_block * enlarged_state)[..., None] * key_block,
            precision=maximum_level,
        )
        surrogate_value = jnp.einsum(
            "hij,hjv->hiv", inverse, write_block[..., None] * value_block, precision=maximum_level
        )
        surrogate_value = surrogate_value - jnp.einsum(
            "mlz,mzx->mlx", weighted_rows, current_state, precision=maximum_level
        )
        scores = (
            jnp.einsum("hik,hjk->hij", query_tile_rows, key_block, precision=maximum_level) * fading
        )
        outputs = jnp.einsum(
            "mlz,mzx->mlx",
            query_tile_rows * enlarged_state[..., None],
            current_state,
            precision=maximum_level,
        )
        outputs = outputs + jnp.einsum(
            "hij,hjv->hiv", scores, surrogate_value, precision=maximum_level
        )
        last_sum = cumulative[:, -1]
        decayed_key_rows = key_block * jnp.exp(last_sum[:, None] - cumulative)[..., None]
        state_next = jnp.exp(last_sum)[:, None, None] * current_state + jnp.einsum(
            "mlt,mlr->mtr", decayed_key_rows, surrogate_value, precision=maximum_level
        )
        return (state_next, outputs)

    initial = jnp.zeros((heads_here, head_width, head_width), jnp.float32)
    final_state, outputs = lax.scan(
        jax.checkpoint(block_step),
        initial,
        (
            to_blocks(queries),
            to_blocks(keys_all),
            to_blocks(values_all),
            to_blocks(log_decay),
            to_blocks(writes),
            carried,
        ),
    )
    return jnp.moveaxis(outputs, 1, 2).reshape(rows_here, heads_here, head_width)


def mixer(
    positions,
    carried,
    query_proj,
    key_proj,
    value_proj,
    gate_proj,
    scalar_proj,
    conv_taps,
    decay_log,
    decay_bias,
    head_gain,
):
    rows_here = query_proj.shape[0]
    queries = conv_silu(query_proj, conv_taps[0], positions).reshape(rows_here, -1, HEAD_DIM)
    keys_all = conv_silu(key_proj, conv_taps[1], positions).reshape(rows_here, -1, HEAD_DIM)
    values_all = conv_silu(value_proj, conv_taps[2], positions).reshape(rows_here, -1, HEAD_DIM)
    queries = (
        queries
        * lax.rsqrt(jnp.sum(queries * queries, axis=-1, keepdims=True) + epsilon)
        * HEAD_DIM ** (-0.5)
    )
    keys_all = keys_all * lax.rsqrt(jnp.sum(keys_all * keys_all, axis=-1, keepdims=True) + epsilon)
    writes = jax.nn.sigmoid(scalar_proj[..., 1])
    log_decay = -jnp.exp(decay_log) * jax.nn.softplus(scalar_proj[..., 0] + decay_bias)
    mixed = span_rule(queries, keys_all, values_all, log_decay, writes, carried)
    normed = mixed * head_scale(mixed) * head_gain
    return normed.reshape(query_proj.shape) * jax.nn.silu(gate_proj)


def body(
    tokens,
    seq_lengths,
    out_cotangent,
    attn_norm_gain,
    query_weight,
    key_weight,
    value_weight,
    out_gate_weight,
    head_scalar_weight,
    conv_weight,
    decay_log,
    decay_bias,
    head_norm_gain,
    output_weight,
    mlp_norm_gain,
    mlp_gate_weight,
    mlp_up_weight,
    mlp_down_weight,
):
    inputs_local = tokens[0].astype(jnp.float32)
    local_rows = inputs_local.shape[0]
    group_rows = local_rows * lax.axis_size("tp")
    positions, carried = doc_layout(seq_lengths[0], group_rows)
    scale_in = rms_scale(inputs_local)
    unit_in = inputs_local * scale_in
    normed_local = (unit_in * attn_norm_gain).astype(jnp.bfloat16)
    normed_in = lax.all_gather(normed_local, "tp", axis=0, tiled=True)
    query_proj = jnp.dot(normed_in, query_weight, preferred_element_type=jnp.float32)
    key_proj = jnp.dot(normed_in, key_weight, preferred_element_type=jnp.float32)
    value_proj = jnp.dot(normed_in, value_weight, preferred_element_type=jnp.float32)
    gate_proj = jnp.dot(normed_in, out_gate_weight, preferred_element_type=jnp.float32)
    scalar_proj = jnp.einsum(
        "td,dhc->thc", normed_in, head_scalar_weight, preferred_element_type=jnp.float32
    )
    gated, mixer_pull = jax.vjp(
        partial(mixer, positions, carried),
        query_proj,
        key_proj,
        value_proj,
        gate_proj,
        scalar_proj,
        conv_weight,
        decay_log,
        decay_bias,
        head_norm_gain,
    )
    gated_low = gated.astype(jnp.bfloat16)
    piece = gated_low
    middle = inputs_local + lax.psum_scatter(
        jnp.dot(piece, output_weight, preferred_element_type=jnp.float32),
        "tp",
        scatter_dimension=0,
        tiled=True,
    )
    scale_mid = rms_scale(middle)
    unit_mid = middle * scale_mid
    normed_mid = lax.all_gather(
        (unit_mid * mlp_norm_gain).astype(jnp.bfloat16), "tp", axis=0, tiled=True
    )
    gate_pre = jnp.dot(normed_mid, mlp_gate_weight, preferred_element_type=jnp.float32)
    up_pre = jnp.dot(normed_mid, mlp_up_weight, preferred_element_type=jnp.float32)
    sigmoid_gate = jax.nn.sigmoid(gate_pre)
    silu_gate = gate_pre * sigmoid_gate
    hidden = (silu_gate * up_pre).astype(jnp.bfloat16)
    piece = hidden
    result = middle + lax.psum_scatter(
        jnp.dot(piece, mlp_down_weight, preferred_element_type=jnp.float32).astype(jnp.bfloat16),
        "tp",
        scatter_dimension=0,
        tiled=True,
    ).astype(jnp.float32)
    cotangent_local = out_cotangent[0]
    cotangent_all = lax.all_gather(cotangent_local, "tp", axis=0, tiled=True)
    grad_down = jnp.einsum("tf,td->fd", hidden, cotangent_all, preferred_element_type=jnp.float32)
    hidden_grad = jnp.einsum(
        "td,fd->tf", cotangent_all, mlp_down_weight, preferred_element_type=jnp.float32
    )
    gate_grad = (
        hidden_grad * up_pre * sigmoid_gate * (1.0 + gate_pre * (1.0 - sigmoid_gate))
    ).astype(jnp.bfloat16)
    up_grad = (hidden_grad * silu_gate).astype(jnp.bfloat16)
    grad_mlp_gate = jnp.einsum(
        "td,tf->df", normed_mid, gate_grad, preferred_element_type=jnp.float32
    )
    grad_mlp_up = jnp.einsum("td,tf->df", normed_mid, up_grad, preferred_element_type=jnp.float32)
    summed = jnp.einsum("tf,df->td", gate_grad, mlp_gate_weight, preferred_element_type=jnp.float32)
    mid_normed_grad = lax.psum_scatter(
        (
            summed
            + jnp.einsum("tf,df->td", up_grad, mlp_up_weight, preferred_element_type=jnp.float32)
        ).astype(jnp.bfloat16),
        "tp",
        scatter_dimension=0,
        tiled=True,
    ).astype(jnp.float32)
    gain_mid_part = jnp.sum(mid_normed_grad * unit_mid, axis=0)
    unit_grad = mid_normed_grad * mlp_norm_gain
    middle_grad = cotangent_local.astype(jnp.float32) + scale_mid * (
        unit_grad - unit_mid * jnp.mean(unit_grad * unit_mid, axis=-1, keepdims=True)
    )
    attn_grad = lax.all_gather(middle_grad.astype(jnp.bfloat16), "tp", axis=0, tiled=True)
    grad_output = jnp.einsum("tl,td->ld", gated_low, attn_grad, preferred_element_type=jnp.float32)
    gated_grad = jnp.einsum(
        "td,ld->tl", attn_grad, output_weight, preferred_element_type=jnp.float32
    )
    (
        query_grad,
        key_grad,
        value_grad,
        gate_in_grad,
        scalar_grad,
        grad_conv,
        grad_decay_log,
        grad_decay_bias,
        gain_head_part,
    ) = mixer_pull(gated_grad)
    query_low = query_grad.astype(jnp.bfloat16)
    key_low = key_grad.astype(jnp.bfloat16)
    value_low = value_grad.astype(jnp.bfloat16)
    gate_low = gate_in_grad.astype(jnp.bfloat16)
    scalar_low = scalar_grad.astype(jnp.bfloat16)
    grad_query = jnp.einsum("td,tl->dl", normed_in, query_low, preferred_element_type=jnp.float32)
    grad_key = jnp.einsum("td,tl->dl", normed_in, key_low, preferred_element_type=jnp.float32)
    grad_value = jnp.einsum("td,tl->dl", normed_in, value_low, preferred_element_type=jnp.float32)
    grad_gate = jnp.einsum("td,tl->dl", normed_in, gate_low, preferred_element_type=jnp.float32)
    grad_scalar = jnp.einsum(
        "td,thc->dhc", normed_in, scalar_low, preferred_element_type=jnp.float32
    )
    summed = jnp.einsum("tl,dl->td", query_low, query_weight, preferred_element_type=jnp.float32)
    summed = summed + jnp.einsum(
        "tl,dl->td", key_low, key_weight, preferred_element_type=jnp.float32
    )
    summed = summed + jnp.einsum(
        "tl,dl->td", value_low, value_weight, preferred_element_type=jnp.float32
    )
    summed = summed + jnp.einsum(
        "tl,dl->td", gate_low, out_gate_weight, preferred_element_type=jnp.float32
    )
    in_normed_grad = lax.psum_scatter(
        (
            summed
            + jnp.einsum(
                "thc,dhc->td", scalar_low, head_scalar_weight, preferred_element_type=jnp.float32
            )
        ).astype(jnp.bfloat16),
        "tp",
        scatter_dimension=0,
        tiled=True,
    ).astype(jnp.float32)
    gain_in_part = jnp.sum(in_normed_grad * unit_in, axis=0)
    unit_grad_in = in_normed_grad * attn_norm_gain
    input_grad = middle_grad + scale_in * (
        unit_grad_in - unit_in * jnp.mean(unit_grad_in * unit_in, axis=-1, keepdims=True)
    )
    gain_in, gain_mid, gain_head = lax.psum((gain_in_part, gain_mid_part, gain_head_part), "tp")
    (
        gain_in,
        grad_query,
        grad_key,
        grad_value,
        grad_gate,
        grad_scalar,
        grad_conv,
        grad_decay_log,
        grad_decay_bias,
        gain_head,
        grad_output,
        gain_mid,
        grad_mlp_gate,
        grad_mlp_up,
        grad_down,
    ) = (
        lax.psum(gain_in.astype(jnp.bfloat16), "dp").astype(jnp.float32),
        lax.psum(grad_query.astype(jnp.bfloat16), "dp").astype(jnp.float32),
        lax.psum(grad_key.astype(jnp.bfloat16), "dp").astype(jnp.float32),
        lax.psum(grad_value.astype(jnp.bfloat16), "dp").astype(jnp.float32),
        lax.psum(grad_gate.astype(jnp.bfloat16), "dp").astype(jnp.float32),
        lax.psum(grad_scalar.astype(jnp.bfloat16), "dp").astype(jnp.float32),
        lax.psum(grad_conv.astype(jnp.bfloat16), "dp").astype(jnp.float32),
        lax.psum(grad_decay_log.astype(jnp.bfloat16), "dp").astype(jnp.float32),
        lax.psum(grad_decay_bias.astype(jnp.bfloat16), "dp").astype(jnp.float32),
        lax.psum(gain_head.astype(jnp.bfloat16), "dp").astype(jnp.float32),
        lax.psum(grad_output.astype(jnp.bfloat16), "dp").astype(jnp.float32),
        lax.psum(gain_mid.astype(jnp.bfloat16), "dp").astype(jnp.float32),
        lax.psum(grad_mlp_gate.astype(jnp.bfloat16), "dp").astype(jnp.float32),
        lax.psum(grad_mlp_up.astype(jnp.bfloat16), "dp").astype(jnp.float32),
        lax.psum(grad_down.astype(jnp.bfloat16), "dp").astype(jnp.float32),
    )
    return (
        result.astype(jnp.bfloat16)[None],
        input_grad.astype(jnp.bfloat16)[None],
        gain_in,
        grad_query,
        grad_key,
        grad_value,
        grad_gate,
        grad_scalar,
        grad_conv,
        grad_decay_log,
        grad_decay_bias,
        gain_head,
        grad_output,
        gain_mid,
        grad_mlp_gate,
        grad_mlp_up,
        grad_down,
    )


def solution(mesh):
    return jax.shard_map(
        body,
        mesh=mesh,
        in_specs=(
            P("dp", "tp", None),
            P("dp", None),
            P("dp", "tp", None),
            P(),
            P(None, "tp"),
            P(None, "tp"),
            P(None, "tp"),
            P(None, "tp"),
            P(None, "tp", None),
            P(None, None, "tp"),
            P("tp"),
            P("tp"),
            P(),
            P("tp", None),
            P(),
            P(None, "tp"),
            P(None, "tp"),
            P("tp", None),
        ),
        out_specs=(
            P("dp", "tp", None),
            P("dp", "tp", None),
            P(),
            P(None, "tp"),
            P(None, "tp"),
            P(None, "tp"),
            P(None, "tp"),
            P(None, "tp", None),
            P(None, None, "tp"),
            P("tp"),
            P("tp"),
            P(),
            P("tp", None),
            P(),
            P(None, "tp"),
            P(None, "tp"),
            P("tp", None),
        ),
        check_vma=False,
    )
```

profile of v0, /device:TPU:1, one launch (start us, length us, event | category | flops | bytes accessed | tf_op | source)
XLA Modules:
  0.0 2117.4 jit_solution(6200180149686214485)
XLA Ops:
  12.8 54.2 %all-gather.6.cloned.1.call-done = bf16[1024,2048]{1,0:T(8,128)(2,1)} async-done(((bf16[256,2048]{1,0:T(8,128)(2,1)}), bf16[1024,2048]{1,0:T(8,128)(2,1)}) %all-gather.6.cloned.1.call-update) | async-done | bytes 4194320 | tf_op jit(solution)/shard_map/all_gather | solution.py:184
  125.5 254.7 %while.44 = (s32[]{:T(128)}, f32[4,128,128]{2,1,0:T(8,128)S(1)}, f32[16,4,64,128]{3,1,2,0:T(4,128)}, f32[16,4,128,128]{3,2,1,0:T(8,128)}, f32[16,4,64]{2,1,0:T(4...) while((s32[]{:T(128)}, f32[4,128,128]{2,1,0:T(8,128)S(1)}, ...), condition=%wide.region_8.9_spmd.clone.clone, body=%wide.region_6.8_spmd.clone.clone.sunk | while | flops 403726592 | bytes 6179130 | solution.py:112
  402.1 86.5 %reduce-scatter.5.cloned.1.call-done = f32[256,2048]{1,0:T(8,128)} async-done(((f32[1024,2048]{1,0:T(8,128)}), f32[256,2048]{1,0:T(8,128)}) %reduce-scatter.5.cloned.1.call-update) | async-done | bytes 2097168 | tf_op jit(solution)/shard_map/reduce_scatter | solution.py:206
  493.8 52.3 %all-gather.8.cloned.1.call-done = bf16[1024,2048]{1,0:T(8,128)(2,1)} async-done(((bf16[256,2048]{1,0:T(8,128)(2,1)}), bf16[1024,2048]{1,0:T(8,128)(2,1)}) %all-gather.8.cloned.1.call-update) | async-done | bytes 4194320 | tf_op jit(solution)/shard_map/all_gather | solution.py:214
  546.0 12.0 fusion.249
  558.0 10.2 fusion.250
  568.2 32.4 %all-gather.12.cloned.1.call-done = bf16[1,1024,2048]{2,1,0:T(8,128)(2,1)} async-done(((bf16[1,256,2048]{2,1,0:T(8,128)(2,1)}), bf16[1,1024,2048]{2,1,0:T(8,128)(2,1)}) %all-gather.12.cloned.1.call-update) | async-done | bytes 4194320 | tf_op jit(solution)/shard_map/all_gather | solution.py:230
  600.6 15.6 multiply_convert_fusion
  616.2 10.8 fusion.251
  627.0 11.4 add_convert_fusion
  638.5 52.8 %reduce-scatter.9.cloned.1.call-done = bf16[256,2048]{1,0:T(8,128)(2,1)} async-done(((bf16[1024,2048]{1,0:T(8,128)(2,1)}), bf16[256,2048]{1,0:T(8,128)(2,1)}) %reduce-scatter.9.cloned.1.call-update) | async-done | bytes 1048592 | tf_op jit(solution)/shard_map/reduce_scatter | solution.py:244
  703.7 46.8 %all-gather.10.cloned.1.call-done = bf16[1024,2048]{1,0:T(8,128)(2,1)} async-done(((bf16[256,2048]{1,0:T(8,128)(2,1)}), bf16[1024,2048]{1,0:T(8,128)(2,1)}) %all-gather.10.cloned.1.call-update) | async-done | bytes 4194320 | tf_op jit(solution)/shard_map/all_gather | solution.py:258
  750.5 8.7 multiply_reduce_fusion.7
  782.8 542.7 %while.43 = (s32[]{:T(128)}, f32[4,128,128]{2,1,0:T(8,128)}, f32[16,4,64,128]{3,2,1,0:T(8,128)}, f32[16,4,64,128]{3,2,1,0:T(8,128)}, f32[16,4,64,128]{3,2,1,0:T(...) while((s32[]{:T(128)}, f32[4,128,128]{2,1,0:T(8,128)}, ...), condition=%wide.region_28.29_spmd.clone, body=%wide.region_16.28_spmd.clone.sunk | while | flops 1085278208 | bytes 20863532 | solution.py:112
  1355.8 8.8 multiply_reduce_fusion.15
  1364.7 7.5 multiply_reduce_fusion.18
  1403.7 13.7 fusion.151
  1417.5 10.9 convolution_convert_fusion.3
  1428.5 10.8 convolution_convert_fusion
  1439.3 8.7 convolution_convert_fusion.2
  1448.0 8.9 convolution_convert_fusion.1
  1482.9 13.0 all-reduce.36
  1495.9 26.6 %all-reduce.37 = (bf16[2048,4,2]{0,1,2:T(4,128)(2,1)S(1)}, bf16[2048]{0:T(1024)(128)(2,1)S(1)}, bf16[3,4,512]{2,1,0:T(4,128)(2,1)S(1)}, bf16[4]{0:T(256)(128)(2,...) all-reduce(bf16[2048,4,2]{0,1,2:T(4,128)(2,1)S(1)} %fusion.167, ...), channel_id=1, replica_groups=mesh['tp'=4,'dp'=8] {'dp'}, use_global_device_ids=true, to_apply=%region_40.41 | all-reduce | flops 26760 | bytes 107040 | tf_op jit(solution)/shard_map/psum | solution.py:335
  1532.5 545.0 %all-reduce.41.cloned.1.call-done = (bf16[2048,512]{1,0:T(8,128)(2,1)}, bf16[2048,512]{1,0:T(8,128)(2,1)}, bf16[2048,512]{1,0:T(8,128)(2,1)}, bf16[2048,512]{1,0...) async-done(((bf16[2048,512]{1,0:T(8,128)(2,1)}, bf16[2048,512]{1,0:T(8,128)(2,1)}, ...) | async-done | bytes 27787280 | tf_op jit(solution)/shard_map/psum | solution.py:331
  (2111 shorter events, 1043.8 us)
Async XLA Ops:
  7.2 389.1 %copy-start = (bf16[512,2048]{1,0:T(8,128)(2,1)S(1)}, bf16[512,2048]{1,0:T(8,128)(2,1)}, u32[]{:S(2)}) copy-start(bf16[512,2048]{1,0:T(8,128)(2,1)} %param.35) | copy-start | bytes 6291460
  7.3 59.7 %all-gather.6.cloned.1.call-start = ((), (), s32[]{:S(2)}) async-start(), calls=%async_computation.4 | async-start | bytes 5242880 | tf_op jit(solution)/shard_map/all_gather | solution.py:184
  12.0 476.6 %reduce-scatter.5.cloned.1.call-start = ((), (), s32[]{:S(2)}) async-start(), calls=%async_computation.5 | async-start | bytes 10485760 | tf_op jit(solution)/shard_map/reduce_scatter | solution.py:206
  12.5 112.9 %copy-start.103 = (f32[4]{0:T(128)}, f32[4]{0:T(128)S(1)}, u32[]{:S(2)}) copy-start(f32[4]{0:T(128)S(1)} %exponential_negate_fusion) | copy-start | bytes 52
  12.6 88.7 %copy-start.60 = (f32[1024]{0:T(1024)}, f32[1024]{0:T(1024)S(1)}, u32[]{:S(2)}) copy-start(f32[1024]{0:T(1024)S(1)} %get-tuple-element.1088) | copy-start | bytes 12292
  12.6 88.7 %copy-start.62 = (f32[1024]{0:T(1024)}, f32[1024]{0:T(1024)S(1)}, u32[]{:S(2)}) copy-start(f32[1024]{0:T(1024)S(1)} %get-tuple-element.1086) | copy-start | bytes 12292
  12.6 88.7 %copy-start.64 = (f32[1024]{0:T(1024)}, f32[1024]{0:T(1024)S(1)}, u32[]{:S(2)}) copy-start(f32[1024]{0:T(1024)S(1)} %get-tuple-element.1087) | copy-start | bytes 12292
  12.6 65.8 %copy-start.72 = (f32[1,1,512]{2,1,0:T(1,128)}, f32[1,1,512]{2,1,0:T(1,128)S(1)}, u32[]{:S(2)}) copy-start(f32[1,1,512]{2,1,0:T(1,128)S(1)} %get-tuple-element.1062) | copy-start | bytes 6148
  12.7 65.8 %copy-start.74 = (f32[1,1,512]{2,1,0:T(1,128)}, f32[1,1,512]{2,1,0:T(1,128)S(1)}, u32[]{:S(2)}) copy-start(f32[1,1,512]{2,1,0:T(1,128)S(1)} %get-tuple-element.1063) | copy-start | bytes 6148
  12.7 65.8 %copy-start.76 = (f32[1,1,512]{2,1,0:T(1,128)}, f32[1,1,512]{2,1,0:T(1,128)S(1)}, u32[]{:S(2)}) copy-start(f32[1,1,512]{2,1,0:T(1,128)S(1)} %get-tuple-element.1064) | copy-start | bytes 6148
  12.7 88.6 %copy-start.84 = (f32[1,1,512]{2,1,0:T(1,128)}, f32[1,1,512]{2,1,0:T(1,128)S(1)}, u32[]{:S(2)}) copy-start(f32[1,1,512]{2,1,0:T(1,128)S(1)} %get-tuple-element.1058) | copy-start | bytes 6148
  12.7 88.6 %copy-start.86 = (f32[1,1,512]{2,1,0:T(1,128)}, f32[1,1,512]{2,1,0:T(1,128)S(1)}, u32[]{:S(2)}) copy-start(f32[1,1,512]{2,1,0:T(1,128)S(1)} %get-tuple-element.1059) | copy-start | bytes 6148
  12.7 88.6 %copy-start.88 = (f32[1,1,512]{2,1,0:T(1,128)}, f32[1,1,512]{2,1,0:T(1,128)S(1)}, u32[]{:S(2)}) copy-start(f32[1,1,512]{2,1,0:T(1,128)S(1)} %get-tuple-element.1060) | copy-start | bytes 6148
  12.8 88.6 %copy-start.94 = (f32[1,1,512]{2,1,0:T(1,128)}, f32[1,1,512]{2,1,0:T(1,128)S(1)}, u32[]{:S(2)}) copy-start(f32[1,1,512]{2,1,0:T(1,128)S(1)} %get-tuple-element.1061) | copy-start | bytes 6148
  402.1 86.6 %copy-start.13 = (bf16[1,256,2048]{2,1,0:T(8,128)(2,1)S(1)}, bf16[1,256,2048]{2,1,0:T(8,128)(2,1)}, u32[]{:S(2)}) copy-start(bf16[1,256,2048]{2,1,0:T(8,128)(2,1)} %param.22) | copy-start | bytes 3145732
  402.1 89.8 %copy-start.55 = (f32[2048]{0:T(1024)S(1)}, f32[2048]{0:T(1024)}, u32[]{:S(2)}) copy-start(f32[2048]{0:T(1024)} %param.36) | copy-start | bytes 24580
  402.1 143.9 %all-gather.8.cloned.1.call-start = ((), (), s32[]{:S(2)}) async-start(), calls=%async_computation.6 | async-start | bytes 5242880 | tf_op jit(solution)/shard_map/all_gather | solution.py:214
  490.6 204.1 %copy-start.69 = (f32[256]{0:T(256)}, f32[256]{0:T(256)S(1)}, u32[]{:S(2)}) copy-start(f32[256]{0:T(256)S(1)} %add_rsqrt_fusion.2) | copy-start | bytes 3076
  493.1 107.5 %all-gather.12.cloned.1.call-start = ((), (), s32[]{:S(2)}) async-start(), calls=%async_computation.11 | async-start | bytes 5242880 | tf_op jit(solution)/shard_map/all_gather | solution.py:230
  493.7 197.6 %reduce-scatter.9.cloned.1.call-start = ((), (), s32[]{:S(2)}) async-start(), calls=%async_computation.8 | async-start | bytes 5242880 | tf_op jit(solution)/shard_map/reduce_scatter | solution.py:244
  638.4 112.1 %all-gather.10.cloned.1.call-start = ((), (), s32[]{:S(2)}) async-start(), calls=%async_computation.9 | async-start | bytes 5242880 | tf_op jit(solution)/shard_map/all_gather | solution.py:258
  697.6 782.6 %reduce-scatter.11.cloned.1.call-start = ((), (), s32[]{:S(2)}) async-start(), calls=%async_computation.10 | async-start | bytes 5242880 | tf_op jit(solution)/shard_map/reduce_scatter | solution.py:296
  1417.5 110.3 %reduce-scatter.7.cloned.1.call-start = ((), (), s32[]{:S(2)}) async-start(), calls=%async_computation.7 | async-start | bytes 5242880 | tf_op jit(solution)/shard_map/reduce_scatter | solution.py:223
  1428.4 649.2 %all-reduce.41.cloned.1.call-start = ((), (), s32[]{:S(2)}) async-start(), calls=%async_computation.12 | async-start | bytes 55574528 | tf_op jit(solution)/shard_map/psum | solution.py:331
  (112 other events, 1156.6 us)
Sparse Core Ops, SparseCore 0:
  12.1 54.7 all-gather.5
  402.2 86.3 reduce-scatter.4
  493.3 52.7 all-gather.7
  547.9 52.6 all-gather.11
  638.6 52.6 reduce-scatter.8
  697.8 52.6 all-gather.9
  1417.6 52.6 reduce-scatter.10
  1474.1 53.6 reduce-scatter.6
  1533.0 544.5 all-reduce.40
where the time goes:
time: 2130 us; the launch traced here: 2120 us
  waiting for transfers between devices  872 us (41%)
  matrix products  809 us (38%)
  local copies, waits for them, and re-layouts  192 us (9%)
  other arithmetic  179 us (8%)
  blocking collectives  39.7 us (2%)
    psum x1, waiting for transfers between devices, body(): lax.psum(grad_query.astype(jnp.bfloat16), 'dp').astype(jnp.float32)  545 us
    dot_general x320, matrix products, unit_inverse(): jnp.einsum('hij,hjk->hik', powered, powered, precision=maximum_level)  109 us
    dot_general x320, matrix products, unit_inverse(): jnp.einsum('hij,hjk->hik', result, identity + powered, precision=maximum_...  104 us
    reduce_scatter x1, waiting for transfers between devices, body(): lax.psum_scatter(jnp.dot(piece, output_weight, preferred_element_type=jnp...  86.5 us
    dot_general x64, matrix products, block_step(): jnp.einsum('mlz,mzx->mlx', weighted_rows, current_state, precision=maximu...  83.4 us
    dot_general x48, matrix products, block_step(): jnp.einsum('mlz,mzx->mlx', query_tile_rows * enlarged_state[..., None], c...  63.5 us
    all_gather x1, waiting for transfers between devices, body(): normed_in = lax.all_gather(normed_local, 'tp', axis=0, tiled=True)  54.2 us
    dot_general x48, matrix products, block_step(): jnp.einsum('mlt,mlr->mtr', decayed_key_rows, surrogate_value, precision=m...  53.7 us
  transfers between devices with their start and end apart: 9, of which 8 were waited for; matrix products, arithmetic and copies ran while one was open for 5% of the time, Pallas kernels for 0%

commit v1 on v0

v1 whole, which is shorter than its diff:
```python
from functools import partial

import jax
import jax.numpy as jnp
from jax import lax
from jax.experimental import pallas as pl
from jax.experimental.pallas import tpu as pltpu
from jax.sharding import PartitionSpec as P

HEAD_DIM = 128
CONV = 4
SPAN = 64
TILE = 2 * SPAN
VMEM_BYTES = 48 * 1024 * 1024
epsilon = 1e-06
head_epsilon = 0.001
f32 = jnp.float32
bf16 = jnp.bfloat16


def dot(left, right, dims=((1,), (0,)), precise=False):
    return lax.dot_general(
        left, right, (dims, ((), ())), preferred_element_type=f32,
        precision=lax.Precision.HIGHEST if precise else None,
    )


def iota(shape, axis):
    return lax.broadcasted_iota(jnp.int32, shape, axis)


def spread(packed):
    left = iota(packed.shape, 1) < SPAN
    none = jnp.zeros_like(packed)
    return jnp.concatenate([jnp.where(left, packed, none), jnp.where(left, none, packed)], axis=0)


def halves(full):
    left = iota((SPAN, TILE), 1) < SPAN
    return jnp.where(left, full[:SPAN], full[SPAN:])


def packed_masks():
    row, col = iota((SPAN, TILE), 0), iota((SPAN, TILE), 1) % SPAN
    return row, col


def unit_inverse(stricts):
    row, col = packed_masks()
    near = (row // 2) == (col // 2)
    eye = jnp.where(row == col, 1.0, 0.0)
    results = [eye - jnp.where(near, strict, 0.0) for strict in stricts]
    width = 2
    while width < SPAN:
        inside = ((row // (2 * width)) == (col // (2 * width))) & ((row // width) != (col // width))
        pieces = [jnp.where(inside, strict, 0.0).astype(bf16) for strict in stricts]
        kept = [result.astype(bf16) for result in results]
        moved = [dot(piece, spread(keep)) for piece, keep in zip(pieces, kept)]
        results = [result - dot(keep, spread(move.astype(bf16))) for result, keep, move in zip(results, kept, moved)]
        width *= 2
    return results


def softplus(value):
    return jnp.maximum(value, 0.0) + jnp.log1p(jnp.exp(-jnp.abs(value)))


def row_places(first, rows, starts_ref):
    place = iota((rows, HEAD_DIM), 0) + first
    one, two = starts_ref[1], starts_ref[2]
    start = jnp.where(place >= two, two, jnp.where(place >= one, one, 0))
    end = jnp.where(place >= two, 1 << 30, jnp.where(place >= one, two, one))
    return place, start, end


def carry_flag(first, starts_ref):
    fresh = (first == 0) | (first == starts_ref[1]) | (first == starts_ref[2])
    return jnp.where(fresh, 0.0, 1.0).astype(f32)


def decay_parts(scalars, rates, biases):
    row, col = iota((TILE, TILE), 0), iota((TILE, TILE), 1)
    running = jnp.where((row >= col) & ((row // SPAN) == (col // SPAN)), 1.0, 0.0)
    log_decay = -jnp.exp(rates) * softplus(scalars + biases)
    total = dot(running, log_decay, precise=True)
    return log_decay, total, total.T


def fading_of(total, total_rows, head):
    row, col = packed_masks()
    left = iota((SPAN, TILE), 1) < SPAN
    column = jnp.broadcast_to(total[:, head:head + 1], (TILE, TILE))
    gaps = jnp.where(left, column[:SPAN], column[SPAN:]) - total_rows[head:head + 1, :]
    incl = row >= col
    return jnp.where(incl, jnp.exp(jnp.where(incl, gaps, 0.0)), 0.0)


def last_rows(total, head):
    ends = [jnp.broadcast_to(total[SPAN * i + SPAN - 1:SPAN * (i + 1), head:head + 1], (SPAN, TILE)) for i in range(2)]
    return jnp.concatenate(ends, axis=0)


def forward_kernel(tiles, heads, starts_ref, q_ref, k_ref, v_ref, gate_ref, sp_ref, taps_ref, rate_ref, bias_ref, gain_ref,
                   gated_ref, mixed_ref, cq_ref, ck_ref, cv_ref, inv_ref, qk_ref, gram_ref, w_ref, u_ref, s_ref,
                   ext_ref, state_ref):
    step = pl.program_id(0)
    rows = tiles * TILE

    @pl.when(step == 0)
    def _():
        ext_ref[:, :8, :] = jnp.zeros((3, 8, heads * HEAD_DIM), f32)
        state_ref[...] = jnp.zeros(state_ref.shape, f32)

    ones = jnp.ones((HEAD_DIM, HEAD_DIM), bf16)
    place, start, _ = row_places(step * rows, rows, starts_ref)
    position = place - start
    masks = [jnp.where(position >= j, 1.0, 0.0) for j in range(1, CONV)]
    for which, source in enumerate((q_ref, k_ref, v_ref)):
        ext_ref[which, 8:8 + rows, :] = source[...].astype(f32)

    def activated(which, head, out):
        lanes = slice(head * HEAD_DIM, (head + 1) * HEAD_DIM)
        conv = ext_ref[which, 8:8 + rows, lanes] * taps_ref[which * CONV:which * CONV + 1, lanes]
        for j in range(1, CONV):
            conv = conv + ext_ref[which, 8 - j:8 - j + rows, lanes] * masks[j - 1] * taps_ref[which * CONV + j:which * CONV + j + 1, lanes]
        low = conv.astype(bf16)
        out[:, lanes] = low
        conv = low.astype(f32)
        return conv * jax.nn.sigmoid(conv)

    active = [[activated(which, h, out) for h in range(heads)] for which, out in enumerate((cq_ref, ck_ref, cv_ref))]
    norms = [[dot((one * one).astype(bf16), ones) for one in active[which]] for which in range(2)]
    queries = [one * (lax.rsqrt(norm + epsilon) * HEAD_DIM ** -0.5) for one, norm in zip(active[0], norms[0])]
    keys = [one * lax.rsqrt(norm + epsilon) for one, norm in zip(active[1], norms[1])]
    values = active[2]
    for which in range(3):
        ext_ref[which, :8, :] = ext_ref[which, rows:rows + 8, :]

    lanes_of = lambda head: slice(head * HEAD_DIM, (head + 1) * HEAD_DIM)
    row, col = packed_masks()
    left = iota((SPAN, TILE), 1) < SPAN
    pairs = [(tile, head) for tile in range(tiles) for head in range(heads)]
    spans = [slice(tile * TILE, (tile + 1) * TILE) for tile in range(tiles)]
    packs = [slice(tile * SPAN, (tile + 1) * SPAN) for tile in range(tiles)]
    scalars = [sp_ref[span, :] for span in spans]
    decays = [decay_parts(one, rate_ref[...], bias_ref[...]) for one in scalars]
    writes = [jax.nn.sigmoid(one) for one in scalars]
    grams = []
    for tile, head in pairs:
        k_low = keys[head][spans[tile]].astype(bf16)
        grams.append(dot(jnp.concatenate([queries[head][spans[tile]].astype(bf16), k_low], axis=0), k_low, ((1,), (1,))))
    stricts, scores, spread_writes, columns = [], [], [], []
    for (tile, head), both in zip(pairs, grams):
        _, total, total_rows = decays[tile]
        write = jnp.broadcast_to(writes[tile][:, heads + head:heads + head + 1], (TILE, HEAD_DIM))
        column = jnp.broadcast_to(total[:, head:head + 1], (TILE, HEAD_DIM))
        gaps = jnp.where(left, column[:SPAN], column[SPAN:]) - total_rows[head:head + 1, :]
        fading = jnp.where(row >= col, jnp.exp(jnp.where(row >= col, gaps, 0.0)), 0.0)
        qk, gram = halves(both[:TILE]), halves(both[TILE:])
        qk_ref[packs[tile], lanes_of(head)] = qk.astype(bf16)
        gram_ref[packs[tile], lanes_of(head)] = gram.astype(bf16)
        write_pack = jnp.where(left, write[:SPAN], write[SPAN:])
        stricts.append(jnp.where(row > col, write_pack * gram * fading, 0.0))
        scores.append(spread((qk * fading).astype(bf16)))
        spread_writes.append(write)
        columns.append(column)
    inverses = [one.astype(bf16) for one in unit_inverse(stricts)]
    weighted, free, q_grown, k_tail, ends = [], [], [], [], []
    for (tile, head), inverse, write, column in zip(pairs, inverses, spread_writes, columns):
        total = decays[tile][1]
        q, k, v = queries[head][spans[tile]], keys[head][spans[tile]], values[head][spans[tile]]
        grown = jnp.exp(column)
        tails = jnp.exp(last_rows(total, head) - column)
        inv_ref[packs[tile], lanes_of(head)] = inverse
        sides = jnp.concatenate([(write * grown * k).astype(bf16), (write * v).astype(bf16)], axis=1)
        solved = dot(spread(inverse), sides)
        low = solved[:, :HEAD_DIM].astype(bf16)
        w_ref[spans[tile], lanes_of(head)] = low
        weighted.append(low)
        free.append(solved[:, HEAD_DIM:])
        q_grown.append((q * grown).astype(bf16))
        k_tail.append((k * tails).astype(bf16))
        ends.append([jnp.exp(total[SPAN * i + SPAN - 1:SPAN * (i + 1), head:head + 1]) for i in range(2)])

    states = [state_ref[head] for head in range(heads)]
    for tile in range(tiles):
        at = tile * heads
        seen, changes = [[] for _ in range(heads)], [[] for _ in range(heads)]
        for i in range(2):
            flag = carry_flag(step * rows + tile * TILE + i * SPAN, starts_ref)
            states = [state * flag for state in states]
            lows = [state.astype(bf16) for state in states]
            base = (tile * 2 + i) * HEAD_DIM
            part = slice(i * SPAN, (i + 1) * SPAN)
            both = [dot(jnp.concatenate([weighted[at + h][part], q_grown[at + h][part]], axis=0), lows[h]) for h in range(heads)]
            new = [(free[at + h][part] - both[h][:SPAN]).astype(bf16) for h in range(heads)]
            states = [ends[at + h][i] * states[h] + dot(k_tail[at + h][part], new[h], ((0,), (0,))) for h in range(heads)]
            for h in range(heads):
                s_ref[base:base + HEAD_DIM, lanes_of(h)] = lows[h]
                seen[h].append(both[h][SPAN:])
                changes[h].append(new[h])
        change = [jnp.concatenate(parts, axis=0) for parts in changes]
        mixed = [jnp.concatenate(seen[h], axis=0) + dot(scores[at + h], change[h]) for h in range(heads)]
        squares = [dot((one * one).astype(bf16), ones) * (1.0 / HEAD_DIM) for one in mixed]
        for h in range(heads):
            u_ref[spans[tile], lanes_of(h)] = change[h]
            mixed_ref[spans[tile], lanes_of(h)] = mixed[h].astype(bf16)
            normed = mixed[h] * lax.rsqrt(squares[h] + head_epsilon) * gain_ref[...]
            gate = gate_ref[spans[tile], lanes_of(h)].astype(f32)
            gated_ref[spans[tile], lanes_of(h)] = (normed * gate * jax.nn.sigmoid(gate)).astype(bf16)
    for h in range(heads):
        state_ref[h] = states[h]


def blocked(rows, width, place):
    return pl.BlockSpec((rows, width), lambda i, s: (place(i) ^ s[0], 0))


def constant(shape):
    return pl.BlockSpec(shape, lambda i, s: (0,) * len(shape))


def mixer_forward(starts, q, k, v, gate, sp, taps, rate, bias, gain):
    rows, width = q.shape
    heads = width // HEAD_DIM
    block = rows // 4
    tiles = block // TILE
    spec = lambda r, w: blocked(r, w, lambda i: i)
    wide, half, state = spec(block, width), spec(block // 2, width), spec(block * 2, width)
    shape = lambda r: jax.ShapeDtypeStruct((r, width), bf16)
    return pl.pallas_call(
        partial(forward_kernel, tiles, heads),
        grid_spec=pltpu.PrefetchScalarGridSpec(
            num_scalar_prefetch=1,
            grid=(4,),
            in_specs=[wide] * 4 + [spec(block, HEAD_DIM)] + [constant(a.shape) for a in (taps, rate, bias, gain)],
            out_specs=[wide] * 5 + [half] * 3 + [wide] * 2 + [state],
            scratch_shapes=[pltpu.VMEM((3, block + 8, width), f32), pltpu.VMEM((heads, HEAD_DIM, HEAD_DIM), f32)],
        ),
        out_shape=[shape(rows)] * 5 + [shape(rows // 2)] * 3 + [shape(rows)] * 2 + [shape(rows * 2)],
        compiler_params=pltpu.CompilerParams(dimension_semantics=("arbitrary",), vmem_limit_bytes=VMEM_BYTES),
        cost_estimate=pl.CostEstimate(flops=10 * 10**9, bytes_accessed=16 * 10**6, transcendentals=10**6),
    )(starts, q, k, v, gate, sp, taps, rate, bias, gain)


def row_sums(product, ones_tall):
    high = product.astype(bf16)
    low = (product - high.astype(f32)).astype(bf16)
    return dot(jnp.concatenate([high, low], axis=1), ones_tall)


def backward_kernel(tiles, heads, starts_ref, gg_ref, mixed_ref, gate_ref, cq_ref, ck_ref, cv_ref, q_ref, k_ref, v_ref, sp_ref,
                    inv_ref, qk_ref, gram_ref, w_ref, u_ref, s_ref, taps_ref, rate_ref, bias_ref, gain_ref,
                    dq_ref, dk_ref, dv_ref, dgate_ref, dsp_ref, dtaps_ref, dmisc_ref, ext_ref, state_ref):
    step = pl.num_programs(0) - 1 - pl.program_id(0)
    rows = tiles * TILE

    @pl.when(pl.program_id(0) == 0)
    def _():
        ext_ref[:, rows:, :] = jnp.zeros((3, 8, heads * HEAD_DIM), f32)
        state_ref[...] = jnp.zeros(state_ref.shape, f32)
        dtaps_ref[...] = jnp.zeros(dtaps_ref.shape, f32)
        dmisc_ref[...] = jnp.zeros(dmisc_ref.shape, f32)

    ones = jnp.ones((HEAD_DIM, HEAD_DIM), bf16)
    ones_tall = jnp.ones((2 * HEAD_DIM, HEAD_DIM), bf16)
    lanes_of = lambda head: slice(head * HEAD_DIM, (head + 1) * HEAD_DIM)
    row, col = packed_masks()
    left = iota((SPAN, TILE), 1) < SPAN
    full_row, full_col = iota((TILE, TILE), 0), iota((TILE, TILE), 1)
    same = (full_row // SPAN) == (full_col // SPAN)
    pairs = [(tile, head) for tile in range(tiles) for head in range(heads)]
    spans = [slice(tile * TILE, (tile + 1) * TILE) for tile in range(tiles)]
    packs = [slice(tile * SPAN, (tile + 1) * SPAN) for tile in range(tiles)]
    gain = gain_ref[...]

    mixed = [mixed_ref[spans[t], lanes_of(h)].astype(f32) for t, h in pairs]
    squares = [dot((one * one).astype(bf16), ones) * (1.0 / HEAD_DIM) for one in mixed]
    partial_gain = jnp.zeros((1, HEAD_DIM), f32)
    scales, pulled, inner = [], [], []
    for (t, h), one, square in zip(pairs, mixed, squares):
        scale = lax.rsqrt(square + head_epsilon)
        gate = gate_ref[spans[t], lanes_of(h)].astype(f32)
        grad = gg_ref[spans[t], lanes_of(h)].astype(f32)
        sig = jax.nn.sigmoid(gate)
        unit = one * scale
        dgate_ref[spans[t], lanes_of(h)] = (grad * unit * gain * (sig * (1.0 + gate * (1.0 - sig)))).astype(bf16)
        norm_grad = grad * gate * sig
        partial_gain = partial_gain + jnp.sum(norm_grad * unit, axis=0, keepdims=True)
        norm_grad = norm_grad * gain
        scales.append(scale)
        pulled.append(norm_grad)
        inner.append(dot((norm_grad * unit).astype(bf16), ones) * (1.0 / HEAD_DIM))
    dmisc_ref[2:3, :] = dmisc_ref[2:3, :] + partial_gain
    dout = [(scale * (grad - one * scale * mean)).astype(bf16) for scale, grad, one, mean in zip(scales, pulled, mixed, inner)]

    def silu_parts(ref, t, h):
        conv = ref[spans[t], lanes_of(h)].astype(f32)
        sig = jax.nn.sigmoid(conv)
        return conv * sig, sig * (1.0 + conv * (1.0 - sig))

    raw_q = [silu_parts(cq_ref, t, h) for t, h in pairs]
    raw_k = [silu_parts(ck_ref, t, h) for t, h in pairs]
    norm_q = [lax.rsqrt(dot((one[0] * one[0]).astype(bf16), ones) + epsilon) for one in raw_q]
    norm_k = [lax.rsqrt(dot((one[0] * one[0]).astype(bf16), ones) + epsilon) for one in raw_k]
    decays = [decay_parts(sp_ref[span, :], rate_ref[...], bias_ref[...]) for span in spans]
    writes = [jax.nn.sigmoid(sp_ref[span, :]) for span in spans]
    queries, keys, fadings, growns, tails, spread_writes, write_packs, ends = [], [], [], [], [], [], [], []
    for n, (t, h) in enumerate(pairs):
        _, total, total_rows = decays[t]
        queries.append(raw_q[n][0] * (norm_q[n] * HEAD_DIM ** -0.5))
        keys.append(raw_k[n][0] * norm_k[n])
        write = jnp.broadcast_to(writes[t][:, heads + h:heads + h + 1], (TILE, HEAD_DIM))
        column = jnp.broadcast_to(total[:, h:h + 1], (TILE, HEAD_DIM))
        gaps = jnp.where(left, column[:SPAN], column[SPAN:]) - total_rows[h:h + 1, :]
        fadings.append(jnp.where(row >= col, jnp.exp(jnp.where(row >= col, gaps, 0.0)), 0.0))
        growns.append(jnp.exp(column))
        tails.append(jnp.exp(last_rows(total, h) - column))
        spread_writes.append(write)
        write_packs.append(jnp.where(left, write[:SPAN], write[SPAN:]))
        ends.append([jnp.exp(total[SPAN * i + SPAN - 1:SPAN * (i + 1), h:h + 1]) for i in range(2)])
    qk = [qk_ref[packs[t], lanes_of(h)].astype(f32) for t, h in pairs]
    score_grads = [dot(spread((qk[n] * fadings[n]).astype(bf16)), dout[n], ((0,), (0,))) for n in range(len(pairs))]
    q_grown = [(queries[n] * growns[n]).astype(bf16) for n in range(len(pairs))]
    k_tail = [(keys[n] * tails[n]).astype(bf16) for n in range(len(pairs))]
    parts = [slice(0, SPAN), slice(SPAN, TILE)]
    q_outs = [[dot(q_grown[n][part], dout[n][part], ((0,), (0,))) for part in parts] for n in range(len(pairs))]

    states = [state_ref[h] for h in range(heads)]
    change_grads = [[None, None] for _ in pairs]
    tail_grads = [[None, None] for _ in pairs]
    end_grads = [[None, None] for _ in pairs]
    for t in reversed(range(tiles)):
        for i in (1, 0):
            part = parts[i]
            here = slice(t * TILE + i * SPAN, t * TILE + (i + 1) * SPAN)
            at = slice((t * 2 + i) * HEAD_DIM, (t * 2 + i + 1) * HEAD_DIM)
            flag = carry_flag(step * rows + t * TILE + i * SPAN, starts_ref)
            lows = [one.astype(bf16) for one in states]
            news = []
            for h in range(heads):
                n = t * heads + h
                news.append((score_grads[n][part] + dot(k_tail[n][part], lows[h])).astype(bf16))
            for h in range(heads):
                n = t * heads + h
                change_grads[n][i] = news[h]
                tail_grads[n][i] = dot(u_ref[here, lanes_of(h)], lows[h], ((1,), (1,)))
                held = jnp.sum(states[h] * s_ref[at, lanes_of(h)].astype(f32), axis=0, keepdims=True)
                end_grads[n][i] = ends[n][i] * jnp.sum(held, axis=1, keepdims=True)
            states = [
                flag * (ends[t * heads + h][i] * states[h] + q_outs[t * heads + h][i] - dot(w_ref[here, lanes_of(h)], news[h], ((0,), (0,))))
                for h in range(heads)
            ]
    for h in range(heads):
        state_ref[h] = states[h]

    change_grads = [jnp.concatenate(one, axis=0) for one in change_grads]
    side_grads = [dot(spread(inv_ref[packs[t], lanes_of(h)]), change_grads[n], ((0,), (0,))) for n, (t, h) in enumerate(pairs)]
    side_low = [one.astype(bf16) for one in side_grads]
    crossed = []
    for n, (t, h) in enumerate(pairs):
        through = []
        for i, part in enumerate(parts):
            at = slice((t * 2 + i) * HEAD_DIM, (t * 2 + i + 1) * HEAD_DIM)
            through.append(dot(jnp.concatenate([side_low[n][part], dout[n][part]], axis=0), s_ref[at, lanes_of(h)], ((1,), (1,))))
        grams = dot(jnp.concatenate([dout[n], side_low[n]], axis=0), u_ref[spans[t], lanes_of(h)], ((1,), (1,)))
        crossed.append((through, grams))
    query_grads, key_grads = [], []
    flat_q = [one.astype(bf16) for one in queries]
    flat_k = [one.astype(bf16) for one in keys]
    products = []
    for n, (t, h) in enumerate(pairs):
        through, grams = crossed[n]
        weighted_grad = -jnp.concatenate([one[:SPAN] for one in through], axis=0)
        grown_grad = jnp.concatenate([one[SPAN:] for one in through], axis=0)
        gram = gram_ref[packs[t], lanes_of(h)].astype(f32)
        pair_grad = halves(grams[:TILE]) * fadings[n]
        strict_grad = jnp.where(row > col, -halves(grams[TILE:]), 0.0) * fadings[n]
        gram_grad = strict_grad * write_packs[n]
        matrix = jnp.concatenate([spread(pair_grad.astype(bf16)), spread(gram_grad.astype(bf16))], axis=0)
        forward = dot(matrix, flat_k[n])
        backward = dot(matrix, jnp.concatenate([flat_q[n], flat_k[n]], axis=0), ((0,), (0,)))
        tail_grad = jnp.concatenate(tail_grads[n], axis=0)
        grown_key = growns[n] * keys[n]
        write = spread_writes[n]
        query_grads.append(forward[:TILE] + grown_grad * growns[n])
        key_grads.append(forward[TILE:] + backward + tail_grad * tails[n] + weighted_grad * write * growns[n])
        value = cv_ref[spans[t], lanes_of(h)].astype(f32)
        value = value * jax.nn.sigmoid(value)
        moving = pair_grad * qk[n] + gram_grad * gram
        inner_key = weighted_grad * grown_key
        products.append((
            spread(strict_grad * gram) + inner_key + side_grads[n] * value,
            spread(moving) + grown_grad * growns[n] * queries[n] + inner_key * write,
            tail_grad * tails[n] * keys[n],
            jnp.sum(moving, axis=0, keepdims=True),
        ))
    sums = [[row_sums(one, ones_tall) for one in three[:3]] for three in products]
    upper = jnp.where((full_row <= full_col) & same, 1.0, 0.0)
    lower = jnp.where((full_row > full_col) & same, 1.0, 0.0)
    for t in range(tiles):
        gap_grad = jnp.zeros((TILE, HEAD_DIM), f32)
        tail_sum = jnp.zeros((TILE, HEAD_DIM), f32)
        write_grad = jnp.zeros((TILE, HEAD_DIM), f32)
        ends_grad = jnp.zeros((TILE, HEAD_DIM), f32)
        across = jnp.zeros((TILE, HEAD_DIM), f32)
        for h in range(heads):
            n = t * heads + h
            mine = full_col == h
            gap_grad = jnp.where(mine, sums[n][1], gap_grad)
            tail_sum = jnp.where(mine, sums[n][2], tail_sum)
            write_grad = jnp.where(full_col == heads + h, sums[n][0], write_grad)
            across = jnp.where(full_row == h, products[n][3], across)
            ends_grad = jnp.where(mine, jnp.where(full_row < SPAN, end_grads[n][0], end_grads[n][1]), ends_grad)
        log_grad = dot(upper, gap_grad - across.T, precise=True) + dot(lower, tail_sum, precise=True) + ends_grad
        scalars = sp_ref[spans[t], :]
        rate = -jnp.exp(rate_ref[...])
        inside = log_grad * rate * jax.nn.sigmoid(scalars + bias_ref[...])
        write = writes[t]
        out = jnp.where(full_col < heads, inside, write_grad * write * (1.0 - write))
        dsp_ref[spans[t], :] = jnp.where(full_col < 2 * heads, out, 0.0).astype(bf16)
        dmisc_ref[0:1, :] = dmisc_ref[0:1, :] + jnp.sum(log_grad * decays[t][0], axis=0, keepdims=True)
        dmisc_ref[1:2, :] = dmisc_ref[1:2, :] + jnp.sum(inside, axis=0, keepdims=True)

    inner_q = [dot((query_grads[n] * raw_q[n][0]).astype(bf16), ones) for n in range(len(pairs))]
    inner_k = [dot((key_grads[n] * raw_k[n][0]).astype(bf16), ones) for n in range(len(pairs))]
    for n, (t, h) in enumerate(pairs):
        scale = norm_q[n]
        grad = (query_grads[n] - raw_q[n][0] * (scale * scale * inner_q[n])) * (scale * HEAD_DIM ** -0.5)
        ext_ref[0, spans[t], lanes_of(h)] = grad * raw_q[n][1]
        scale = norm_k[n]
        grad = (key_grads[n] - raw_k[n][0] * (scale * scale * inner_k[n])) * scale
        ext_ref[1, spans[t], lanes_of(h)] = grad * raw_k[n][1]
        ext_ref[2, spans[t], lanes_of(h)] = side_grads[n] * spread_writes[n] * silu_parts(cv_ref, t, h)[1]
    place, _, end = row_places(step * rows, rows, starts_ref)
    masks = [None] + [jnp.where(place + j < end, 1.0, 0.0) for j in range(1, CONV)]
    for which, (source, out) in enumerate(((q_ref, dq_ref), (k_ref, dk_ref), (v_ref, dv_ref))):
        for h in range(heads):
            lanes = lanes_of(h)
            proj = source[:, lanes].astype(f32)
            total = None
            for j in range(CONV):
                moved = ext_ref[which, j:j + rows, lanes]
                if j:
                    moved = moved * masks[j]
                at = which * CONV + j
                dtaps_ref[at:at + 1, lanes] = dtaps_ref[at:at + 1, lanes] + jnp.sum(proj * moved, axis=0, keepdims=True)
                term = moved * taps_ref[at:at + 1, lanes]
                total = term if total is None else total + term
            out[:, lanes] = total.astype(bf16)
        ext_ref[which, rows:, :] = ext_ref[which, :8, :]


def mixer_backward(starts, gg, gate, q, k, v, sp, kept, taps, rate, bias, gain):
    mixed, cq, ck, cv, inv, qk, gram, w, u, s = kept
    rows, width = q.shape
    heads = width // HEAD_DIM
    block = rows // 4
    tiles = block // TILE
    spec = lambda r, w: blocked(r, w, lambda i: 3 - i)
    wide, half, state, scal = spec(block, width), spec(block // 2, width), spec(block * 2, width), spec(block, HEAD_DIM)
    shape = lambda r: jax.ShapeDtypeStruct((r, width), bf16)
    return pl.pallas_call(
        partial(backward_kernel, tiles, heads),
        grid_spec=pltpu.PrefetchScalarGridSpec(
            num_scalar_prefetch=1,
            grid=(4,),
            in_specs=[wide] * 9 + [scal] + [half] * 3 + [wide] * 2 + [state] + [constant(a.shape) for a in (taps, rate, bias, gain)],
            out_specs=[wide] * 4 + [scal, constant((3 * CONV, width)), constant((8, HEAD_DIM))],
            scratch_shapes=[pltpu.VMEM((3, block + 8, width), f32), pltpu.VMEM((heads, HEAD_DIM, HEAD_DIM), f32)],
        ),
        out_shape=[shape(rows)] * 4
        + [
            jax.ShapeDtypeStruct((rows, HEAD_DIM), bf16),
            jax.ShapeDtypeStruct((3 * CONV, width), f32),
            jax.ShapeDtypeStruct((8, HEAD_DIM), f32),
        ],
        compiler_params=pltpu.CompilerParams(dimension_semantics=("arbitrary",), vmem_limit_bytes=VMEM_BYTES),
        cost_estimate=pl.CostEstimate(flops=20 * 10**9, bytes_accessed=24 * 10**6, transcendentals=10**6),
    )(starts, gg, mixed, gate, cq, ck, cv, q, k, v, sp, inv, qk, gram, w, u, s, taps, rate, bias, gain)


def xor_pairs(size, mask):
    return [(i, i ^ mask) for i in range(size)]


def tied(first, *rest):
    return lax.optimization_barrier((first,) + rest)


def gather_rows(mine):
    size = lax.axis_size("tp")
    half = mine.shape[0] // 2
    across = lax.ppermute(mine, "tp", xor_pairs(size, 1))
    down = lax.ppermute(mine, "tp", xor_pairs(size, 2))
    far_top = lax.ppermute(down[:half], "tp", xor_pairs(size, 1))
    far_low = lax.ppermute(across[half:], "tp", xor_pairs(size, 2))
    return [mine, across, down, jnp.concatenate([far_top, far_low], axis=0)]


def scatter_rows(parts):
    size = lax.axis_size("tp")
    mine, across, down, far = parts
    half = mine.shape[0] // 2
    far_top = lax.ppermute(far[:half], "tp", xor_pairs(size, 1))
    far_low = lax.ppermute(far[half:], "tp", xor_pairs(size, 2))
    down = jnp.concatenate([down[:half] + far_top, down[half:]], axis=0)
    across = jnp.concatenate([across[:half], across[half:] + far_low], axis=0)
    return (
        mine.astype(f32)
        + lax.ppermute(across, "tp", xor_pairs(size, 1)).astype(f32)
        + lax.ppermute(down, "tp", xor_pairs(size, 2)).astype(f32)
    )


def sum_small(values, axis):
    size, mask = lax.axis_size(axis), 1
    while mask < size:
        values = values + lax.ppermute(values, axis, xor_pairs(size, mask))
        mask *= 2
    return values


def line_sums(chunks):
    size = lax.axis_size("dp")
    stride = size // 4
    hops = [
        [(j, j + stride) for j in range(stride)] + [(j + 3 * stride, j + 2 * stride) for j in range(stride)],
        [(j + stride, j + 2 * stride) for j in range(stride)] + [(j + 2 * stride, j + stride) for j in range(stride)],
        [(j + stride, j) for j in range(stride)] + [(j + 2 * stride, j + 3 * stride) for j in range(stride)],
    ]
    place = lax.axis_index("dp") // stride
    center = (place == 1) | (place == 2)
    chunks = list(chunks)
    count = len(chunks)
    sums, wholes, results = {}, {}, []
    gone = ()
    for step in range(count + 2):
        going = []
        if step < count:
            chunk = chunks[step]
            mask = 2
            while mask < stride:
                chunk = chunk + lax.ppermute(chunk, "dp", xor_pairs(size, mask))
                mask *= 2
            going.append((0, step, chunk))
        if 0 <= step - 1 < count:
            going.append((1, step - 1, sums.pop(step - 1)))
        if 0 <= step - 2 < count:
            going.append((2, step - 2, wholes.pop(step - 2)))
        held = lax.optimization_barrier(tuple(one[2] for one in going) + gone)
        gone = ()
        for (stage, which, _), value in zip(going, held):
            moved = lax.ppermute(value, "dp", hops[stage])
            gone += (moved,)
            if stage == 0:
                sums[which] = value + moved
            elif stage == 1:
                wholes[which] = value + moved
            else:
                results.append(jnp.where(center, value, moved))
    return results


def core_sum(keep, send):
    return keep + lax.ppermute(send, "dp", xor_pairs(lax.axis_size("dp"), 1))


def core_join(part, axis, first):
    other = lax.ppermute(part, "dp", xor_pairs(lax.axis_size("dp"), 1))
    low = jnp.where(first, part, other)
    high = jnp.where(first, other, part)
    return jnp.concatenate([low, high], axis=axis).astype(f32)


def rms_scale(values):
    return lax.rsqrt(jnp.mean(values * values, axis=-1, keepdims=True) + epsilon)


def product(left, right):
    return jnp.dot(left, right, preferred_element_type=f32)


def product_t(left, right):
    return jnp.einsum("td,ld->tl", left, right, preferred_element_type=f32)


def outer(left, right):
    return jnp.einsum("ta,tb->ab", left, right, preferred_element_type=f32).astype(bf16)


def body(
    tokens,
    seq_lengths,
    out_cotangent,
    attn_norm_gain,
    query_weight,
    key_weight,
    value_weight,
    out_gate_weight,
    head_scalar_weight,
    conv_weight,
    decay_log,
    decay_bias,
    head_norm_gain,
    output_weight,
    mlp_norm_gain,
    mlp_gate_weight,
    mlp_up_weight,
    mlp_down_weight,
):
    width = tokens.shape[2]
    half = width // 2
    heads = decay_log.shape[0]
    first_core = lax.axis_index("dp") % 2 == 0
    rank = lax.axis_index("tp").astype(jnp.int32)
    lengths = seq_lengths[0]
    starts = jnp.stack([rank, lengths[0], lengths[0] + lengths[1]])

    def mine_first(values):
        low, high = values[:, :half], values[:, half:]
        return jnp.where(first_core, low, high), jnp.where(first_core, high, low)

    token_parts = gather_rows(tokens[0])
    weight_part = jnp.where(first_core, output_weight[:, :half], output_weight[:, half:])
    weight_part, _ = tied(weight_part, token_parts[3])
    weight_mine = jnp.concatenate(gather_rows(weight_part), axis=0)
    weight_other = lax.ppermute(weight_mine, "dp", xor_pairs(lax.axis_size("dp"), 1))
    weight_full = jnp.concatenate(
        [jnp.where(first_core, weight_mine, weight_other), jnp.where(first_core, weight_other, weight_mine)], axis=1
    )
    cotangent_part, _ = tied(out_cotangent[0], weight_mine)

    scalar_weight = jnp.pad(
        jnp.transpose(head_scalar_weight, (0, 2, 1)).reshape(width, 2 * heads), ((0, 0), (0, HEAD_DIM - 2 * heads))
    )
    pad_row = lambda row: jnp.pad(row, (0, HEAD_DIM - heads))[None]
    rates, biases = pad_row(decay_log), pad_row(decay_bias)
    taps = conv_weight.reshape(3 * CONV, -1)
    inputs = jnp.concatenate(token_parts, axis=0).astype(f32)
    scale_in = rms_scale(inputs)
    normed_in = (inputs * scale_in * attn_norm_gain).astype(bf16)
    query_proj = product(normed_in, query_weight).astype(bf16)
    key_proj = product(normed_in, key_weight).astype(bf16)
    value_proj = product(normed_in, value_weight).astype(bf16)
    gate_proj = product(normed_in, out_gate_weight).astype(bf16)
    scalar_proj = product(normed_in, scalar_weight)
    gated, *kept = mixer_forward(
        starts, query_proj, key_proj, value_proj, gate_proj, scalar_proj, taps, rates, biases, head_norm_gain[None]
    )
    rows = tokens.shape[1]
    order = lambda values, mask: jnp.concatenate([values[(m ^ mask) * rows:((m ^ mask) + 1) * rows] for m in range(4)], axis=0)
    gated_parts = gather_rows(gated)
    gated_full = jnp.concatenate([order(part, mask) for mask, part in enumerate(gated_parts)], axis=1)
    middle = inputs + product(gated_full, weight_full)
    scale_mid = rms_scale(middle)
    normed_mid = (middle * scale_mid * mlp_norm_gain).astype(bf16)

    gate_pre = product(normed_mid, mlp_gate_weight)
    up_pre = product(normed_mid, mlp_up_weight)
    sigmoid_gate = jax.nn.sigmoid(gate_pre)
    silu_gate = gate_pre * sigmoid_gate
    hidden = (silu_gate * up_pre).astype(bf16)
    cotangent_part, _ = tied(cotangent_part, gated_parts[3])
    cotangent_all = jnp.concatenate(gather_rows(cotangent_part), axis=0)
    cot_keep, cot_send = mine_first(cotangent_all)
    down_sum = core_sum(outer(hidden, cot_keep), outer(hidden, cot_send))
    hidden_grad = product_t(cotangent_all, mlp_down_weight)
    gate_grad = (hidden_grad * up_pre * sigmoid_gate * (1.0 + gate_pre * (1.0 - sigmoid_gate))).astype(bf16)
    up_grad = (hidden_grad * silu_gate).astype(bf16)
    split = lambda values: [values[m * rows:(m + 1) * rows] for m in range(4)]
    mid_partial = (product_t(gate_grad, mlp_gate_weight) + product_t(up_grad, mlp_up_weight)).astype(bf16)
    mid_normed_grad = scatter_rows(split(mid_partial))
    mid_keep, mid_send = mine_first(normed_mid)
    gate_sum = core_sum(outer(mid_keep, gate_grad), outer(mid_send, gate_grad))
    up_sum = core_sum(outer(mid_keep, up_grad), outer(mid_send, up_grad))

    middle_mine, scale_mine = middle[:rows], scale_mid[:rows]
    unit_mid = middle_mine * scale_mine
    gain_mid = jnp.sum(mid_normed_grad * unit_mid, axis=0)
    unit_grad = mid_normed_grad * mlp_norm_gain
    middle_grad = out_cotangent[0].astype(f32) + scale_mine * (
        unit_grad - unit_mid * jnp.mean(unit_grad * unit_mid, axis=-1, keepdims=True)
    )
    attn_grad = jnp.concatenate(gather_rows(middle_grad.astype(bf16)), axis=0)
    gated_grad = product_t(attn_grad, output_weight).astype(bf16)
    result_partial, _ = tied(product(hidden, mlp_down_weight).astype(bf16), attn_grad)
    result = middle_mine + scatter_rows(split(result_partial))
    attn_keep, attn_send = mine_first(attn_grad)
    out_sum = core_sum(outer(gated, attn_keep), outer(gated, attn_send))
    query_low, key_low, value_low, gate_low, scalar_low, grad_taps, misc = mixer_backward(
        starts, gated_grad, gate_proj, query_proj, key_proj, value_proj, scalar_proj, kept, taps, rates, biases, head_norm_gain[None]
    )
    in_keep, in_send = mine_first(normed_in)
    gate_proj_sum = core_sum(outer(in_keep, gate_low), outer(in_send, gate_low))
    query_sum = core_sum(outer(in_keep, query_low), outer(in_send, query_low))
    key_sum = core_sum(outer(in_keep, key_low), outer(in_send, key_low))
    value_sum = core_sum(outer(in_keep, value_low), outer(in_send, value_low))
    in_partial = (
        product_t(query_low, query_weight)
        + product_t(key_low, key_weight)
        + product_t(value_low, value_weight)
        + product_t(gate_low, out_gate_weight)
        + product_t(scalar_low, scalar_weight)
    ).astype(bf16)
    in_normed_grad = scatter_rows(split(in_partial))
    unit_in = inputs[:rows] * scale_in[:rows]
    gain_in = jnp.sum(in_normed_grad * unit_in, axis=0)
    unit_grad_in = in_normed_grad * attn_norm_gain
    input_grad = middle_grad + scale_in[:rows] * (
        unit_grad_in - unit_in * jnp.mean(unit_grad_in * unit_in, axis=-1, keepdims=True)
    )

    cut = lambda values: jnp.split(values, 2, axis=0)
    down_low, down_high = cut(down_sum)
    gate_top, gate_low_rows = cut(gate_sum)
    up_top, up_low_rows = cut(up_sum)
    even = line_sums([down_low, gate_top, up_top, out_sum, query_sum, value_sum])
    odd = line_sums([down_high, gate_low_rows, up_low_rows, gate_proj_sum, key_sum])
    join = lambda part, axis: core_join(part, axis, first_core)
    grad_down = join(jnp.concatenate([even[0], odd[0]], axis=0), 1)
    grad_mlp_gate = join(jnp.concatenate([even[1], odd[1]], axis=0), 0)
    grad_mlp_up = join(jnp.concatenate([even[2], odd[2]], axis=0), 0)
    grad_output = join(even[3], 1)
    grad_gate = join(odd[3], 0)
    grad_query = join(even[4], 0)
    grad_key = join(odd[4], 0)
    grad_value = join(even[5], 0)

    scalar_grad = jnp.einsum("td,tl->dl", normed_in, scalar_low, preferred_element_type=f32)[:, :2 * heads]
    shared = jnp.concatenate([gain_in, gain_mid, misc[2]])
    shared = sum_small(shared, "tp")
    small = jnp.concatenate([scalar_grad.reshape(-1), grad_taps.reshape(-1), misc[0, :heads], misc[1, :heads], shared])
    small = sum_small(small, "dp")
    pieces = []
    at = 0
    for size in (width * 2 * heads, grad_taps.size, heads, heads, width, width, HEAD_DIM):
        pieces.append(small[at:at + size])
        at += size
    scalar_sum, taps_sum, log_sum, bias_sum, gain_in, gain_mid, gain_head = pieces
    return (
        result.astype(bf16)[None],
        input_grad.astype(bf16)[None],
        gain_in,
        grad_query,
        grad_key,
        grad_value,
        grad_gate,
        jnp.transpose(scalar_sum.reshape(width, 2, heads), (0, 2, 1)),
        taps_sum.reshape(conv_weight.shape),
        log_sum,
        bias_sum,
        gain_head,
        grad_output,
        gain_mid,
        grad_mlp_gate,
        grad_mlp_up,
        grad_down,
    )


def solution(mesh):
    return jax.shard_map(
        body,
        mesh=mesh,
        in_specs=(
            P("dp", "tp", None),
            P("dp", None),
            P("dp", "tp", None),
            P(),
            P(None, "tp"),
            P(None, "tp"),
            P(None, "tp"),
            P(None, "tp"),
            P(None, "tp", None),
            P(None, None, "tp"),
            P("tp"),
            P("tp"),
            P(),
            P("tp", None),
            P(),
            P(None, "tp"),
            P(None, "tp"),
            P("tp", None),
        ),
        out_specs=(
            P("dp", "tp", None),
            P("dp", "tp", None),
            P(),
            P(None, "tp"),
            P(None, "tp"),
            P(None, "tp"),
            P(None, "tp"),
            P(None, "tp", None),
            P(None, None, "tp"),
            P("tp"),
            P("tp"),
            P(),
            P("tp", None),
            P(),
            P(None, "tp"),
            P(None, "tp"),
            P("tp", None),
        ),
        check_vma=False,
    )
```

time: 2130 us -> 900 us (0.42)
  waiting for transfers between devices: 872 us -> 209 us
  matrix products: 809 us -> 203 us
  starting transfers between devices: 0.37 us -> 200 us
  local copies, waits for them, and re-layouts: 192 us -> 64 us
  Pallas kernels: 0 us -> 56.4 us
  blocking collectives: 39.7 us -> 0 us
  other arithmetic: 179 us -> 152 us
    dot_general x1131 -> x34, matrix products: 809 us -> 201 us  [the longest x9 80.9 us: product_t(): return jnp.einsum('td,ld->tl', left, right, preferred_element_type=f32)]
    psum x1 -> x0, waiting for transfers between devices: 545 us -> none  [body(): lax.psum(grad_query.astype(jnp.bfloat16), 'dp').astype(jnp.float32)]
    ppermute x0 -> x87, waiting for transfers between devices: none -> 209 us  [the longest x33 87.8 us: line_sums(): moved = lax.ppermute(value, 'dp', hops[stage])]
    ppermute x0 -> x87, starting transfers between devices: none -> 200 us  [the longest x33 75.2 us: line_sums(): moved = lax.ppermute(value, 'dp', hops[stage])]
    all_gather x4 -> x0, waiting for transfers between devices: 186 us -> none  [the longest x1 54.2 us: body(): normed_in = lax.all_gather(normed_local, 'tp', axis=0, tiled=True)]
    reduce_scatter x4 -> x0, waiting for transfers between devices: 141 us -> none  [the longest x1 86.5 us: body(): lax.psum_scatter(jnp.dot(piece, output_weight, preferred_element_type=jnp...]
    pallas_call x0 -> x2, Pallas kernels: none -> 56.4 us  [the longest x1 32.8 us: mixer_backward(): pl.pallas_call(partial(backward_kernel, tiles, heads), grid_spec=pltpu.Pr...]
    reduce_sum x80 -> x2, other arithmetic: 55.8 us -> 3.44 us  [the longest x1 2.52 us: body(): gain_in = jnp.sum(in_normed_grad * unit_in, axis=0)]
  transfers between devices with their start and end apart: 9 -> 87, of which waited for: 8 -> 30; matrix products, arithmetic and copies ran while one was open for 5% -> 36% of each run, Pallas kernels for 0% -> 6%
where the time goes in v1:
time: 900 us; the launch traced here: 889 us
  waiting for transfers between devices  209 us (23%)
  matrix products  203 us (23%)
  starting transfers between devices  200 us (22%)
  other arithmetic  152 us (17%)
  local copies, waits for them, and re-layouts  64 us (7%)
  Pallas kernels  56.4 us (6%)
    ppermute x33, waiting for transfers between devices, line_sums(): moved = lax.ppermute(value, 'dp', hops[stage])  87.8 us
    dot_general x9, matrix products, product_t(): return jnp.einsum('td,ld->tl', left, right, preferred_element_type=f32)  80.9 us
    ppermute x33, starting transfers between devices, line_sums(): moved = lax.ppermute(value, 'dp', hops[stage])  75.2 us
    ppermute x5, waiting for transfers between devices, gather_rows(): down = lax.ppermute(mine, 'tp', xor_pairs(size, 2))  68.7 us
    dot_general x9, matrix products, product(): return jnp.dot(left, right, preferred_element_type=f32)  61.9 us
    dot_general x16, matrix products, outer(): jnp.einsum('ta,tb->ab', left, right, preferred_element_type=f32)  58.4 us
    ppermute x8, starting transfers between devices, core_join(): other = lax.ppermute(part, 'dp', xor_pairs(lax.axis_size('dp'), 1))  39.2 us
    ppermute x8, starting transfers between devices, core_sum(): return keep + lax.ppermute(send, 'dp', xor_pairs(lax.axis_size('dp'), 1))  39 us
  transfers between devices with their start and end apart: 87, of which 30 were waited for; matrix products, arithmetic and copies ran while one was open for 36% of the time, Pallas kernels for 6%

profile of v1, /device:TPU:1, one launch (start us, length us, event | category | flops | bytes accessed | tf_op | source)
XLA Modules:
  0.0 888.6 jit_solution(2972879315432717063)
XLA Ops:
  11.3 16.4 %collective-permute-done.9 = bf16[512,1024]{1,0:T(8,128)(2,1)} collective-permute-done((bf16[512,1024]{1,0:T(8,128)(2,1)S(1)}, bf16[512,1024]{1,0:T(8,128)(2,1)}, u32[]{:S(2)}, u32[]{:S(2)}) %collective-permute-start.9) | collective-permute-done | bytes 1048608 | tf_op jit(solution)/shard_map/ppermute | solution.py:495
  32.3 17.8 %collective-permute-done.1 = bf16[256,2048]{1,0:T(8,128)(2,1)} collective-permute-done((bf16[256,2048]{1,0:T(8,128)(2,1)}, bf16[256,2048]{1,0:T(8,128)(2,1)}, u32[]{:S(2)}, u32[]{:S(2)}) %collective-permute-start.1) | collective-permute-done | bytes 1048608 | tf_op jit(solution)/shard_map/ppermute | solution.py:495
  91.0 23.5 %shard_map.305 = (bf16[1024,512]{1,0:T(8,128)(2,1)S(1)}, bf16[1024,512]{1,0:T(8,128)(2,1)S(1)}, bf16[1024,512]{1,0:T(8,128)(2,1)S(1)}, bf16[1024,512]{1,0:T(8,12...) custom-call(s32[3]{0:T(128)S(1)} %pad_add_fusion.starts_ref, ...), custom_call_target="tpu_custom_call" | custom-call | flops 10000000000 | bytes 16000000 | tf_op jit(solution)/shard_map/pallas_call | solution.py:231
  132.8 9.0 %collective-permute-done.5 = bf16[1024,512]{1,0:T(8,128)(2,1)} collective-permute-done((bf16[1024,512]{1,0:T(8,128)(2,1)S(1)}, bf16[1024,512]{1,0:T(8,128)(2,1)}, u32[]{:S(2)}, u32[]{:S(2)}) %collective-permute-start.5) | collective-permute-done | bytes 1048608 | tf_op jit(solution)/shard_map/ppermute | solution.py:495
  146.5 17.8 %collective-permute-done.14 = bf16[256,2048]{1,0:T(8,128)(2,1)} collective-permute-done((bf16[256,2048]{1,0:T(8,128)(2,1)}, bf16[256,2048]{1,0:T(8,128)(2,1)}, u32[]{:S(2)}, u32[]{:S(2)}) %collective-permute-start.14) | collective-permute-done | bytes 1048608 | tf_op jit(solution)/shard_map/ppermute | solution.py:495
  172.8 14.2 %collective-permute-done.15 = bf16[128,2048]{1,0:T(8,128)(2,1)S(1)} collective-permute-done((bf16[128,2048]{1,0:T(8,128)(2,1)S(1)}, bf16[128,2048]{1,0:T(8,128)(2,1)S(1)}, u32[]{:S(2)}, u32[]{:S(2)}) %collective-permute-start.15) | collective-permute-done | bytes 524320 | tf_op jit(solution)/shard_map/ppermute | solution.py:496
  195.6 17.8 %multiply_reduce_fusion = (f32[1024]{0:T(1024)S(1)}, f32[1024,2048]{1,0:T(8,128)}) fusion(bf16[2048,1024]{1,0:T(8,128)(2,1)} %get-tuple-element.147, bf16[2048,1024]{1,0:T(8,128)(2,1)} %get-tuple-element.146, bf16[256,512]{1,0:T(8,128)(2,1)} %get-tuple-element.199, bf16[256,512]{1,0:T(8,128)(2,1)S(1)} %get-tuple-element.198, ...), kind=kOutput, calls=%fused_computation.7 | convolution fusion | flops 8661236736 | bytes 25169920 | tf_op jit(solution)/shard_map/dot_general | solution.py:581
  217.6 10.4 %fusion.88 = f32[1024,1408]{1,0:T(8,128)} fusion(bf16[1024,2048]{1,0:T(8,128)(2,1)S(1)} %multiply_convert_fusion, bf16[2048,1408]{1,0:T(8,128)(2,1)} %param.33), kind=kOutput, calls=%fused_computation.208 | convolution fusion | flops 5905580032 | bytes 15728640 | tf_op jit(solution)/shard_map/dot_general | solution.py:581
  228.0 8.5 fusion.89
  236.5 16.2 %multiply_convert_fusion.2 = (bf16[1024,1408]{1,0:T(8,128)(2,1)}, bf16[1024,1408]{1,0:T(8,128)(2,1)S(1)}, bf16[1024,1408]{1,0:T(8,128)(2,1)}) fusion(f32[1024,1408]{1,0:T(8,128)} %fusion.88, f32[1024,1408]{1,0:T(8,128)} %fusion.89, bf16[1024,2048]{1,0:T(8,128)(2,1)} %copy-done.73, bf16[1408,2048]{1,0:T(8,128)(2,1)} %param.35), kind=kOutput, calls=%fused_computation.14 | convolution fusion | flops 5927206912 | bytes 30146560 | tf_op jit(solution)/shard_map/td,ld->tl/dot_general | solution.py:585
  252.7 11.8 %fusion.90 = f32[1024,2048]{1,0:T(8,128)} fusion(bf16[1024,1408]{1,0:T(8,128)(2,1)S(1)} %get-tuple-element.144, bf16[2048,1408]{1,0:T(8,128)(2,1)} %param.33), kind=kOutput, calls=%fused_computation.210 | convolution fusion | flops 5905580032 | bytes 17039360 | tf_op jit(solution)/shard_map/td,ld->tl/dot_general | solution.py:585
  264.5 10.7 %add_convert_fusion.1 = bf16[1024,2048]{1,0:T(8,128)(2,1)S(1)} fusion(f32[1024,2048]{1,0:T(8,128)} %fusion.90, bf16[1024,1408]{1,0:T(8,128)(2,1)S(1)} %copy-done.100, bf16[2048,1408]{1,0:T(8,128)(2,1)} %param.34), kind=kOutput, calls=%fused_computation.5 | convolution fusion | flops 5909774336 | bytes 21233664 | tf_op jit(solution)/shard_map/td,ld->tl/dot_general | solution.py:585
  314.2 10.8 %convolution_convert_fusion = bf16[1024,2048]{1,0:T(8,128)(2,1)} fusion(bf16[1024,1408]{1,0:T(8,128)(2,1)} %get-tuple-element.145, bf16[1408,2048]{1,0:T(8,128)(2,1)} %param.35), kind=kOutput, calls=%fused_computation.42 | convolution fusion | flops 5907677184 | bytes 12845056 | tf_op jit(solution)/shard_map/dot_general | solution.py:581
  367.4 32.8 %shard_map.306 = (bf16[1024,512]{1,0:T(8,128)(2,1)S(1)}, bf16[1024,512]{1,0:T(8,128)(2,1)S(1)}, bf16[1024,512]{1,0:T(8,128)(2,1)S(1)}, bf16[1024,512]{1,0:T(8,12...) custom-call(s32[3]{0:T(128)S(1)} %copy-done.2, ...), custom_call_target="tpu_custom_call" | custom-call | flops 20000000000 | bytes 24000000 | tf_op jit(solution)/shard_map/pallas_call | solution.py:463
  425.3 13.8 %add_convert_fusion = bf16[1024,2048]{1,0:T(8,128)(2,1)} fusion(f32[1024,2048]{1,0:T(8,128)} %fusion.94, f32[1024,2048]{1,0:T(8,128)} %fusion.93, f32[1024,2048]{1,0:T(8,128)} %fusion.91, f32[1024,2048]{1,0:T(8,128)} %fusion.92, bf16[1024,128]{1,0:T(8,128)(2,1)S(1)} %get-tuple-element.85, bf16[2048,8]{0,1:T(8,128)(2,1)S(1)} %copy-done.76), kind=kOutput, calls=%fused_computation.4 | convolution fusion | flops 547356672 | bytes 38043648 | tf_op jit(solution)/shard_map/td,ld->tl/dot_general | solution.py:585
  454.9 18.5 %collective-permute-start.38 = (bf16[1024,512]{1,0:T(8,128)(2,1)S(1)}, bf16[1024,512]{1,0:T(8,128)(2,1)S(1)}, u32[]{:S(2)}, u32[]{:S(2)}) collective-permute-start(bf16[1024,512]{1,0:T(8,128)(2,1)S(1)} %convolution_convert_fusion.13), channel_id=1, source_target_pairs={{0,1},{1,0},{2,3},{3,2},{4,5},{5,4},{6,7},{7,6},{8,9},{9,8},{10,11... | collective-permute-start | bytes 3145736 | tf_op jit(solution)/shard_map/ppermute | solution.py:566
  483.4 8.9 %collective-permute-done.27 = bf16[128,2048]{1,0:T(8,128)(2,1)S(1)} collective-permute-done((bf16[128,2048]{1,0:T(8,128)(2,1)S(1)}, bf16[128,2048]{1,0:T(8,128)(2,1)S(1)}, u32[]{:S(2)}, u32[]{:S(2)}) %collective-permute-start.27) | collective-permute-done | bytes 524320 | tf_op jit(solution)/shard_map/ppermute | solution.py:505
  516.5 13.0 %collective-permute-start.61 = (bf16[1024,512]{1,0:T(8,128)(2,1)}, bf16[1024,512]{1,0:T(8,128)(2,1)}, u32[]{:S(2)}, u32[]{:S(2)}) collective-permute-start(bf16[1024,512]{1,0:T(8,128)(2,1)} %convolution_convert_fusion.9), channel_id=1, source_target_pairs={{0,1},{1,0},{2,3},{3,2},{4,5},{5,4},{6,7},{7,6},{8,9},{9,8},{10,11... | collective-permute-start | bytes 3145736 | tf_op jit(solution)/shard_map/ppermute | solution.py:566
  587.8 12.7 %collective-permute-done.36 = f32[26760]{0:T(1024)S(1)} collective-permute-done((f32[26760]{0:T(1024)S(1)}, f32[26760]{0:T(1024)S(1)}, u32[]{:S(2)}, u32[]{:S(2)}) %collective-permute-start.36) | collective-permute-done | bytes 107072 | tf_op jit(solution)/shard_map/ppermute | solution.py:519
  631.8 21.6 %collective-permute-start.86 = (bf16[1408,1024]{1,0:T(8,128)(2,1)}, bf16[1408,1024]{1,0:T(8,128)(2,1)}, u32[]{:S(2)}, u32[]{:S(2)}) collective-permute-start(bf16[1408,1024]{1,0:T(8,128)(2,1)} %pad_maximum_fusion.2), channel_id=1, source_target_pairs={{0,1},{1,0},{2,3},{3,2},{4,5},{5,4},{6,7},{7,6},{8,9},{9,8},{10,11... | collective-permute-start | bytes 8650760 | tf_op jit(solution)/shard_map/ppermute | solution.py:570
  699.1 8.2 collective-permute-done.53
  717.1 12.6 %collective-permute-done.72 = bf16[1024,512]{1,0:T(8,128)(2,1)S(1)} collective-permute-done((bf16[1024,512]{1,0:T(8,128)(2,1)S(1)}, bf16[1024,512]{1,0:T(8,128)(2,1)S(1)}, u32[]{:S(2)}, u32[]{:S(2)}) %collective-permute-start.72) | collective-permute-done | bytes 1048608 | tf_op jit(solution)/shard_map/ppermute | solution.py:554
  779.8 19.6 %collective-permute-done.76 = bf16[1024,512]{1,0:T(8,128)(2,1)S(1)} collective-permute-done((bf16[1024,512]{1,0:T(8,128)(2,1)}, bf16[1024,512]{1,0:T(8,128)(2,1)S(1)}, u32[]{:S(2)}, u32[]{:S(2)}) %collective-permute-start.76) | collective-permute-done | bytes 1048608 | tf_op jit(solution)/shard_map/ppermute | solution.py:554
  827.8 16.6 %collective-permute-done.77 = bf16[1024,512]{1,0:T(8,128)(2,1)} collective-permute-done((bf16[1024,512]{1,0:T(8,128)(2,1)S(1)}, bf16[1024,512]{1,0:T(8,128)(2,1)}, u32[]{:S(2)}, u32[]{:S(2)}) %collective-permute-start.77) | collective-permute-done | bytes 1048608 | tf_op jit(solution)/shard_map/ppermute | solution.py:554
  (547 shorter events, 521.1 us)
Async XLA Ops:
  5.9 44.3 %collective-permute-start.1 = (bf16[256,2048]{1,0:T(8,128)(2,1)}, bf16[256,2048]{1,0:T(8,128)(2,1)}, u32[]{:S(2)}, u32[]{:S(2)}) collective-permute-start(bf16[256,2048]{1,0:T(8,128)(2,1)} %bitcast), channel_id=1, source_target_pairs={{0,16},{8,24},{16,0},{24,8},{1,17},{9,25},{17,1},{25,9},{2,18},{10... | collective-permute-start | bytes 3145736 | tf_op jit(solution)/shard_map/ppermute | solution.py:495
  6.1 46.3 %collective-permute-start = (bf16[256,2048]{1,0:T(8,128)(2,1)}, bf16[256,2048]{1,0:T(8,128)(2,1)}, u32[]{:S(2)}, u32[]{:S(2)}) collective-permute-start(bf16[256,2048]{1,0:T(8,128)(2,1)} %bitcast), channel_id=1, source_target_pairs={{0,8},{8,0},{16,24},{24,16},{1,9},{9,1},{17,25},{25,17},{2,10},{10... | collective-permute-start | bytes 3145736 | tf_op jit(solution)/shard_map/ppermute | solution.py:494
  63.7 125.6 %collective-permute-start.12 = (bf16[2048,1024]{1,0:T(8,128)(2,1)}, bf16[2048,1024]{1,0:T(8,128)(2,1)}, u32[]{:S(2)}, u32[]{:S(2)}) collective-permute-start(bf16[2048,1024]{1,0:T(8,128)(2,1)} %constant_dynamic-update-slice_fusion.5), channel_id=1, source_target_pairs={{0,1},{1,0},{2,3},{3,2},{4,5},{5,4},{6,7},{7,6},{8,9},{9,8},{10,11... | collective-permute-start | bytes 12582920 | tf_op jit(solution)/shard_map/ppermute | solution.py:628
  120.3 43.9 %collective-permute-start.14 = (bf16[256,2048]{1,0:T(8,128)(2,1)}, bf16[256,2048]{1,0:T(8,128)(2,1)}, u32[]{:S(2)}, u32[]{:S(2)}) collective-permute-start(bf16[256,2048]{1,0:T(8,128)(2,1)} %bitcast.8), channel_id=1, source_target_pairs={{0,16},{8,24},{16,0},{24,8},{1,17},{9,25},{17,1},{25,9},{2,18},{10... | collective-permute-start | bytes 3145736 | tf_op jit(solution)/shard_map/ppermute | solution.py:495
  121.5 45.0 %collective-permute-start.13 = (bf16[256,2048]{1,0:T(8,128)(2,1)}, bf16[256,2048]{1,0:T(8,128)(2,1)}, u32[]{:S(2)}, u32[]{:S(2)}) collective-permute-start(bf16[256,2048]{1,0:T(8,128)(2,1)} %bitcast.8), channel_id=1, source_target_pairs={{0,8},{8,0},{16,24},{24,16},{1,9},{9,1},{17,25},{25,17},{2,10},{10... | collective-permute-start | bytes 3145736 | tf_op jit(solution)/shard_map/ppermute | solution.py:494
  298.4 43.5 %collective-permute-start.42 = (bf16[1024,1408]{1,0:T(8,128)(2,1)}, bf16[1024,1408]{1,0:T(8,128)(2,1)}, u32[]{:S(2)}, u32[]{:S(2)}) collective-permute-start(bf16[1024,1408]{1,0:T(8,128)(2,1)} %convolution_convert_fusion.3), channel_id=1, source_target_pairs={{0,1},{1,0},{2,3},{3,2},{4,5},{5,4},{6,7},{7,6},{8,9},{9,8},{10,11... | collective-permute-start | bytes 8650760 | tf_op jit(solution)/shard_map/ppermute | solution.py:566
  303.2 44.9 %collective-permute-start.43 = (bf16[1408,1024]{1,0:T(8,128)(2,1)}, bf16[1408,1024]{1,0:T(8,128)(2,1)}, u32[]{:S(2)}, u32[]{:S(2)}) collective-permute-start(bf16[1408,1024]{1,0:T(8,128)(2,1)} %convolution_convert_fusion.1), channel_id=1, source_target_pairs={{0,1},{1,0},{2,3},{3,2},{4,5},{5,4},{6,7},{7,6},{8,9},{9,8},{10,11... | collective-permute-start | bytes 8650760 | tf_op jit(solution)/shard_map/ppermute | solution.py:566
  356.6 98.3 %collective-permute-start.44 = (bf16[704,1024]{1,0:T(8,128)(2,1)}, bf16[704,1024]{1,0:T(8,128)(2,1)}, u32[]{:S(2)}, u32[]{:S(2)}) collective-permute-start(bf16[704,1024]{1,0:T(8,128)(2,1)} %get-tuple-element.175), channel_id=1, source_target_pairs={{0,2},{1,3},{6,4},{7,5},{8,10},{9,11},{14,12},{15,13},{16,18},{17,... | collective-permute-start | bytes 4325384 | tf_op jit(solution)/shard_map/ppermute | solution.py:554
  361.0 133.3 %collective-permute-start.63 = (bf16[704,1024]{1,0:T(8,128)(2,1)}, bf16[704,1024]{1,0:T(8,128)(2,1)}, u32[]{:S(2)}, u32[]{:S(2)}) collective-permute-start(bf16[704,1024]{1,0:T(8,128)(2,1)} %get-tuple-element.174), channel_id=1, source_target_pairs={{0,2},{1,3},{6,4},{7,5},{8,10},{9,11},{14,12},{15,13},{16,18},{17,... | collective-permute-start | bytes 4325384 | tf_op jit(solution)/shard_map/ppermute | solution.py:554
  516.5 43.4 %collective-permute-start.61 = (bf16[1024,512]{1,0:T(8,128)(2,1)}, bf16[1024,512]{1,0:T(8,128)(2,1)}, u32[]{:S(2)}, u32[]{:S(2)}) collective-permute-start(bf16[1024,512]{1,0:T(8,128)(2,1)} %convolution_convert_fusion.9), channel_id=1, source_target_pairs={{0,1},{1,0},{2,3},{3,2},{4,5},{5,4},{6,7},{7,6},{8,9},{9,8},{10,11... | collective-permute-start | bytes 3145736 | tf_op jit(solution)/shard_map/ppermute | solution.py:566
  560.1 43.9 %collective-permute-start.66 = (bf16[512,1408]{1,0:T(8,128)(2,1)S(1)}, bf16[512,1408]{1,0:T(8,128)(2,1)S(1)}, u32[]{:S(2)}, u32[]{:S(2)}) collective-permute-start(bf16[512,1408]{1,0:T(8,128)(2,1)S(1)} %copy-done.40), channel_id=1, source_target_pairs={{0,2},{1,3},{6,4},{7,5},{8,10},{9,11},{14,12},{15,13},{16,18},{17,... | collective-permute-start | bytes 4325384 | tf_op jit(solution)/shard_map/ppermute | solution.py:554
  610.8 49.4 %collective-permute-start.26 = (bf16[256,2048]{1,0:T(8,128)(2,1)S(1)}, bf16[256,2048]{1,0:T(8,128)(2,1)S(1)}, u32[]{:S(2)}, u32[]{:S(2)}) collective-permute-start(bf16[256,2048]{1,0:T(8,128)(2,1)S(1)} %copy-done.64), channel_id=1, source_target_pairs={{0,8},{8,0},{16,24},{24,16},{1,9},{9,1},{17,25},{25,17},{2,10},{10... | collective-permute-start | bytes 3145736 | tf_op jit(solution)/shard_map/ppermute | solution.py:511
  617.7 45.9 %collective-permute-start.37 = (f32[26760]{0:T(1024)S(1)}, f32[26760]{0:T(1024)S(1)}, u32[]{:S(2)}, u32[]{:S(2)}) collective-permute-start(f32[26760]{0:T(1024)S(1)} %add.245), channel_id=1, source_target_pairs={{0,4},{1,5},{2,6},{3,7},{4,0},{5,1},{6,2},{7,3},{8,12},{9,13},{10,... | collective-permute-start | bytes 321128 | tf_op jit(solution)/shard_map/ppermute | solution.py:519
  621.4 66.2 %collective-permute-start.70 = (bf16[512,1408]{1,0:T(8,128)(2,1)}, bf16[512,1408]{1,0:T(8,128)(2,1)}, u32[]{:S(2)}, u32[]{:S(2)}) collective-permute-start(bf16[512,1408]{1,0:T(8,128)(2,1)} %add.269), channel_id=1, source_target_pairs={{2,4},{3,5},{4,2},{5,3},{10,12},{11,13},{12,10},{13,11},{18,20},{1... | collective-permute-start | bytes 4325384 | tf_op jit(solution)/shard_map/ppermute | solution.py:554
  623.1 69.0 %collective-permute-start.71 = (bf16[512,1408]{1,0:T(8,128)(2,1)}, bf16[512,1408]{1,0:T(8,128)(2,1)}, u32[]{:S(2)}, u32[]{:S(2)}) collective-permute-start(bf16[512,1408]{1,0:T(8,128)(2,1)} %add.270), channel_id=1, source_target_pairs={{2,0},{3,1},{4,6},{5,7},{10,8},{11,9},{12,14},{13,15},{18,16},{19,... | collective-permute-start | bytes 4325384 | tf_op jit(solution)/shard_map/ppermute | solution.py:554
  631.8 109.0 %collective-permute-start.86 = (bf16[1408,1024]{1,0:T(8,128)(2,1)}, bf16[1408,1024]{1,0:T(8,128)(2,1)}, u32[]{:S(2)}, u32[]{:S(2)}) collective-permute-start(bf16[1408,1024]{1,0:T(8,128)(2,1)} %pad_maximum_fusion.2), channel_id=1, source_target_pairs={{0,1},{1,0},{2,3},{3,2},{4,5},{5,4},{6,7},{7,6},{8,9},{9,8},{10,11... | collective-permute-start | bytes 8650760 | tf_op jit(solution)/shard_map/ppermute | solution.py:570
  663.6 43.7 %collective-permute-start.53 = (bf16[1024,512]{1,0:T(8,128)(2,1)}, bf16[1024,512]{1,0:T(8,128)(2,1)}, u32[]{:S(2)}, u32[]{:S(2)}) collective-permute-start(bf16[1024,512]{1,0:T(8,128)(2,1)} %fusion.58), channel_id=1, source_target_pairs={{0,2},{1,3},{6,4},{7,5},{8,10},{9,11},{14,12},{15,13},{16,18},{17,... | collective-permute-start | bytes 3145736 | tf_op jit(solution)/shard_map/ppermute | solution.py:554
  687.6 46.1 %collective-permute-start.55 = (bf16[512,1408]{1,0:T(8,128)(2,1)S(1)}, bf16[512,1408]{1,0:T(8,128)(2,1)S(1)}, u32[]{:S(2)}, u32[]{:S(2)}) collective-permute-start(bf16[512,1408]{1,0:T(8,128)(2,1)S(1)} %copy-done.37), channel_id=1, source_target_pairs={{2,0},{3,1},{4,6},{5,7},{10,8},{11,9},{12,14},{13,15},{18,16},{19,... | collective-permute-start | bytes 4325384 | tf_op jit(solution)/shard_map/ppermute | solution.py:554
  729.7 74.8 %collective-permute-start.84 = (bf16[1024,1408]{1,0:T(8,128)(2,1)}, bf16[1024,1408]{1,0:T(8,128)(2,1)}, u32[]{:S(2)}, u32[]{:S(2)}) collective-permute-start(bf16[1024,1408]{1,0:T(8,128)(2,1)} %pad_maximum_fusion), channel_id=1, source_target_pairs={{0,1},{1,0},{2,3},{3,2},{4,5},{5,4},{6,7},{7,6},{8,9},{9,8},{10,11... | collective-permute-start | bytes 8650760 | tf_op jit(solution)/shard_map/ppermute | solution.py:570
  766.9 92.6 %collective-permute-start.85 = (bf16[1024,1408]{1,0:T(8,128)(2,1)}, bf16[1024,1408]{1,0:T(8,128)(2,1)}, u32[]{:S(2)}, u32[]{:S(2)}) collective-permute-start(bf16[1024,1408]{1,0:T(8,128)(2,1)} %pad_maximum_fusion.1), channel_id=1, source_target_pairs={{0,1},{1,0},{2,3},{3,2},{4,5},{5,4},{6,7},{7,6},{8,9},{9,8},{10,11... | collective-permute-start | bytes 8650760 | tf_op jit(solution)/shard_map/ppermute | solution.py:570
  776.9 45.0 %collective-permute-start.59 = (bf16[1024,512]{1,0:T(8,128)(2,1)}, bf16[1024,512]{1,0:T(8,128)(2,1)}, u32[]{:S(2)}, u32[]{:S(2)}) collective-permute-start(bf16[1024,512]{1,0:T(8,128)(2,1)} %add.263), channel_id=1, source_target_pairs={{2,0},{3,1},{4,6},{5,7},{10,8},{11,9},{12,14},{13,15},{18,16},{19,... | collective-permute-start | bytes 3145736 | tf_op jit(solution)/shard_map/ppermute | solution.py:554
  799.4 45.0 %collective-permute-start.77 = (bf16[1024,512]{1,0:T(8,128)(2,1)S(1)}, bf16[1024,512]{1,0:T(8,128)(2,1)}, u32[]{:S(2)}, u32[]{:S(2)}) collective-permute-start(bf16[1024,512]{1,0:T(8,128)(2,1)S(1)} %add.275), channel_id=1, source_target_pairs={{2,0},{3,1},{4,6},{5,7},{10,8},{11,9},{12,14},{13,15},{18,16},{19,... | collective-permute-start | bytes 3145736 | tf_op jit(solution)/shard_map/ppermute | solution.py:554
  800.7 47.6 %collective-permute-start.79 = (bf16[1024,512]{1,0:T(8,128)(2,1)S(1)}, bf16[1024,512]{1,0:T(8,128)(2,1)}, u32[]{:S(2)}, u32[]{:S(2)}) collective-permute-start(bf16[1024,512]{1,0:T(8,128)(2,1)S(1)} %add.262), channel_id=1, source_target_pairs={{2,4},{3,5},{4,2},{5,3},{10,12},{11,13},{12,10},{13,11},{18,20},{1... | collective-permute-start | bytes 3145736 | tf_op jit(solution)/shard_map/ppermute | solution.py:554
  804.5 45.4 %collective-permute-start.82 = (bf16[1024,512]{1,0:T(8,128)(2,1)}, bf16[1024,512]{1,0:T(8,128)(2,1)}, u32[]{:S(2)}, u32[]{:S(2)}) collective-permute-start(bf16[1024,512]{1,0:T(8,128)(2,1)} %broadcast_select_fusion.19), channel_id=1, source_target_pairs={{0,1},{1,0},{2,3},{3,2},{4,5},{5,4},{6,7},{7,6},{8,9},{9,8},{10,11... | collective-permute-start | bytes 3145736 | tf_op jit(solution)/shard_map/ppermute | solution.py:570
  (171 other events, 3337.5 us)

commit v2 on v1

--- a/solution.py
+++ b/solution.py
@@ -1,3 +1,4 @@
+import math
 from functools import partial
 
 import jax
@@ -11,7 +12,8 @@
 CONV = 4
 SPAN = 64
 TILE = 2 * SPAN
-VMEM_BYTES = 48 * 1024 * 1024
+VMEM_BYTES = 60 * 1024 * 1024
+SMALL = pl.CostEstimate(flops=0, bytes_accessed=0, transcendentals=0)
 epsilon = 1e-06
 head_epsilon = 0.001
 f32 = jnp.float32
@@ -220,10 +222,10 @@
     return pl.BlockSpec(shape, lambda i, s: (0,) * len(shape))
 
 
-def mixer_forward(starts, q, k, v, gate, sp, taps, rate, bias, gain):
+def mixer_forward(count, starts, q, k, v, gate, sp, taps, rate, bias, gain):
     rows, width = q.shape
     heads = width // HEAD_DIM
-    block = rows // 4
+    block = rows // count
     tiles = block // TILE
     spec = lambda r, w: blocked(r, w, lambda i: i)
     wide, half, state = spec(block, width), spec(block // 2, width), spec(block * 2, width)
@@ -232,14 +234,14 @@
         partial(forward_kernel, tiles, heads),
         grid_spec=pltpu.PrefetchScalarGridSpec(
             num_scalar_prefetch=1,
-            grid=(4,),
+            grid=(count,),
             in_specs=[wide] * 4 + [spec(block, HEAD_DIM)] + [constant(a.shape) for a in (taps, rate, bias, gain)],
             out_specs=[wide] * 5 + [half] * 3 + [wide] * 2 + [state],
             scratch_shapes=[pltpu.VMEM((3, block + 8, width), f32), pltpu.VMEM((heads, HEAD_DIM, HEAD_DIM), f32)],
         ),
         out_shape=[shape(rows)] * 5 + [shape(rows // 2)] * 3 + [shape(rows)] * 2 + [shape(rows * 2)],
         compiler_params=pltpu.CompilerParams(dimension_semantics=("arbitrary",), vmem_limit_bytes=VMEM_BYTES),
-        cost_estimate=pl.CostEstimate(flops=10 * 10**9, bytes_accessed=16 * 10**6, transcendentals=10**6),
+        cost_estimate=SMALL,
     )(starts, q, k, v, gate, sp, taps, rate, bias, gain)
 
 
@@ -251,7 +253,7 @@
 
 def backward_kernel(tiles, heads, starts_ref, gg_ref, mixed_ref, gate_ref, cq_ref, ck_ref, cv_ref, q_ref, k_ref, v_ref, sp_ref,
                     inv_ref, qk_ref, gram_ref, w_ref, u_ref, s_ref, taps_ref, rate_ref, bias_ref, gain_ref,
-                    dq_ref, dk_ref, dv_ref, dgate_ref, dsp_ref, dtaps_ref, dmisc_ref, ext_ref, state_ref):
+                    flat_ref, dsp_ref, dtaps_ref, dmisc_ref, ext_ref, state_ref):
     step = pl.num_programs(0) - 1 - pl.program_id(0)
     rows = tiles * TILE
 
@@ -284,7 +286,7 @@
         grad = gg_ref[spans[t], lanes_of(h)].astype(f32)
         sig = jax.nn.sigmoid(gate)
         unit = one * scale
-        dgate_ref[spans[t], lanes_of(h)] = (grad * unit * gain * (sig * (1.0 + gate * (1.0 - sig)))).astype(bf16)
+        flat_ref[spans[t], lanes_of(3 * heads + h)] = (grad * unit * gain * (sig * (1.0 + gate * (1.0 - sig)))).astype(bf16)
         norm_grad = grad * gate * sig
         partial_gain = partial_gain + jnp.sum(norm_grad * unit, axis=0, keepdims=True)
         norm_grad = norm_grad * gain
@@ -434,7 +436,7 @@
         ext_ref[2, spans[t], lanes_of(h)] = side_grads[n] * spread_writes[n] * silu_parts(cv_ref, t, h)[1]
     place, _, end = row_places(step * rows, rows, starts_ref)
     masks = [None] + [jnp.where(place + j < end, 1.0, 0.0) for j in range(1, CONV)]
-    for which, (source, out) in enumerate(((q_ref, dq_ref), (k_ref, dk_ref), (v_ref, dv_ref))):
+    for which, source in enumerate((q_ref, k_ref, v_ref)):
         for h in range(heads):
             lanes = lanes_of(h)
             proj = source[:, lanes].astype(f32)
@@ -447,146 +449,705 @@
                 dtaps_ref[at:at + 1, lanes] = dtaps_ref[at:at + 1, lanes] + jnp.sum(proj * moved, axis=0, keepdims=True)
                 term = moved * taps_ref[at:at + 1, lanes]
                 total = term if total is None else total + term
-            out[:, lanes] = total.astype(bf16)
+            flat_ref[:, lanes_of(which * heads + h)] = total.astype(bf16)
         ext_ref[which, rows:, :] = ext_ref[which, :8, :]
 
 
-def mixer_backward(starts, gg, gate, q, k, v, sp, kept, taps, rate, bias, gain):
+def mixer_backward(count, starts, gg, gate, q, k, v, sp, kept, taps, rate, bias, gain):
     mixed, cq, ck, cv, inv, qk, gram, w, u, s = kept
     rows, width = q.shape
     heads = width // HEAD_DIM
-    block = rows // 4
+    block = rows // count
     tiles = block // TILE
-    spec = lambda r, w: blocked(r, w, lambda i: 3 - i)
+    spec = lambda r, w: blocked(r, w, lambda i: count - 1 - i)
     wide, half, state, scal = spec(block, width), spec(block // 2, width), spec(block * 2, width), spec(block, HEAD_DIM)
     shape = lambda r: jax.ShapeDtypeStruct((r, width), bf16)
     return pl.pallas_call(
         partial(backward_kernel, tiles, heads),
         grid_spec=pltpu.PrefetchScalarGridSpec(
             num_scalar_prefetch=1,
-            grid=(4,),
+            grid=(count,),
             in_specs=[wide] * 9 + [scal] + [half] * 3 + [wide] * 2 + [state] + [constant(a.shape) for a in (taps, rate, bias, gain)],
-            out_specs=[wide] * 4 + [scal, constant((3 * CONV, width)), constant((8, HEAD_DIM))],
+            out_specs=[spec(block, 4 * width), scal, constant((3 * CONV, width)), constant((8, HEAD_DIM))],
             scratch_shapes=[pltpu.VMEM((3, block + 8, width), f32), pltpu.VMEM((heads, HEAD_DIM, HEAD_DIM), f32)],
         ),
-        out_shape=[shape(rows)] * 4
-        + [
+        out_shape=[
+            jax.ShapeDtypeStruct((rows, 4 * width), bf16),
             jax.ShapeDtypeStruct((rows, HEAD_DIM), bf16),
             jax.ShapeDtypeStruct((3 * CONV, width), f32),
             jax.ShapeDtypeStruct((8, HEAD_DIM), f32),
         ],
         compiler_params=pltpu.CompilerParams(dimension_semantics=("arbitrary",), vmem_limit_bytes=VMEM_BYTES),
-        cost_estimate=pl.CostEstimate(flops=20 * 10**9, bytes_accessed=24 * 10**6, transcendentals=10**6),
+        cost_estimate=SMALL,
     )(starts, gg, mixed, gate, cq, ck, cv, q, k, v, sp, inv, qk, gram, w, u, s, taps, rate, bias, gain)
+
+
+def after(values, *others):
+    single = not isinstance(values, (list, tuple))
+    values = [values] if single else list(values)
+    others = [one for one in others if one is not None]
+    out = pl.pallas_call(
+        lambda *refs: None,
+        out_shape=[jax.ShapeDtypeStruct(one.shape, one.dtype) for one in values],
+        in_specs=[pl.BlockSpec(memory_space=pl.ANY)] * (len(values) + len(others)),
+        out_specs=[pl.BlockSpec(memory_space=pl.ANY)] * len(values),
+        input_output_aliases={i: i for i in range(len(values))},
+    )(*values, *others)
+    return out[0] if single else list(out)
+
+
+def once(shape):
+    return pl.BlockSpec(shape, lambda *_: (0,) * len(shape), pipeline_mode=pl.Buffered(1))
+
+
+def params():
+    return pltpu.CompilerParams(dimension_semantics=("arbitrary",), vmem_limit_bytes=VMEM_BYTES)
+
+
+def project_kernel(pieces, *refs):
+    gain_ref, weights, outs = refs[pieces], refs[pieces + 1:pieces + 6], refs[-6:]
+    x = whole(refs[:pieces]).astype(f32)
+    scale = lax.rsqrt(jnp.mean(x * x, axis=-1, keepdims=True) + epsilon)
+    normed = (x * scale * gain_ref[...]).astype(bf16)
+    outs[5][...] = normed
+    for weight, out in zip(weights, outs[:5]):
+        out[...] = dot(normed, weight[...]).astype(out.dtype)
+
+
+def project(pieces, at, total, gain, weights, held):
+    rows, depth = sum(one.shape[0] for one in pieces), pieces[0].shape[1]
+    first, count = at // rows, len(pieces)
+    shapes = [jax.ShapeDtypeStruct((total, w.shape[1]), f32 if i == 4 else bf16) for i, w in enumerate(weights)]
+    shapes.append(jax.ShapeDtypeStruct((total, depth), bf16))
+    return pl.pallas_call(
+        partial(project_kernel, count),
+        grid=(1,),
+        in_specs=[once(one.shape) for one in pieces]
+        + [once(gain.shape)]
+        + [once(w.shape) for w in weights]
+        + [pl.BlockSpec(memory_space=pl.ANY)] * len(held),
+        out_specs=[pl.BlockSpec((rows, s.shape[1]), lambda i: (first, 0)) for s in shapes],
+        out_shape=shapes,
+        input_output_aliases={count + 6 + i: i for i in range(len(held))},
+        compiler_params=params(),
+        cost_estimate=SMALL,
+    )(*pieces, gain, *weights, *held)
+
+
+def pick(count, refs, held):
+    step = pl.program_id(0)
+    for which in range(count):
+        @pl.when(step == which)
+        def _():
+            held[...] = whole(refs[which]) if isinstance(refs[which], (list, tuple)) else refs[which][...]
+
+
+def middle_kernel(sizes, rank_ref, *refs):
+    count = len(sizes)
+    x_refs, refs = split_pieces(refs, sizes)
+    g_refs = refs[:count]
+    weight_ref, gain_ref, normed_ref, own_ref, scr, x_scr = refs[count:]
+    pick(count, x_refs, x_scr)
+    gated = jnp.concatenate([one[...] for one in g_refs], axis=1)
+    width = gated.shape[1] // count
+    for a, b in column_cuts(scr.shape[1]):
+        weight = [weight_ref[:, rank_ref[0] ^ m, :, a:b].reshape(width, b - a) for m in range(count)]
+        scr[:, a:b] = dot(gated, jnp.concatenate(weight, axis=0)) + x_scr[:, a:b].astype(f32)
+    middle = scr[...]
+    scale = lax.rsqrt(jnp.mean(middle * middle, axis=-1, keepdims=True) + epsilon)
+    normed_ref[...] = (middle * scale * gain_ref[...]).astype(bf16)
+
+    @pl.when(pl.program_id(0) == 0)
+    def _():
+        own_ref[...] = middle
+
+
+def middle_rows(rank, x_parts, gated_parts, weight, gain):
+    count = len(x_parts)
+    rows, depth = x_parts[0][0].shape
+    width = gated_parts[0].shape[1]
+    flat = [one for part in x_parts for one in part]
+    return pl.pallas_call(
+        partial(middle_kernel, [len(part) for part in x_parts]),
+        grid_spec=pltpu.PrefetchScalarGridSpec(
+            num_scalar_prefetch=1,
+            grid=(count,),
+            in_specs=[once(one.shape) for one in flat]
+            + [pl.BlockSpec((rows, width), lambda i, s, at=at: (i ^ at, 0)) for at in range(count)]
+            + [once(weight.shape), once(gain.shape)],
+            out_specs=[pl.BlockSpec((rows, depth), lambda i, s: (i, 0)), once((rows, depth))],
+            scratch_shapes=[pltpu.VMEM((rows, depth), f32), pltpu.VMEM((rows, depth), bf16)],
+        ),
+        out_shape=[jax.ShapeDtypeStruct((count * rows, depth), bf16), jax.ShapeDtypeStruct((rows, depth), f32)],
+        compiler_params=params(),
+        cost_estimate=SMALL,
+    )(rank, *flat, *gated_parts, weight, gain)
+
+
+def gated_grad_kernel(rank_ref, rows_ref, weight_ref, *refs):
+    refs[-1][...] = dot(rows_ref[...], weight_ref[...], ((1,), (1,))).astype(bf16)
+
+
+def gated_grads(count, rank, gathered, weight, *others):
+    rows, depth = gathered.shape[0] // count, gathered.shape[1]
+    width = weight.shape[0]
+    return pl.pallas_call(
+        gated_grad_kernel,
+        grid_spec=pltpu.PrefetchScalarGridSpec(
+            num_scalar_prefetch=1,
+            grid=(count,),
+            in_specs=[pl.BlockSpec((rows, depth), lambda i, s: (i ^ s[0], 0)), once(weight.shape)]
+            + [pl.BlockSpec(memory_space=pl.ANY)] * len(others),
+            out_specs=pl.BlockSpec((rows, width), lambda i, s: (i, 0)),
+        ),
+        out_shape=jax.ShapeDtypeStruct((count * rows, width), bf16),
+        compiler_params=params(),
+        cost_estimate=SMALL,
+    )(rank, gathered, weight, *others)
+
+
+def column_cuts(width, chunk=512):
+    return [(lo, min(lo + chunk, width)) for lo in range(0, width, chunk)]
+
+
+def hidden_kernel(x_ref, wg_ref, wu_ref, *refs):
+    gate_ref, up_ref, hidden_ref = refs[-3:]
+    x = x_ref[...]
+    for a, b in column_cuts(wg_ref.shape[1]):
+        gate, up = dot(x, wg_ref[:, a:b]), dot(x, wu_ref[:, a:b])
+        gate_ref[:, a:b] = gate.astype(bf16)
+        up_ref[:, a:b] = up.astype(bf16)
+        hidden_ref[:, a:b] = (gate * jax.nn.sigmoid(gate) * up).astype(bf16)
+
+
+def hidden_units(x, gate_weight, up_weight, *others):
+    rows, depth = x.shape
+    width = gate_weight.shape[1]
+    block = rows // 4
+    out = pl.BlockSpec((block, width), lambda i: (i, 0))
+    return pl.pallas_call(
+        hidden_kernel,
+        grid=(4,),
+        in_specs=[pl.BlockSpec((block, depth), lambda i: (i, 0)), once(gate_weight.shape), once(up_weight.shape)]
+        + [pl.BlockSpec(memory_space=pl.ANY)] * len(others),
+        out_specs=[out] * 3,
+        out_shape=[jax.ShapeDtypeStruct((rows, width), bf16)] * 3,
+        compiler_params=params(),
+        cost_estimate=SMALL,
+    )(x, gate_weight, up_weight, *others)
+
+
+def whole(refs):
+    values = [one[...] for one in refs]
+    return values[0] if len(values) == 1 else jnp.concatenate(values, axis=0)
+
+
+def outer_kernel(parts, info_ref, *refs):
+    total, at = None, 0
+    for count in parts:
+        term = dot(whole(refs[at:at + count]), refs[at + count][...], ((0,), (0,)))
+        total = term if total is None else total + term
+        at += count + 1
+    refs[-1][...] = total.astype(bf16)
+
+
+def half_column(count, own):
+    return lambda i, s: (s[0] if own else 1 - s[0]) * count + i
+
+
+def outer_half(info, own, sides, *others):
+    lefts, right = sides[0]
+    half, block = lefts[0].shape[1] // 2, 2 * TILE
+    count, units = half // block, right.shape[1]
+    column = half_column(count, own)
+    in_specs, values = [], []
+    for lefts, right in sides:
+        in_specs += [pl.BlockSpec((one.shape[0], block), lambda i, s: (0, column(i, s))) for one in lefts] + [once(right.shape)]
+        values += list(lefts) + [right]
+    return pl.pallas_call(
+        partial(outer_kernel, [len(lefts) for lefts, _ in sides]),
+        grid_spec=pltpu.PrefetchScalarGridSpec(
+            num_scalar_prefetch=1,
+            grid=(count,),
+            in_specs=in_specs + [pl.BlockSpec(memory_space=pl.ANY)] * len(others),
+            out_specs=pl.BlockSpec((block, units), lambda i, s: (i, 0)),
+        ),
+        out_shape=jax.ShapeDtypeStruct((half, units), bf16),
+        compiler_params=params(),
+        cost_estimate=SMALL,
+    )(info, *values, *others)
+
+
+def split_pieces(refs, sizes):
+    pieces, at = [], 0
+    for size in sizes:
+        pieces.append(refs[at:at + size])
+        at += size
+    return pieces, refs[at:]
+
+
+def hidden_grad_kernel(sizes, rank_ref, *refs):
+    c_refs, refs = split_pieces(refs, sizes)
+    gate_ref, up_ref, wg_ref, wu_ref, wd_ref = refs[:5]
+    gg_ref, ug_ref, mid_ref, held = refs[-4:]
+    pick(len(sizes), c_refs, held)
+    grad_rows = held[...]
+    nt = ((1,), (1,))
+    for a, b in column_cuts(wg_ref.shape[1]):
+        grad = dot(grad_rows, wd_ref[a:b, :], nt)
+        gate, up = gate_ref[:, a:b].astype(f32), up_ref[:, a:b].astype(f32)
+        sig = jax.nn.sigmoid(gate)
+        gg_ref[:, a:b] = (grad * up * sig * (1.0 + gate * (1.0 - sig))).astype(bf16)
+        ug_ref[:, a:b] = (grad * gate * sig).astype(bf16)
+    gate_grad, up_grad = gg_ref[...], ug_ref[...]
+    for a, b in column_cuts(wg_ref.shape[0]):
+        mid_ref[:, a:b] = (dot(gate_grad, wg_ref[a:b, :], nt) + dot(up_grad, wu_ref[a:b, :], nt)).astype(bf16)
+
+
+def hidden_grads(rank, cot_parts, gates, ups, gate_weight, up_weight, down_weight, *others):
+    count = len(cot_parts)
+    rows, depth = cot_parts[0][0].shape
+    width = gate_weight.shape[1]
+    spec = pl.BlockSpec((rows, width), lambda i, s: (i, 0))
+    flat = [one for part in cot_parts for one in part]
+    return pl.pallas_call(
+        partial(hidden_grad_kernel, [len(part) for part in cot_parts]),
+        grid_spec=pltpu.PrefetchScalarGridSpec(
+            num_scalar_prefetch=1,
+            grid=(count,),
+            in_specs=[once(one.shape) for one in flat]
+            + [spec] * 2
+            + [once(gate_weight.shape), once(up_weight.shape), once(down_weight.shape)]
+            + [pl.BlockSpec(memory_space=pl.ANY)] * len(others),
+            out_specs=[spec, spec, pl.BlockSpec((rows, depth), lambda i, s: (i ^ s[0], 0))],
+            scratch_shapes=[pltpu.VMEM((rows, depth), bf16)],
+        ),
+        out_shape=[jax.ShapeDtypeStruct((count * rows, width), bf16)] * 2 + [jax.ShapeDtypeStruct((count * rows, depth), bf16)],
+        compiler_params=params(),
+        cost_estimate=SMALL,
+    )(rank, *flat, gates, ups, gate_weight, up_weight, down_weight, *others)
+
+
+def input_grad_kernel(rank_ref, grad_ref, scalar_ref, *refs):
+    weights, out = refs[:5], refs[-1]
+    grad = jnp.concatenate([grad_ref[...], scalar_ref[...]], axis=1)
+    for a, b in column_cuts(out.shape[1]):
+        weight = jnp.concatenate([one[a:b, :] for one in weights], axis=1)
+        out[:, a:b] = dot(grad, weight, ((1,), (1,))).astype(bf16)
+
+
+def input_grads(count, rank, grad, scalar_grad, weights, *others):
+    rows, depth = grad.shape[0] // count, weights[0].shape[0]
+    return pl.pallas_call(
+        input_grad_kernel,
+        grid_spec=pltpu.PrefetchScalarGridSpec(
+            num_scalar_prefetch=1,
+            grid=(count,),
+            in_specs=[pl.BlockSpec((rows, one.shape[1]), lambda i, s: (i, 0)) for one in (grad, scalar_grad)]
+            + [once(one.shape) for one in weights]
+            + [pl.BlockSpec(memory_space=pl.ANY)] * len(others),
+            out_specs=pl.BlockSpec((rows, depth), lambda i, s: (i ^ s[0], 0)),
+        ),
+        out_shape=jax.ShapeDtypeStruct((count * rows, depth), bf16),
+        compiler_params=params(),
+        cost_estimate=SMALL,
+    )(rank, grad, scalar_grad, *weights, *others)
+
+
+def result_kernel(rank_ref, hidden_ref, weight_ref, *refs):
+    out = refs[-1]
+    for a, b in column_cuts(out.shape[1]):
+        out[:, a:b] = dot(hidden_ref[...], weight_ref[:, a:b]).astype(bf16)
+
+
+def result_rows(count, rank, hidden, weight, *others):
+    rows, depth = hidden.shape[0] // count, weight.shape[1]
+    return pl.pallas_call(
+        result_kernel,
+        grid_spec=pltpu.PrefetchScalarGridSpec(
+            num_scalar_prefetch=1,
+            grid=(count,),
+            in_specs=[pl.BlockSpec((rows, hidden.shape[1]), lambda i, s: (i, 0)), once(weight.shape)]
+            + [pl.BlockSpec(memory_space=pl.ANY)] * len(others),
+            out_specs=pl.BlockSpec((rows, depth), lambda i, s: (i ^ s[0], 0)),
+        ),
+        out_shape=jax.ShapeDtypeStruct((count * rows, depth), bf16),
+        compiler_params=params(),
+        cost_estimate=SMALL,
+    )(rank, hidden, weight, *others)
+
+
+def small_call(kernel, outs, *values):
+    return pl.pallas_call(
+        kernel,
+        out_shape=outs,
+        compiler_params=pltpu.CompilerParams(vmem_limit_bytes=VMEM_BYTES),
+        cost_estimate=SMALL,
+    )(*values)
+
+
+def merge_kernel(across_ref, down_ref, top_ref, low_ref, *refs):
+    half = top_ref.shape[0]
+    across_out, down_out = refs[-2:]
+    down_out[:half] = (down_ref[:half].astype(f32) + top_ref[...].astype(f32)).astype(bf16)
+    down_out[half:] = down_ref[half:]
+    across_out[:half] = across_ref[:half]
+    across_out[half:] = (across_ref[half:].astype(f32) + low_ref[...].astype(f32)).astype(bf16)
+
+
+def halves_kernel(across_ref, down_ref, top_out, low_out):
+    top_out[...] = down_ref[...]
+    low_out[...] = across_ref[...]
+
+
+def far_halves(across, down):
+    rows, columns = across.shape[0] // 2, across.shape[1]
+    top, low = pl.BlockSpec((rows, columns), lambda i: (0, 0)), pl.BlockSpec((rows, columns), lambda i: (1, 0))
+    return pl.pallas_call(
+        halves_kernel,
+        grid=(1,),
+        in_specs=[low, top],
+        out_specs=[top, top],
+        out_shape=[jax.ShapeDtypeStruct((rows, columns), across.dtype)] * 2,
+        compiler_params=params(),
+        cost_estimate=SMALL,
+    )(across, down)
+
+
+def norm_grad_kernel(count, *refs):
+    terms, (x_ref, cot_ref, gain_ref, grad_out, low_out, gain_out) = refs[:count], refs[count:]
+    grad = terms[0][...].astype(f32)
+    for one in terms[1:]:
+        grad = grad + one[...].astype(f32)
+    x = x_ref[...].astype(f32)
+    scale = lax.rsqrt(jnp.mean(x * x, axis=-1, keepdims=True) + epsilon)
+    unit = x * scale
+    gain_out[...] = jnp.sum(grad * unit, axis=0, keepdims=True)
+    inner = grad * gain_ref[...]
+    total = cot_ref[...].astype(f32) + scale * (inner - unit * jnp.mean(inner * unit, axis=-1, keepdims=True))
+    if grad_out is not None:
+        grad_out[...] = total
+    low_out[...] = total.astype(bf16)
+
+
+def norm_grad(terms, x, cot, gain):
+    rows, depth = x.shape
+    return small_call(
+        partial(norm_grad_kernel, len(terms)),
+        [jax.ShapeDtypeStruct((rows, depth), f32), jax.ShapeDtypeStruct((rows, depth), bf16), jax.ShapeDtypeStruct((1, depth), f32)],
+        *terms, x, cot, gain,
+    )
+
+
+def total_kernel(*refs):
+    refs[-1][...] = (refs[0][...] + refs[1][...].astype(f32)).astype(bf16)
+
+
+def wide_call(kernel, out_dtype, values, *others):
+    rows, columns = values[0].shape
+    block = next(size for size in (256, 128, 64, 32, 16) if rows % size == 0)
+    spec = pl.BlockSpec((block, columns), lambda i, *_: (i, 0))
+    return pl.pallas_call(
+        kernel,
+        grid=(rows // block,),
+        in_specs=[spec] * len(values) + [pl.BlockSpec(memory_space=pl.ANY)] * len(others),
+        out_specs=spec,
+        out_shape=jax.ShapeDtypeStruct((rows, columns), out_dtype),
+        compiler_params=params(),
+        cost_estimate=SMALL,
+    )(*values, *others)
+
+
+def add_kernel(left, right, *refs):
+    refs[-1][...] = (left[...].astype(f32) + right[...].astype(f32)).astype(bf16)
+
+
+def cast_kernel(value, *refs):
+    refs[-1][...] = value[...].astype(f32)
+
+
+def choose_kernel(flag_ref, left, right, *refs):
+    refs[-1][...] = jnp.where(flag_ref[0] == 1, left[...], right[...])
+
+
+def choose(flag, left, right, *others):
+    rows, columns = left.shape
+    block = next(size for size in (256, 128, 64, 32, 16) if rows % size == 0)
+    spec = pl.BlockSpec((block, columns), lambda i, s: (i, 0))
+    return pl.pallas_call(
+        choose_kernel,
+        grid_spec=pltpu.PrefetchScalarGridSpec(
+            num_scalar_prefetch=1,
+            grid=(rows // block,),
+            in_specs=[spec, spec] + [pl.BlockSpec(memory_space=pl.ANY)] * len(others),
+            out_specs=spec,
+        ),
+        out_shape=jax.ShapeDtypeStruct((rows, columns), left.dtype),
+        compiler_params=params(),
+        cost_estimate=SMALL,
+    )(flag, left, right, *others)
+
+
+def head_outer_kernel(parts, info_ref, *refs):
+    attn, (gated_ref, in_ref, flat_ref, scalar_ref) = refs[:parts], refs[parts:parts + 4]
+    one, two = refs[-2:]
+    units = one.shape[1]
+    tn = ((0,), (0,))
+    left = in_ref[...]
+    columns = [dot(whole(attn), gated_ref[...], tn), dot(left, flat_ref[...], tn), dot(left, scalar_ref[...], tn)]
+    joined = jnp.concatenate([one.astype(bf16) for one in columns], axis=1)
+    spare = 2 * units - joined.shape[1]
+    if spare:
+        joined = jnp.concatenate([joined, jnp.zeros((joined.shape[0], spare), bf16)], axis=1)
+    one[...] = joined[:, :units]
+    two[...] = joined[:, units:]
+
+
+def head_outer(info, own, parts, attn, gated, normed, flat, scalar, units, *others):
+    tokens, width = normed.shape
+    half, block = width // 2, 2 * TILE
+    count, rows = half // block, tokens // parts
+    column = half_column(count, own)
+    attn_specs = [pl.BlockSpec((rows, block), lambda i, s, m=m: (s[2] ^ m, column(i, s))) for m in range(parts)]
+    out = pl.BlockSpec((block, units), lambda i, s: (i, 0))
+    return pl.pallas_call(
+        partial(head_outer_kernel, parts),
+        grid_spec=pltpu.PrefetchScalarGridSpec(
+            num_scalar_prefetch=1,
+            grid=(count,),
+            in_specs=attn_specs
+            + [once(gated.shape), pl.BlockSpec((tokens, block), lambda i, s: (0, column(i, s))), once(flat.shape), once(scalar.shape)]
+            + [pl.BlockSpec(memory_space=pl.ANY)] * len(others),
+            out_specs=[out, out],
+        ),
+        out_shape=[jax.ShapeDtypeStruct((half, units), bf16)] * 2,
+        compiler_params=params(),
+        cost_estimate=SMALL,
+    )(info, *[attn] * parts, gated, normed, flat, scalar, *others)
+
+
+SLAB = 128
+
+
+def summed(refs):
+    total = refs[0][...].astype(f32)
+    for one in refs[1:]:
+        total = total + one[...].astype(f32)
+    return total
+
+
+def line_start_kernel(count, info_ref, *refs):
+    refs[-1][...] = summed(refs[:count]).astype(bf16)
+
+
+def line_step_kernel(now_count, later_count, info_ref, *refs):
+    now, later, refs = refs[:now_count], refs[now_count:now_count + later_count], refs[now_count + later_count:]
+    right_sent, left_sent, right_came, left_came = refs[:4]
+    result_ref, right_ref, left_ref = refs[-3:]
+    center, upper = info_ref[1] == 1, info_ref[3] == 1
+    add = lambda one, two: one[...].astype(f32) + two[...].astype(f32)
+
+    @pl.when(jnp.logical_not(center))
+    def _():
+        value = summed(later or now).astype(bf16)
+        right_ref[...] = value
+        left_ref[...] = value
+        result_ref[...] = jnp.where(upper, right_came[...], left_came[...])
+
+    @pl.when(center & upper)
+    def _():
+        result_ref[...] = right_sent[...]
+        right_ref[...] = add(left_sent, right_came).astype(bf16)
+        left_ref[...] = (summed(now) + left_came[...].astype(f32)).astype(bf16)
+
+    @pl.when(center & jnp.logical_not(upper))
+    def _():
+        result_ref[...] = left_sent[...]
+        left_ref[...] = add(right_sent, left_came).astype(bf16)
+        right_ref[...] = (summed(now) + right_came[...].astype(f32)).astype(bf16)
+
+
+class Line:
+    def __init__(self, info, rows, chunks):
+        self.info, self.rows, self.chunks, self.step = info, rows, chunks, 0
+        size = lax.axis_size("dp")
+        self.stride = size // 4
+        self.sent = self.came = None
+        self.results = []
+
+    def send(self, right, left):
+        count, step = len(self.chunks), self.step
+        inner, middle, outer_hop = step < count, 1 <= step <= count, step >= 2
+        hops = lambda pairs: [(j + a * self.stride, j + b * self.stride) for a, b in pairs for j in range(self.stride)]
+        rightward = [(0, 1)] * inner + [(1, 2)] * middle + [(2, 3)] * outer_hop
+        leftward = [(3, 2)] * inner + [(2, 1)] * middle + [(1, 0)] * outer_hop
+        self.sent = (right, left)
+        self.came = (lax.ppermute(right, "dp", hops(rightward)), lax.ppermute(left, "dp", hops(leftward)))
+
+    def land(self, *others):
+        self.came = tuple(after(list(self.came), *others))
+        return self.came[0]
+
+    def begin(self, *others):
+        *sources, row = self.chunks[0]()
+        units = sources[0].shape[1]
+        spec = pl.BlockSpec((SLAB, units), lambda i, s: (row * (self.rows // SLAB) + i, 0))
+        value = pl.pallas_call(
+            partial(line_start_kernel, len(sources)),
+            grid_spec=pltpu.PrefetchScalarGridSpec(
+                num_scalar_prefetch=1,
+                grid=(self.rows // SLAB,),
+                in_specs=[spec] * len(sources) + [pl.BlockSpec(memory_space=pl.ANY)] * len(others),
+                out_specs=pl.BlockSpec((SLAB, units), lambda i, s: (i, 0)),
+            ),
+            out_shape=jax.ShapeDtypeStruct((self.rows, units), bf16),
+            compiler_params=params(),
+            cost_estimate=SMALL,
+        )(self.info, *sources, *others)
+        self.send(value, value)
+        return value
+
+    def advance(self, *others):
+        count, step = len(self.chunks), self.step
+        *now, first = self.chunks[min(step, count - 1)]()
+        *later, second = self.chunks[min(step + 1, count - 1)]()
+        per = self.rows // SLAB
+        units = now[0].shape[1]
+        if now[0] is later[0]:
+            later = []
+            specs = [pl.BlockSpec((SLAB, units), lambda i, s: (jnp.where(s[1] == 1, first, second) * per + i, 0))] * len(now)
+        else:
+            specs = [pl.BlockSpec((SLAB, units), lambda i, s: (first * per + i, 0))] * len(now)
+            specs += [pl.BlockSpec((SLAB, units), lambda i, s: (second * per + i, 0))] * len(later)
+        slab = pl.BlockSpec((SLAB, units), lambda i, s: (i, 0))
+        result, right, left = pl.pallas_call(
+            partial(line_step_kernel, len(now), len(later)),
+            grid_spec=pltpu.PrefetchScalarGridSpec(
+                num_scalar_prefetch=1,
+                grid=(per,),
+                in_specs=specs + [slab] * 4 + [pl.BlockSpec(memory_space=pl.ANY)] * len(others),
+                out_specs=[slab] * 3,
+            ),
+            out_shape=[jax.ShapeDtypeStruct((self.rows, units), bf16)] * 3,
+            compiler_params=params(),
+            cost_estimate=SMALL,
+        )(self.info, *now, *later, *self.sent, *self.came, *others)
+        self.step += 1
+        if step >= 2:
+            self.results.append(result)
+        if self.step < count + 2:
+            self.send(right, left)
+        return result
+
+
+def place_kernel(turned, info_ref, mine_ref, other_ref, *refs):
+    value = jnp.where(pl.program_id(0) == info_ref[0], mine_ref[...], other_ref[...]).astype(f32)
+    refs[-2][...] = value.T if turned else value
+    refs[-1][...] = jnp.zeros(refs[-1].shape, f32)
+
+
+def place(info, held, shape, mine, other, row, turned, *others):
+    rows, units = mine.shape
+    block = 2 * TILE
+    per, inner = (shape[1] if turned else shape[0]) // 2 // block, rows // block
+    both = pl.BlockSpec((block, units), lambda i, j, s: (j, 0))
+    if turned:
+        out = pl.BlockSpec((units, block), lambda i, j, s: (0, i * per + row * inner + j))
+    else:
+        out = pl.BlockSpec((block, units), lambda i, j, s: (i * per + row * inner + j, 0))
+    extra = ([] if held is None else [held]) + list(others)
+    return pl.pallas_call(
+        partial(place_kernel, turned),
+        grid_spec=pltpu.PrefetchScalarGridSpec(
+            num_scalar_prefetch=1,
+            grid=(2, inner),
+            in_specs=[both, both] + [pl.BlockSpec(memory_space=pl.ANY)] * len(extra),
+            out_specs=[out, pl.BlockSpec((8, HEAD_DIM), lambda i, j, s: (0, 0))],
+        ),
+        out_shape=[jax.ShapeDtypeStruct(shape, f32), jax.ShapeDtypeStruct((8, HEAD_DIM), f32)],
+        input_output_aliases={} if held is None else {3: 0},
+        compiler_params=pltpu.CompilerParams(dimension_semantics=("arbitrary", "arbitrary"), vmem_limit_bytes=VMEM_BYTES),
+        cost_estimate=SMALL,
+    )(info, mine, other, *extra)
+
+
+def place_heads_kernel(info_ref, *refs):
+    own = pl.program_id(0) == info_ref[0]
+    one = jnp.where(own, refs[0][...], refs[2][...]).astype(f32)
+    two = jnp.where(own, refs[1][...], refs[3][...]).astype(f32)
+    out, query, key, value, gate, scalars, token = refs[-7:]
+    token[...] = jnp.zeros(token.shape, f32)
+    local, units = query.shape[1], one.shape[1]
+    out[...] = one[:, :local].T
+    query[...] = one[:, local:2 * local]
+    cut = units - 2 * local
+    key[:, :cut] = one[:, 2 * local:]
+    key[:, cut:] = two[:, :local - cut]
+    at = local - cut
+    value[...] = two[:, at:at + local]
+    gate[...] = two[:, at + local:at + 2 * local]
+    scalars[...] = two[:, at + 2 * local:at + 2 * local + HEAD_DIM]
+
+
+def place_heads(info, held, width, local, mine, other, row):
+    rows, units = mine[0].shape
+    block = 2 * TILE
+    per, inner = width // 2 // block, rows // block
+    both = pl.BlockSpec((block, units), lambda i, j, s: (j, 0))
+    tall = lambda columns: pl.BlockSpec((block, columns), lambda i, j, s: (i * per + row * inner + j, 0))
+    return pl.pallas_call(
+        place_heads_kernel,
+        grid_spec=pltpu.PrefetchScalarGridSpec(
+            num_scalar_prefetch=1,
+            grid=(2, inner),
+            in_specs=[both] * 4 + [pl.BlockSpec(memory_space=pl.ANY)] * len(held),
+            out_specs=[pl.BlockSpec((local, block), lambda i, j, s: (0, i * per + row * inner + j))] + [tall(local)] * 4 + [tall(HEAD_DIM), pl.BlockSpec((8, HEAD_DIM), lambda i, j, s: (0, 0))],
+        ),
+        out_shape=[jax.ShapeDtypeStruct((local, width), f32)]
+        + [jax.ShapeDtypeStruct((width, local), f32)] * 4
+        + [jax.ShapeDtypeStruct((width, HEAD_DIM), f32), jax.ShapeDtypeStruct((8, HEAD_DIM), f32)],
+        input_output_aliases={5 + i: i for i in range(len(held))},
+        compiler_params=pltpu.CompilerParams(dimension_semantics=("arbitrary", "arbitrary"), vmem_limit_bytes=VMEM_BYTES),
+        cost_estimate=SMALL,
+    )(info, *mine, *other, *held)
 
 
 def xor_pairs(size, mask):
     return [(i, i ^ mask) for i in range(size)]
 
 
-def tied(first, *rest):
-    return lax.optimization_barrier((first,) + rest)
-
-
-def gather_rows(mine):
+def swap(values, axis, mask):
+    return lax.ppermute(values, axis, xor_pairs(lax.axis_size(axis), mask))
+
+
+def gather_rows(mine, *others):
     size = lax.axis_size("tp")
-    half = mine.shape[0] // 2
-    across = lax.ppermute(mine, "tp", xor_pairs(size, 1))
-    down = lax.ppermute(mine, "tp", xor_pairs(size, 2))
-    far_top = lax.ppermute(down[:half], "tp", xor_pairs(size, 1))
-    far_low = lax.ppermute(across[half:], "tp", xor_pairs(size, 2))
-    return [mine, across, down, jnp.concatenate([far_top, far_low], axis=0)]
-
-
-def scatter_rows(parts):
-    size = lax.axis_size("tp")
-    mine, across, down, far = parts
-    half = mine.shape[0] // 2
-    far_top = lax.ppermute(far[:half], "tp", xor_pairs(size, 1))
-    far_low = lax.ppermute(far[half:], "tp", xor_pairs(size, 2))
-    down = jnp.concatenate([down[:half] + far_top, down[half:]], axis=0)
-    across = jnp.concatenate([across[:half], across[half:] + far_low], axis=0)
-    return (
-        mine.astype(f32)
-        + lax.ppermute(across, "tp", xor_pairs(size, 1)).astype(f32)
-        + lax.ppermute(down, "tp", xor_pairs(size, 2)).astype(f32)
-    )
-
-
-def sum_small(values, axis):
-    size, mask = lax.axis_size(axis), 1
-    while mask < size:
-        values = values + lax.ppermute(values, axis, xor_pairs(size, mask))
-        mask *= 2
+    if size != 4:
+        parts, mask = [mine], 1
+        while mask < size:
+            parts = parts + [swap(one, "tp", mask) for one in parts]
+            mask *= 2
+        return [[one] for one in parts]
+    across, down = after([swap(mine, "tp", 1), swap(mine, "tp", 2)], *others)
+    top, low = far_halves(across, down)
+    return [[mine], [across], [down], [swap(top, "tp", 1), swap(low, "tp", 2)]]
+
+
+def joined(part):
+    return part[0] if len(part) == 1 else jnp.concatenate(part, axis=0)
+
+
+def gather_weight(weight):
+    places, count = lax.axis_size("dp"), lax.axis_size("tp")
+    rows = weight.shape[0] // places
+    piece = lax.dynamic_slice_in_dim(weight, lax.axis_index("dp") * rows, rows, axis=0)
+    return lax.all_gather(piece, ("dp", "tp"), axis=0, tiled=True).reshape(places, count, rows, weight.shape[1])
+
+
+def sum_over(values, axis):
+    for i in range(lax.axis_size(axis).bit_length() - 1):
+        values = values + swap(values, axis, 1 << i)
     return values
-
-
-def line_sums(chunks):
-    size = lax.axis_size("dp")
-    stride = size // 4
-    hops = [
-        [(j, j + stride) for j in range(stride)] + [(j + 3 * stride, j + 2 * stride) for j in range(stride)],
-        [(j + stride, j + 2 * stride) for j in range(stride)] + [(j + 2 * stride, j + stride) for j in range(stride)],
-        [(j + stride, j) for j in range(stride)] + [(j + 2 * stride, j + 3 * stride) for j in range(stride)],
-    ]
-    place = lax.axis_index("dp") // stride
-    center = (place == 1) | (place == 2)
-    chunks = list(chunks)
-    count = len(chunks)
-    sums, wholes, results = {}, {}, []
-    gone = ()
-    for step in range(count + 2):
-        going = []
-        if step < count:
-            chunk = chunks[step]
-            mask = 2
-            while mask < stride:
-                chunk = chunk + lax.ppermute(chunk, "dp", xor_pairs(size, mask))
-                mask *= 2
-            going.append((0, step, chunk))
-        if 0 <= step - 1 < count:
-            going.append((1, step - 1, sums.pop(step - 1)))
-        if 0 <= step - 2 < count:
-            going.append((2, step - 2, wholes.pop(step - 2)))
-        held = lax.optimization_barrier(tuple(one[2] for one in going) + gone)
-        gone = ()
-        for (stage, which, _), value in zip(going, held):
-            moved = lax.ppermute(value, "dp", hops[stage])
-            gone += (moved,)
-            if stage == 0:
-                sums[which] = value + moved
-            elif stage == 1:
-                wholes[which] = value + moved
-            else:
-                results.append(jnp.where(center, value, moved))
-    return results
-
-
-def core_sum(keep, send):
-    return keep + lax.ppermute(send, "dp", xor_pairs(lax.axis_size("dp"), 1))
-
-
-def core_join(part, axis, first):
-    other = lax.ppermute(part, "dp", xor_pairs(lax.axis_size("dp"), 1))
-    low = jnp.where(first, part, other)
-    high = jnp.where(first, other, part)
-    return jnp.concatenate([low, high], axis=axis).astype(f32)
-
-
-def rms_scale(values):
-    return lax.rsqrt(jnp.mean(values * values, axis=-1, keepdims=True) + epsilon)
-
-
-def product(left, right):
-    return jnp.dot(left, right, preferred_element_type=f32)
-
-
-def product_t(left, right):
-    return jnp.einsum("td,ld->tl", left, right, preferred_element_type=f32)
-
-
-def outer(left, right):
-    return jnp.einsum("ta,tb->ab", left, right, preferred_element_type=f32).astype(bf16)
 
 
 def body(
@@ -609,138 +1170,209 @@
     mlp_up_weight,
     mlp_down_weight,
 ):
-    width = tokens.shape[2]
+    rows, width = tokens.shape[1:]
     half = width // 2
     heads = decay_log.shape[0]
-    first_core = lax.axis_index("dp") % 2 == 0
+    local = output_weight.shape[0]
+    units = mlp_gate_weight.shape[1]
+    place_at = lax.axis_index("dp") // (lax.axis_size("dp") // 4)
+    core = (lax.axis_index("dp") % 2).astype(jnp.int32)
     rank = lax.axis_index("tp").astype(jnp.int32)
     lengths = seq_lengths[0]
+    center = (place_at == 1) | (place_at == 2)
+    info = jnp.stack([core, center.astype(jnp.int32), rank, (place_at >= 2).astype(jnp.int32)])
+    lines = lax.axis_size("dp") == 8 and units % HEAD_DIM == 0
     starts = jnp.stack([rank, lengths[0], lengths[0] + lengths[1]])
 
-    def mine_first(values):
-        low, high = values[:, :half], values[:, half:]
-        return jnp.where(first_core, low, high), jnp.where(first_core, high, low)
-
-    token_parts = gather_rows(tokens[0])
-    weight_part = jnp.where(first_core, output_weight[:, :half], output_weight[:, half:])
-    weight_part, _ = tied(weight_part, token_parts[3])
-    weight_mine = jnp.concatenate(gather_rows(weight_part), axis=0)
-    weight_other = lax.ppermute(weight_mine, "dp", xor_pairs(lax.axis_size("dp"), 1))
-    weight_full = jnp.concatenate(
-        [jnp.where(first_core, weight_mine, weight_other), jnp.where(first_core, weight_other, weight_mine)], axis=1
-    )
-    cotangent_part, _ = tied(out_cotangent[0], weight_mine)
-
+    count = lax.axis_size("tp")
+    total = count * rows
     scalar_weight = jnp.pad(
         jnp.transpose(head_scalar_weight, (0, 2, 1)).reshape(width, 2 * heads), ((0, 0), (0, HEAD_DIM - 2 * heads))
     )
     pad_row = lambda row: jnp.pad(row, (0, HEAD_DIM - heads))[None]
     rates, biases = pad_row(decay_log), pad_row(decay_bias)
     taps = conv_weight.reshape(3 * CONV, -1)
-    inputs = jnp.concatenate(token_parts, axis=0).astype(f32)
-    scale_in = rms_scale(inputs)
-    normed_in = (inputs * scale_in * attn_norm_gain).astype(bf16)
-    query_proj = product(normed_in, query_weight).astype(bf16)
-    key_proj = product(normed_in, key_weight).astype(bf16)
-    value_proj = product(normed_in, value_weight).astype(bf16)
-    gate_proj = product(normed_in, out_gate_weight).astype(bf16)
-    scalar_proj = product(normed_in, scalar_weight)
+    in_weights = (query_weight, key_weight, value_weight, out_gate_weight, scalar_weight)
+    in_gain, mid_gain = attn_norm_gain[None], mlp_norm_gain[None]
+    across = lambda one: swap(one, "dp", 1)
+    weight_full = gather_weight(output_weight)
+    held = project([tokens[0]], 0, total, in_gain, in_weights, [])
+    token_parts = gather_rows(tokens[0], held[-1])
+    for which in range(1, count):
+        if len(token_parts[which]) > 1:
+            token_parts[which] = after(token_parts[which], held[-1])
+        held = project(token_parts[which], which * rows, total, in_gain, in_weights, held)
+    query_proj, key_proj, value_proj, gate_proj, scalar_proj, normed_in = held
     gated, *kept = mixer_forward(
-        starts, query_proj, key_proj, value_proj, gate_proj, scalar_proj, taps, rates, biases, head_norm_gain[None]
+        count, starts, query_proj, key_proj, value_proj, gate_proj, scalar_proj, taps, rates, biases, head_norm_gain[None]
     )
-    rows = tokens.shape[1]
-    order = lambda values, mask: jnp.concatenate([values[(m ^ mask) * rows:((m ^ mask) + 1) * rows] for m in range(4)], axis=0)
-    gated_parts = gather_rows(gated)
-    gated_full = jnp.concatenate([order(part, mask) for mask, part in enumerate(gated_parts)], axis=1)
-    middle = inputs + product(gated_full, weight_full)
-    scale_mid = rms_scale(middle)
-    normed_mid = (middle * scale_mid * mlp_norm_gain).astype(bf16)
-
-    gate_pre = product(normed_mid, mlp_gate_weight)
-    up_pre = product(normed_mid, mlp_up_weight)
-    sigmoid_gate = jax.nn.sigmoid(gate_pre)
-    silu_gate = gate_pre * sigmoid_gate
-    hidden = (silu_gate * up_pre).astype(bf16)
-    cotangent_part, _ = tied(cotangent_part, gated_parts[3])
-    cotangent_all = jnp.concatenate(gather_rows(cotangent_part), axis=0)
-    cot_keep, cot_send = mine_first(cotangent_all)
-    down_sum = core_sum(outer(hidden, cot_keep), outer(hidden, cot_send))
-    hidden_grad = product_t(cotangent_all, mlp_down_weight)
-    gate_grad = (hidden_grad * up_pre * sigmoid_gate * (1.0 + gate_pre * (1.0 - sigmoid_gate))).astype(bf16)
-    up_grad = (hidden_grad * silu_gate).astype(bf16)
-    split = lambda values: [values[m * rows:(m + 1) * rows] for m in range(4)]
-    mid_partial = (product_t(gate_grad, mlp_gate_weight) + product_t(up_grad, mlp_up_weight)).astype(bf16)
-    mid_normed_grad = scatter_rows(split(mid_partial))
-    mid_keep, mid_send = mine_first(normed_mid)
-    gate_sum = core_sum(outer(mid_keep, gate_grad), outer(mid_send, gate_grad))
-    up_sum = core_sum(outer(mid_keep, up_grad), outer(mid_send, up_grad))
-
-    middle_mine, scale_mine = middle[:rows], scale_mid[:rows]
-    unit_mid = middle_mine * scale_mine
-    gain_mid = jnp.sum(mid_normed_grad * unit_mid, axis=0)
-    unit_grad = mid_normed_grad * mlp_norm_gain
-    middle_grad = out_cotangent[0].astype(f32) + scale_mine * (
-        unit_grad - unit_mid * jnp.mean(unit_grad * unit_mid, axis=-1, keepdims=True)
-    )
-    attn_grad = jnp.concatenate(gather_rows(middle_grad.astype(bf16)), axis=0)
-    gated_grad = product_t(attn_grad, output_weight).astype(bf16)
-    result_partial, _ = tied(product(hidden, mlp_down_weight).astype(bf16), attn_grad)
-    result = middle_mine + scatter_rows(split(result_partial))
-    attn_keep, attn_send = mine_first(attn_grad)
-    out_sum = core_sum(outer(gated, attn_keep), outer(gated, attn_send))
-    query_low, key_low, value_low, gate_low, scalar_low, grad_taps, misc = mixer_backward(
-        starts, gated_grad, gate_proj, query_proj, key_proj, value_proj, scalar_proj, kept, taps, rates, biases, head_norm_gain[None]
-    )
-    in_keep, in_send = mine_first(normed_in)
-    gate_proj_sum = core_sum(outer(in_keep, gate_low), outer(in_send, gate_low))
-    query_sum = core_sum(outer(in_keep, query_low), outer(in_send, query_low))
-    key_sum = core_sum(outer(in_keep, key_low), outer(in_send, key_low))
-    value_sum = core_sum(outer(in_keep, value_low), outer(in_send, value_low))
-    in_partial = (
-        product_t(query_low, query_weight)
-        + product_t(key_low, key_weight)
-        + product_t(value_low, value_weight)
-        + product_t(gate_low, out_gate_weight)
-        + product_t(scalar_low, scalar_weight)
-    ).astype(bf16)
-    in_normed_grad = scatter_rows(split(in_partial))
-    unit_in = inputs[:rows] * scale_in[:rows]
-    gain_in = jnp.sum(in_normed_grad * unit_in, axis=0)
-    unit_grad_in = in_normed_grad * attn_norm_gain
-    input_grad = middle_grad + scale_in[:rows] * (
-        unit_grad_in - unit_in * jnp.mean(unit_grad_in * unit_in, axis=-1, keepdims=True)
-    )
-
-    cut = lambda values: jnp.split(values, 2, axis=0)
-    down_low, down_high = cut(down_sum)
-    gate_top, gate_low_rows = cut(gate_sum)
-    up_top, up_low_rows = cut(up_sum)
-    even = line_sums([down_low, gate_top, up_top, out_sum, query_sum, value_sum])
-    odd = line_sums([down_high, gate_low_rows, up_low_rows, gate_proj_sum, key_sum])
-    join = lambda part, axis: core_join(part, axis, first_core)
-    grad_down = join(jnp.concatenate([even[0], odd[0]], axis=0), 1)
-    grad_mlp_gate = join(jnp.concatenate([even[1], odd[1]], axis=0), 0)
-    grad_mlp_up = join(jnp.concatenate([even[2], odd[2]], axis=0), 0)
-    grad_output = join(even[3], 1)
-    grad_gate = join(odd[3], 0)
-    grad_query = join(even[4], 0)
-    grad_key = join(odd[4], 0)
-    grad_value = join(even[5], 0)
-
-    scalar_grad = jnp.einsum("td,tl->dl", normed_in, scalar_low, preferred_element_type=f32)[:, :2 * heads]
-    shared = jnp.concatenate([gain_in, gain_mid, misc[2]])
-    shared = sum_small(shared, "tp")
-    small = jnp.concatenate([scalar_grad.reshape(-1), grad_taps.reshape(-1), misc[0, :heads], misc[1, :heads], shared])
-    small = sum_small(small, "dp")
+    gated_parts = [joined(one) for one in gather_rows(gated)]
+    cot_mine = after(out_cotangent[0], gated_parts[-1])
+    normed_mid, middle = middle_rows(rank[None], token_parts, gated_parts, weight_full, mid_gain)
+
+    cot_parts = [[cot_mine]] + [[swap(cot_mine, "tp", mask)] for mask in range(1, count)]
+    gates, ups, hidden = hidden_units(normed_mid, mlp_gate_weight, mlp_up_weight)
+    mid_other = after(across(normed_mid), hidden)
+    cot_parts[-1] = after(cot_parts[-1], hidden)
+    cot_flat = [one for part in cot_parts for one in part]
+    if lines:
+        sources = {}
+        chunk = lambda name, row: lambda: (*sources[name], row)
+        names = ["down", "gate", "up"]
+        even = Line(info, half // 4, [chunk(name, row) for name in names for row in (0, 2)] + [chunk("one", row) for row in range(4)])
+        odd = Line(info, half // 4, [chunk(name, row) for name in names for row in (1, 3)] + [chunk("two", row) for row in range(4)])
+        placed, waiting = {}, []
+
+        def settle(step):
+            if not waiting:
+                return step
+            name, row, mine, other = waiting.pop(0)
+            if name in names:
+                shape = (units, width) if name == "down" else (width, units)
+                placed[name], step = place(info, placed.get(name), shape, mine, other, row, name == "down", step)
+                return step
+            *placed["heads"], step = place_heads(
+                info, placed.get("heads", []), width, local, mine, [after(one, step) for one in other], row
+            )
+            return step
+
+        order = {
+            id(even): [(name, row) for name in names for row in (0, 2)] + [("one", row) for row in range(4)],
+            id(odd): [(name, row) for name in names for row in (1, 3)] + [("two", row) for row in range(4)],
+        }
+        firsts = {}
+
+        def tick(line, *others):
+            before = len(line.results)
+            step = line.advance(*others)
+            if len(line.results) > before:
+                name, row = order[id(line)][before]
+                value = line.results[-1]
+                other = across(value)
+                if name == "one":
+                    firsts[row] = (value, other)
+                elif name == "two":
+                    waiting.append((name, row, [firsts[row][0], value], [firsts[row][1], other]))
+                else:
+                    waiting.append((name, row, value, other))
+            return step
+
+        def land(step, lines=(even, odd)):
+            for line in lines:
+                step = line.land(step)
+            return step
+
+        def ticks(step, lines=(even, odd)):
+            for line in lines:
+                step = tick(line, step)
+            return step
+
+        send = outer_half(info, False, [(cot_flat, hidden)])
+        sources["down"] = outer_half(info, True, [(cot_flat, hidden)], send), across(send)
+        step = even.begin()
+        step = odd.begin(step)
+
+        gate_grad, up_grad, mid_partial = hidden_grads(
+            rank[None], cot_parts, gates, ups, mlp_gate_weight, mlp_up_weight, mlp_down_weight, step
+        )
+        step = land(mid_partial)
+        mid_normed_grad = lax.psum_scatter(after(mid_partial, step), "tp", scatter_dimension=0, tiled=True)
+        gate_other = across(gate_grad)
+        step = ticks(step)
+        gate_other = after(gate_other, step)
+        up_other = across(after(up_grad, gate_other))
+        sources["gate"] = (outer_half(info, True, [([normed_mid], gate_grad), ([mid_other], gate_other)], up_other),)
+        step = ticks(sources["gate"][0])
+        sources["up"] = (outer_half(info, True, [([normed_mid], up_grad), ([mid_other], up_other)], step),)
+        mid_normed_grad = after(mid_normed_grad, sources["up"][0])
+        middle_grad, attn_low, gain_mid = norm_grad([mid_normed_grad], middle, out_cotangent[0], mid_gain)
+        attn_all = lax.all_gather(attn_low, "tp", axis=0, tiled=True)
+        step = ticks(attn_low)
+        step = settle(step)
+        step = ticks(step)
+        gated_grad = gated_grads(count, rank[None], attn_all, output_weight, step)
+        grads = mixer_backward(
+            count, starts, gated_grad, gate_proj, query_proj, key_proj, value_proj, scalar_proj, kept, taps, rates, biases, head_norm_gain[None]
+        )
+        flat_low, scalar_low, grad_taps, misc = grads
+        step = land(flat_low)
+        step = ticks(step)
+        one_send, two_send = head_outer(info, False, count, attn_all, gated, normed_in, flat_low, scalar_low, units, step)
+        one_other = across(one_send)
+        one_keep, two_keep = head_outer(info, True, count, attn_all, gated, normed_in, flat_low, scalar_low, units, one_send)
+        one_other = after(one_other, one_keep)
+        two_other = across(after(two_send, one_other))
+        step = settle(one_other)
+        sources["one"], sources["two"] = (one_keep, one_other), (two_keep, after(two_other, step))
+        step = tick(even, step)
+        in_partial = input_grads(count, rank[None], flat_low, scalar_low, in_weights, step)
+        step = tick(odd, in_partial)
+        in_normed_grad = lax.psum_scatter(after(in_partial, step), "tp", scatter_dimension=0, tiled=True)
+        step = settle(step)
+        hops = [("tp", 1 << i) for i in range(count.bit_length() - 1)] + [("dp", 1 << i) for i in range(lax.axis_size("dp").bit_length() - 1)]
+        small = None
+        while len(odd.results) < len(odd.chunks):
+            for line in (even, odd):
+                step = settle(step)
+                step = tick(line, step)
+                if line is even and even.step == 8:
+                    in_normed_grad = after(in_normed_grad, step)
+                    _, input_grad, gain_in = norm_grad([in_normed_grad], tokens[0], middle_grad, in_gain)
+                    small = jnp.concatenate([gain_in[0], gain_mid[0], misc[2]])
+                    result_partial = result_rows(count, rank[None], hidden, mlp_down_weight, input_grad)
+                    result_sum = lax.psum_scatter(result_partial, "tp", scatter_dimension=0, tiled=True)
+                elif small is not None and hops:
+                    axis, mask = hops.pop(0)
+                    small = small + after(swap(small, axis, mask), step)
+                    if hops and hops[0] == ("dp", 1):
+                        small = jnp.concatenate([small, grad_taps.reshape(-1), misc[0, :heads], misc[1, :heads]])
+        while waiting:
+            step = settle(step)
+        result = small_call(total_kernel, jax.ShapeDtypeStruct((rows, width), bf16), middle, result_sum)
+        grad_output, grad_query, grad_key, grad_value, grad_gate, scalar_sum = placed["heads"]
+        scalar_sum = scalar_sum[:, :2 * heads]
+        grad_down, grad_mlp_gate, grad_mlp_up = placed["down"], placed["gate"], placed["up"]
+    else:
+        over = lambda left, right: lax.psum(jnp.einsum("ta,tb->ab", left, right, preferred_element_type=f32).astype(bf16), "dp").astype(f32)
+        gate_grad, up_grad, mid_partial = hidden_grads(
+            rank[None], cot_parts, gates, ups, mlp_gate_weight, mlp_up_weight, mlp_down_weight
+        )
+        mid_normed_grad = lax.psum_scatter(mid_partial, "tp", scatter_dimension=0, tiled=True)
+        middle_grad, attn_low, gain_mid = norm_grad([mid_normed_grad], middle, out_cotangent[0], mid_gain)
+        attn_all = lax.all_gather(attn_low, "tp", axis=0, tiled=True)
+        gated_grad = gated_grads(count, rank[None], attn_all, output_weight)
+        flat_low, scalar_low, grad_taps, misc = mixer_backward(
+            count, starts, gated_grad, gate_proj, query_proj, key_proj, value_proj, scalar_proj, kept, taps, rates, biases, head_norm_gain[None]
+        )
+        in_partial = input_grads(count, rank[None], flat_low, scalar_low, in_weights)
+        in_normed_grad = lax.psum_scatter(in_partial, "tp", scatter_dimension=0, tiled=True)
+        _, input_grad, gain_in = norm_grad([in_normed_grad], tokens[0], middle_grad, in_gain)
+        result_partial = result_rows(count, rank[None], hidden, mlp_down_weight)
+        result_sum = lax.psum_scatter(result_partial, "tp", scatter_dimension=0, tiled=True)
+        result = small_call(total_kernel, jax.ShapeDtypeStruct((rows, width), bf16), middle, result_sum)
+        grad_down = over(hidden, jnp.concatenate([one for part in cot_parts for one in part], axis=0))
+        grad_mlp_gate, grad_mlp_up = over(normed_mid, gate_grad), over(normed_mid, up_grad)
+        blocks = attn_all.reshape(count, rows, width)
+        attn_rows = jnp.concatenate([lax.dynamic_index_in_dim(blocks, rank ^ m, 0, keepdims=False) for m in range(count)], axis=0)
+        grad_output = over(gated, attn_rows)
+        grad_query, grad_key, grad_value, grad_gate = [
+            over(normed_in, flat_low[:, i * local:(i + 1) * local]) for i in range(4)
+        ]
+        scalar_sum = over(normed_in, scalar_low[:, :2 * heads])
+        small = sum_over(jnp.concatenate([gain_in[0], gain_mid[0], misc[2]]), "tp")
+        small = jnp.concatenate([small, grad_taps.reshape(-1), misc[0, :heads], misc[1, :heads]])
+        hops = [("dp", 1 << i) for i in range(lax.axis_size("dp").bit_length() - 1)]
+    for axis, mask in hops:
+        small = small + swap(small, axis, mask)
     pieces = []
     at = 0
-    for size in (width * 2 * heads, grad_taps.size, heads, heads, width, width, HEAD_DIM):
+    for size in (width, width, HEAD_DIM, grad_taps.size, heads, heads):
         pieces.append(small[at:at + size])
         at += size
-    scalar_sum, taps_sum, log_sum, bias_sum, gain_in, gain_mid, gain_head = pieces
+    gain_in, gain_mid, gain_head, taps_sum, log_sum, bias_sum = pieces
     return (
-        result.astype(bf16)[None],
-        input_grad.astype(bf16)[None],
+        result[None],
+        input_grad[None],
         gain_in,
         grad_query,
         grad_key,

time: 900 us -> 820 us (0.911)
  Pallas kernels: 56.4 us -> 441 us
  matrix products: 203 us -> 0 us
  other arithmetic: 152 us -> 5.75 us
  waiting for transfers between devices: 209 us -> 143 us
  starting transfers between devices: 200 us -> 154 us
  local copies, waits for them, and re-layouts: 64 us -> 47.5 us
  between operations: 4.17 us -> 16.2 us
    pallas_call x0 -> x95, Pallas kernels: none -> 382 us  [the longest x24 97 us: advance(): pl.pallas_call(partial(line_step_kernel, len(now), len(later)), grid_spec...]
    dot_general x34 -> x0, matrix products: 201 us -> none  [the longest x9 80.9 us: product_t(): return jnp.einsum('td,ld->tl', left, right, preferred_element_type=f32)]
    ppermute x87 -> x90, waiting for transfers between devices: 209 us -> 143 us  [the longest x42 59.1 us: swap(): return lax.ppermute(values, axis, xor_pairs(lax.axis_size(axis), mask))]
    ppermute x87 -> x90, starting transfers between devices: 200 us -> 154 us  [the longest x24 77.4 us: send(): lax.ppermute(right, 'dp', hops(rightward))]
    add x30 -> x5, other arithmetic: 46 us -> 3.85 us  [body(): small = small + after(swap(small, axis, mask), step)]
    convert_element_type x11 -> x0, other arithmetic: 41.3 us -> none  [the longest x8 29.2 us: core_join(): return jnp.concatenate([low, high], axis=axis).astype(f32)]
    select_n x22 -> x0, other arithmetic: 40.2 us -> none  [the longest x8 19.8 us: core_join(): low = jnp.where(first, part, other)]
    slice x18 -> x1, local copies, waits for them, and re-layouts: 17.8 us -> 1.52 us  [body(): scalar_sum = scalar_sum[:, :2 * heads]]
  transfers between devices with their start and end apart: 87 -> 95, of which waited for: 30 -> 32; matrix products, arithmetic and copies ran while one was open for 36% -> 2% of each run, Pallas kernels for 6% -> 47%
where the time goes in v2:
time: 820 us; the launch traced here: 807 us
  Pallas kernels  441 us (54%)
  starting transfers between devices  154 us (19%)
  waiting for transfers between devices  143 us (17%)
  local copies, waits for them, and re-layouts  47.5 us (6%)
  between operations  16.2 us (2%)
    pallas_call x24, Pallas kernels, advance(): pl.pallas_call(partial(line_step_kernel, len(now), len(later)), grid_spec...  97 us
    ppermute x24, starting transfers between devices, send(): lax.ppermute(right, 'dp', hops(rightward))  77.4 us
    ppermute x42, waiting for transfers between devices, swap(): return lax.ppermute(values, axis, xor_pairs(lax.axis_size(axis), mask))  59.1 us
    ppermute x24, waiting for transfers between devices, send(): lax.ppermute(left, 'dp', hops(leftward))  46.9 us
    ppermute x42, starting transfers between devices, swap(): return lax.ppermute(values, axis, xor_pairs(lax.axis_size(axis), mask))  46.4 us
    pallas_call x12, Pallas kernels, place(): pl.pallas_call(partial(place_kernel, turned), grid_spec=pltpu.PrefetchSca...  45.9 us
    pallas_call x4, Pallas kernels, outer_half(): pl.pallas_call(partial(outer_kernel, [len(lefts) for lefts, _ in sides]),...  41 us
    ppermute x24, waiting for transfers between devices, send(): lax.ppermute(right, 'dp', hops(rightward))  37.1 us
  transfers between devices with their start and end apart: 95, of which 32 were waited for; matrix products, arithmetic and copies ran while one was open for 2% of the time, Pallas kernels for 47%

profile of v2, /device:TPU:1, one launch (start us, length us, event | category | flops | bytes accessed | tf_op | source)
XLA Modules:
  0.0 807.4 jit_solution(11496911110116054341)
XLA Ops:
  14.3 7.3 shard_map.305
  21.6 14.6 %collective-permute-done.refs_0_ = bf16[256,2048]{1,0:T(8,128)(2,1)S(1)} collective-permute-done((bf16[256,2048]{1,0:T(8,128)(2,1)}, bf16[256,2048]{1,0:T(8,128)(2,1)S(1)}, u32[]{:S(2)}, u32[]{:S(2)}) %collective-permute-start) | collective-permute-done | bytes 1048608 | tf_op jit(solution)/shard_map/ppermute | solution.py:1120
  46.4 7.5 shard_map.308
  53.9 7.5 shard_map.309
  62.3 7.3 shard_map.311
  69.6 24.8 %shard_map.312 = (bf16[1024,512]{1,0:T(8,128)(2,1)}, bf16[1024,512]{1,0:T(8,128)(2,1)}, bf16[1024,512]{1,0:T(8,128)(2,1)}, bf16[1024,512]{1,0:T(8,128)(2,1)}, bf...) custom-call(s32[3]{0:T(128)} %pad_add_fusion.starts_ref, ...), custom_call_target="tpu_custom_call" | custom-call | tf_op jit(solution)/shard_map/pallas_call | solution.py:233
  96.5 21.0 %collective-permute-done.4.refs_0_ = bf16[1024,512]{1,0:T(8,128)(2,1)S(1)} collective-permute-done((bf16[1024,512]{1,0:T(8,128)(2,1)}, bf16[1024,512]{1,0:T(8,128)(2,1)S(1)}, u32[]{:S(2)}, u32[]{:S(2)}) %collective-permute-start.4) | collective-permute-done | bytes 1048608 | tf_op jit(solution)/shard_map/ppermute | solution.py:1120
  125.3 7.1 collective-permute-done.6
  138.4 17.7 %shard_map.315 = (bf16[1024,2048]{1,0:T(8,128)(2,1)}, f32[256,2048]{1,0:T(8,128)}) custom-call(s32[1]{0:T(128)} %bitcast.rank_ref, bf16[256,2048]{1,0:T(8,128)(2,1)} %bitcast.37, bf16[256,2048]{1,0:T(8,128)(2,1)} %get-tuple-element.211.across_ref.refs_0_.refs_1_, bf16[256,2048]{1,0:T(8,128)(2,1)} %get-tuple-element.212.down_ref.refs_0_.refs_2_, ...), custom_call_target="tpu_custom_call" | custom-call | tf_op jit(solution)/shard_map/pallas_call | solution.py:570
  156.1 19.6 %shard_map.316 = (bf16[1024,1408]{1,0:T(8,128)(2,1)}, bf16[1024,1408]{1,0:T(8,128)(2,1)}, bf16[1024,1408]{1,0:T(8,128)(2,1)}) custom-call(bf16[1024,2048]{1,0:T(8,128)(2,1)} %get-tuple-element.245.x_ref.refs_0_, bf16[2048,1408]{1,0:T(8,128)(2,1)} %refs_6_.3, bf16[2048,1408]{1,0:T(8,128)(2,1)} %refs_7_.1), custom_call_target="tpu_custom_call" | custom-call | tf_op jit(solution)/shard_map/pallas_call | solution.py:628
  184.2 8.1 %shard_map.319.refs_5_ = bf16[1024,1408]{1,0:T(8,128)(2,1)} custom-call(s32[4]{0:T(128)} %pad_add_fusion.1.info_ref, bf16[256,2048]{1,0:T(8,128)(2,1)} %shard_map.317.refs_0_, bf16[256,2048]{1,0:T(8,128)(2,1)} %copy-done.9, bf16[256,2048]{1,0:T(8,128)(2,1)} %copy-done.10, bf16[256,2048]{1,0:T(8,128)(2,1)} %shard_map.318.refs_3_, ...), custom_call_target="tpu_custom_call" | custom-call | tf_op jit(solution)/shard_map/pallas_call | solution.py:667
  194.7 8.4 %shard_map.320.refs_0_ = bf16[1024,1408]{1,0:T(8,128)(2,1)} custom-call(s32[4]{0:T(128)} %pad_add_fusion.1.info_ref, bf16[256,2048]{1,0:T(8,128)(2,1)} %shard_map.317.refs_0_, bf16[256,2048]{1,0:T(8,128)(2,1)} %copy-done.9, bf16[256,2048]{1,0:T(8,128)(2,1)} %copy-done.10, bf16[256,2048]{1,0:T(8,128)(2,1)} %shard_map.318.refs_3_, ...), custom_call_target="tpu_custom_call" | custom-call | tf_op jit(solution)/shard_map/pallas_call | solution.py:667
  216.1 30.8 %shard_map.323 = (bf16[1024,1408]{1,0:T(8,128)(2,1)}, bf16[1024,1408]{1,0:T(8,128)(2,1)}, bf16[1024,2048]{1,0:T(8,128)(2,1)}) custom-call(s32[1]{0:T(128)} %bitcast.rank_ref, bf16[256,2048]{1,0:T(8,128)(2,1)} %shard_map.317.refs_0_, bf16[256,2048]{1,0:T(8,128)(2,1)} %copy-done.9, bf16[256,2048]{1,0:T(8,128)(2,1)} %copy-done.10, ...), custom_call_target="tpu_custom_call" | custom-call | tf_op jit(solution)/shard_map/pallas_call | solution.py:713
  273.5 12.5 %shard_map.332.refs_2_.refs_7_.refs_0_ = bf16[1024,1408]{1,0:T(8,128)(2,1)} custom-call(s32[4]{0:T(128)} %pad_add_fusion.1.info_ref, bf16[1024,2048]{1,0:T(8,128)(2,1)} %get-tuple-element.245.x_ref.refs_0_, bf16[1024,1408]{1,0:T(8,128)(2,1)} %get-tuple-element.253.refs_1_, bf16[1024,2048]{1,0:T(8,128)(2,1)} %shard_map.327.refs_2_, ...), custom_call_target="tpu_custom_call" | custom-call | tf_op jit(solution)/shard_map/pallas_call | solution.py:667
  286.0 9.9 %collective-permute-done.21.refs_5_ = bf16[256,1408]{1,0:T(8,128)(2,1)} collective-permute-done((bf16[256,1408]{1,0:T(8,128)(2,1)}, bf16[256,1408]{1,0:T(8,128)(2,1)}, u32[]{:S(2)}, u32[]{:S(2)}) %collective-permute-start.21) | collective-permute-done | bytes 720928 | tf_op jit(solution)/shard_map/ppermute | solution.py:985
  304.5 12.0 %shard_map.335.refs_1_.refs_0_ = bf16[1024,1408]{1,0:T(8,128)(2,1)} custom-call(s32[4]{0:T(128)} %pad_add_fusion.1.info_ref, bf16[1024,2048]{1,0:T(8,128)(2,1)} %get-tuple-element.245.x_ref.refs_0_, bf16[1024,1408]{1,0:T(8,128)(2,1)} %get-tuple-element.252.refs_1_, bf16[1024,2048]{1,0:T(8,128)(2,1)} %shard_map.327.refs_2_, bf16[1024,1408]{1,0:T(8,128)(2,1)} %copy-done.7, ...), custom_call_target="tpu_custom_call" | custom-call | tf_op jit(solution)/shard_map/pallas_call | solution.py:667
  333.9 6.6 collective-permute-done.25.refs_3_
  400.3 6.5 shard_map.343.gg_ref
  406.8 33.9 %shard_map.344 = (bf16[1024,2048]{1,0:T(8,128)(2,1)}, bf16[1024,128]{1,0:T(8,128)(2,1)}, f32[12,512]{1,0:T(8,128)}, f32[8,128]{1,0:T(8,128)}) custom-call(s32[3]{0:T(128)} %pad_add_fusion.starts_ref, bf16[1024,512]{1,0:T(8,128)(2,1)} %shard_map.343.gg_ref, bf16[1024,512]{1,0:T(8,128)(2,1)} %get-tuple-element.278.mixed_ref, ...), custom_call_target="tpu_custom_call" | custom-call | tf_op jit(solution)/shard_map/pallas_call | solution.py:465
  450.6 11.6 %shard_map.349 = (bf16[1024,1408]{1,0:T(8,128)(2,1)}, bf16[1024,1408]{1,0:T(8,128)(2,1)}) custom-call(s32[4]{0:T(128)} %pad_add_fusion.1.info_ref, bf16[1024,2048]{1,0:T(8,128)(2,1)} %all-gather.5.cloned.1.call-done.rows_ref.refs_0_.refs_1_.refs_2_.refs_3_, bf16[1024,2048]{1,0:T(8,128)(2,1)} %all-gather.5.cloned.1.call-done.rows_ref.refs_0_.refs_1_.refs_2_.refs_3_, ...), custom_call_target="tpu_custom_call" | custom-call | tf_op jit(solution)/shard_map/pallas_call | solution.py:913
  466.4 11.8 %shard_map.350 = (bf16[1024,1408]{1,0:T(8,128)(2,1)}, bf16[1024,1408]{1,0:T(8,128)(2,1)}) custom-call(s32[4]{0:T(128)} %pad_add_fusion.1.info_ref, bf16[1024,2048]{1,0:T(8,128)(2,1)} %all-gather.5.cloned.1.call-done.rows_ref.refs_0_.refs_1_.refs_2_.refs_3_, bf16[1024,2048]{1,0:T(8,128)(2,1)} %all-gather.5.cloned.1.call-done.rows_ref.refs_0_.refs_1_.refs_2_.refs_3_, ...), custom_call_target="tpu_custom_call" | custom-call | tf_op jit(solution)/shard_map/pallas_call | solution.py:913
  509.5 15.4 %shard_map.354.refs_7_.refs_0_ = bf16[1024,2048]{1,0:T(8,128)(2,1)} custom-call(s32[1]{0:T(128)} %bitcast.rank_ref, bf16[1024,2048]{1,0:T(8,128)(2,1)} %get-tuple-element.288.refs_2_.refs_6_.grad_ref, bf16[1024,128]{1,0:T(8,128)(2,1)} %get-tuple-element.289.refs_7_.scalar_ref, bf16[2048,512]{1,0:T(8,128)(2,1)} %refs_0_.1, bf16[2048,512]{1,0:T(8,128)(2,1)} %refs_1_.1, ...), custom_call_target="tpu_custom_call" | custom-call | tf_op jit(solution)/shard_map/pallas_call | solution.py:741
  596.4 11.1 %shard_map.368 = bf16[1024,2048]{1,0:T(8,128)(2,1)} custom-call(s32[1]{0:T(128)} %bitcast.rank_ref, bf16[1024,1408]{1,0:T(8,128)(2,1)} %get-tuple-element.246.refs_1_.refs_4_.hidden_ref, bf16[1408,2048]{1,0:T(8,128)(2,1)} %weight_ref.3, bf16[256,2048]{1,0:T(8,128)(2,1)} %get-tuple-element.330.refs_0_), custom_call_target="tpu_custom_call" | custom-call | tf_op jit(solution)/shard_map/pallas_call | solution.py:765
  621.5 7.0 collective-permute-done.54.refs_4_
  (444 shorter events, 471.3 us)
Async XLA Ops:
  7.2 131.2 %all-gather.3.cloned.1.call-start = ((), (), s32[]{:S(2)}) async-start(), calls=%async_computation.3 | async-start | bytes 8650752 | tf_op jit(solution)/shard_map/all_gather | solution.py:1144
  8.9 307.5 %reduce-scatter.4.cloned.1.call-start = ((), (), s32[]{:S(2)}) async-start(), calls=%async_computation.4 | async-start | bytes 5242880 | tf_op jit(solution)/shard_map/reduce_scatter | solution.py:1279
  134.5 41.2 %collective-permute-start.10 = (bf16[256,2048]{1,0:T(8,128)(2,1)}, bf16[256,2048]{1,0:T(8,128)(2,1)S(1)}, u32[]{:S(2)}, u32[]{:S(2)}) collective-permute-start(bf16[256,2048]{1,0:T(8,128)(2,1)} %shard_map.317.refs_0_), channel_id=1, source_target_pairs={{0,24},{8,16},{16,8},{24,0},{1,25},{9,17},{17,9},{25,1},{2,26},{10... | collective-permute-start | bytes 3145736 | tf_op jit(solution)/shard_map/ppermute | solution.py:1120
  136.8 43.6 %collective-permute-start.8 = (bf16[256,2048]{1,0:T(8,128)(2,1)}, bf16[256,2048]{1,0:T(8,128)(2,1)S(1)}, u32[]{:S(2)}, u32[]{:S(2)}) collective-permute-start(bf16[256,2048]{1,0:T(8,128)(2,1)} %shard_map.317.refs_0_), channel_id=1, source_target_pairs={{0,8},{8,0},{16,24},{24,16},{1,9},{9,1},{17,25},{25,17},{2,10},{10... | collective-permute-start | bytes 3145736 | tf_op jit(solution)/shard_map/ppermute | solution.py:1120
  137.8 45.4 %collective-permute-start.9 = (bf16[256,2048]{1,0:T(8,128)(2,1)}, bf16[256,2048]{1,0:T(8,128)(2,1)S(1)}, u32[]{:S(2)}, u32[]{:S(2)}) collective-permute-start(bf16[256,2048]{1,0:T(8,128)(2,1)} %shard_map.317.refs_0_), channel_id=1, source_target_pairs={{0,16},{8,24},{16,0},{24,8},{1,17},{9,25},{17,1},{25,9},{2,18},{10... | collective-permute-start | bytes 3145736 | tf_op jit(solution)/shard_map/ppermute | solution.py:1120
  207.5 39.4 %collective-permute-start.14 = (bf16[256,1408]{1,0:T(8,128)(2,1)}, bf16[256,1408]{1,0:T(8,128)(2,1)S(1)}, u32[]{:S(2)}, u32[]{:S(2)}) collective-permute-start(bf16[256,1408]{1,0:T(8,128)(2,1)} %shard_map.321.refs_2_.refs_3_), channel_id=1, source_target_pairs={{0,2},{1,3},{8,10},{9,11},{16,18},{17,19},{24,26},{25,27}} | collective-permute-start | bytes 2162696 | tf_op jit(solution)/shard_map/ppermute | solution.py:985
  210.5 36.4 %collective-permute-start.15 = (bf16[256,1408]{1,0:T(8,128)(2,1)}, bf16[256,1408]{1,0:T(8,128)(2,1)S(1)}, u32[]{:S(2)}, u32[]{:S(2)}) collective-permute-start(bf16[256,1408]{1,0:T(8,128)(2,1)} %shard_map.321.refs_2_.refs_3_), channel_id=1, source_target_pairs={{6,4},{7,5},{14,12},{15,13},{22,20},{23,21},{30,28},{31,29}} | collective-permute-start | bytes 2162696 | tf_op jit(solution)/shard_map/ppermute | solution.py:985
  214.0 34.0 %collective-permute-start.12 = (bf16[256,1408]{1,0:T(8,128)(2,1)}, bf16[256,1408]{1,0:T(8,128)(2,1)S(1)}, u32[]{:S(2)}, u32[]{:S(2)}) collective-permute-start(bf16[256,1408]{1,0:T(8,128)(2,1)} %shard_map.322.refs_9_.refs_2_.refs_3_), channel_id=1, source_target_pairs={{0,2},{1,3},{8,10},{9,11},{16,18},{17,19},{24,26},{25,27}} | collective-permute-start | bytes 2162696 | tf_op jit(solution)/shard_map/ppermute | solution.py:985
  215.4 32.6 %collective-permute-start.13 = (bf16[256,1408]{1,0:T(8,128)(2,1)}, bf16[256,1408]{1,0:T(8,128)(2,1)S(1)}, u32[]{:S(2)}, u32[]{:S(2)}) collective-permute-start(bf16[256,1408]{1,0:T(8,128)(2,1)} %shard_map.322.refs_9_.refs_2_.refs_3_), channel_id=1, source_target_pairs={{6,4},{7,5},{14,12},{15,13},{22,20},{23,21},{30,28},{31,29}} | collective-permute-start | bytes 2162696 | tf_op jit(solution)/shard_map/ppermute | solution.py:985
  249.1 151.2 %all-gather.5.cloned.1.call-start = ((), (), s32[]{:S(2)}) async-start(), calls=%async_computation.5 | async-start | bytes 5242880 | tf_op jit(solution)/shard_map/all_gather | solution.py:1289
  263.8 36.4 %collective-permute-start.19 = (bf16[256,1408]{1,0:T(8,128)(2,1)}, bf16[256,1408]{1,0:T(8,128)(2,1)}, u32[]{:S(2)}, u32[]{:S(2)}) collective-permute-start(bf16[256,1408]{1,0:T(8,128)(2,1)} %get-tuple-element.258.refs_3_), channel_id=1, source_target_pairs={{0,2},{1,3},{2,4},{3,5},{8,10},{9,11},{10,12},{11,13},{16,18},{17,... | collective-permute-start | bytes 2162696 | tf_op jit(solution)/shard_map/ppermute | solution.py:985
  265.9 30.0 %collective-permute-start.21 = (bf16[256,1408]{1,0:T(8,128)(2,1)}, bf16[256,1408]{1,0:T(8,128)(2,1)}, u32[]{:S(2)}, u32[]{:S(2)}) collective-permute-start(bf16[256,1408]{1,0:T(8,128)(2,1)} %get-tuple-element.260.refs_3_), channel_id=1, source_target_pairs={{0,2},{1,3},{2,4},{3,5},{8,10},{9,11},{10,12},{11,13},{16,18},{17,... | collective-permute-start | bytes 2162696 | tf_op jit(solution)/shard_map/ppermute | solution.py:985
  321.8 269.3 %reduce-scatter.6.cloned.1.call-start = ((), (), s32[]{:S(2)}) async-start(), calls=%async_computation.6 | async-start | bytes 5242880 | tf_op jit(solution)/shard_map/reduce_scatter | solution.py:1310
  381.3 59.3 %collective-permute-start.34 = (bf16[256,1408]{1,0:T(8,128)(2,1)}, bf16[256,1408]{1,0:T(8,128)(2,1)S(1)}, u32[]{:S(2)}, u32[]{:S(2)}) collective-permute-start(bf16[256,1408]{1,0:T(8,128)(2,1)} %get-tuple-element.293.refs_1_), channel_id=1, source_target_pairs={{0,2},{1,3},{2,4},{3,5},{4,6},{5,7},{8,10},{9,11},{10,12},{11,13},... | collective-permute-start | bytes 2162696 | tf_op jit(solution)/shard_map/ppermute | solution.py:985
  382.7 58.0 %collective-permute-start.35 = (bf16[256,1408]{1,0:T(8,128)(2,1)}, bf16[256,1408]{1,0:T(8,128)(2,1)S(1)}, u32[]{:S(2)}, u32[]{:S(2)}) collective-permute-start(bf16[256,1408]{1,0:T(8,128)(2,1)} %get-tuple-element.294.refs_2_), channel_id=1, source_target_pairs={{6,4},{7,5},{4,2},{5,3},{2,0},{3,1},{14,12},{15,13},{12,10},{13,11... | collective-permute-start | bytes 2162696 | tf_op jit(solution)/shard_map/ppermute | solution.py:985
  397.5 44.5 %collective-permute-start.32 = (bf16[256,1408]{1,0:T(8,128)(2,1)}, bf16[256,1408]{1,0:T(8,128)(2,1)S(1)}, u32[]{:S(2)}, u32[]{:S(2)}) collective-permute-start(bf16[256,1408]{1,0:T(8,128)(2,1)} %get-tuple-element.291.refs_1_), channel_id=1, source_target_pairs={{0,2},{1,3},{2,4},{3,5},{4,6},{5,7},{8,10},{9,11},{10,12},{11,13},... | collective-permute-start | bytes 2162696 | tf_op jit(solution)/shard_map/ppermute | solution.py:985
  399.0 43.0 %collective-permute-start.33 = (bf16[256,1408]{1,0:T(8,128)(2,1)}, bf16[256,1408]{1,0:T(8,128)(2,1)S(1)}, u32[]{:S(2)}, u32[]{:S(2)}) collective-permute-start(bf16[256,1408]{1,0:T(8,128)(2,1)} %get-tuple-element.292.refs_2_), channel_id=1, source_target_pairs={{6,4},{7,5},{4,2},{5,3},{2,0},{3,1},{14,12},{15,13},{12,10},{13,11... | collective-permute-start | bytes 2162696 | tf_op jit(solution)/shard_map/ppermute | solution.py:985
  479.8 45.1 %collective-permute-start.40 = (bf16[1024,1408]{1,0:T(8,128)(2,1)}, bf16[1024,1408]{1,0:T(8,128)(2,1)S(1)}, u32[]{:S(2)}, u32[]{:S(2)}) collective-permute-start(bf16[1024,1408]{1,0:T(8,128)(2,1)} %shard_map.355), channel_id=1, source_target_pairs={{0,1},{1,0},{2,3},{3,2},{4,5},{5,4},{6,7},{7,6},{8,9},{9,8},{10,11... | collective-permute-start | bytes 8650760 | tf_op jit(solution)/shard_map/ppermute | solution.py:1120
  486.9 39.6 %collective-permute-start.41 = (bf16[256,1408]{1,0:T(8,128)(2,1)}, bf16[256,1408]{1,0:T(8,128)(2,1)}, u32[]{:S(2)}, u32[]{:S(2)}) collective-permute-start(bf16[256,1408]{1,0:T(8,128)(2,1)} %get-tuple-element.310.refs_3_), channel_id=1, source_target_pairs={{0,2},{1,3},{2,4},{3,5},{4,6},{5,7},{8,10},{9,11},{10,12},{11,13},... | collective-permute-start | bytes 2162696 | tf_op jit(solution)/shard_map/ppermute | solution.py:985
  491.8 34.7 %collective-permute-start.42 = (bf16[256,1408]{1,0:T(8,128)(2,1)}, bf16[256,1408]{1,0:T(8,128)(2,1)}, u32[]{:S(2)}, u32[]{:S(2)}) collective-permute-start(bf16[256,1408]{1,0:T(8,128)(2,1)} %get-tuple-element.311.refs_4_), channel_id=1, source_target_pairs={{6,4},{7,5},{4,2},{5,3},{2,0},{3,1},{14,12},{15,13},{12,10},{13,11... | collective-permute-start | bytes 2162696 | tf_op jit(solution)/shard_map/ppermute | solution.py:985
  530.8 266.9 %reduce-scatter.8.cloned.1.call-start = ((), (), s32[]{:S(2)}) async-start(), calls=%async_computation.7 | async-start | bytes 5242880 | tf_op jit(solution)/shard_map/reduce_scatter | solution.py:1323
  538.0 37.0 %collective-permute-start.49 = (bf16[256,1408]{1,0:T(8,128)(2,1)S(1)}, bf16[256,1408]{1,0:T(8,128)(2,1)}, u32[]{:S(2)}, u32[]{:S(2)}) collective-permute-start(bf16[256,1408]{1,0:T(8,128)(2,1)S(1)} %copy-done.37), channel_id=1, source_target_pairs={{0,1},{1,0},{2,3},{3,2},{4,5},{5,4},{6,7},{7,6},{8,9},{9,8},{10,11... | collective-permute-start | bytes 2162696 | tf_op jit(solution)/shard_map/ppermute | solution.py:1120
  628.5 30.7 %collective-permute-start.64 = (bf16[256,1408]{1,0:T(8,128)(2,1)S(1)}, bf16[256,1408]{1,0:T(8,128)(2,1)S(1)}, u32[]{:S(2)}, u32[]{:S(2)}) collective-permute-start(bf16[256,1408]{1,0:T(8,128)(2,1)S(1)} %copy-done.33), channel_id=1, source_target_pairs={{0,1},{1,0},{2,3},{3,2},{4,5},{5,4},{6,7},{7,6},{8,9},{9,8},{10,11... | collective-permute-start | bytes 2162696 | tf_op jit(solution)/shard_map/ppermute | solution.py:1120
  749.4 35.4 %collective-permute-start.88 = (bf16[256,1408]{1,0:T(8,128)(2,1)}, bf16[256,1408]{1,0:T(8,128)(2,1)S(1)}, u32[]{:S(2)}, u32[]{:S(2)}) collective-permute-start(bf16[256,1408]{1,0:T(8,128)(2,1)} %get-tuple-element.377.refs_1_.refs_0_), channel_id=1, source_target_pairs={{0,1},{1,0},{2,3},{3,2},{4,5},{5,4},{6,7},{7,6},{8,9},{9,8},{10,11... | collective-permute-start | bytes 2162696 | tf_op jit(solution)/shard_map/ppermute | solution.py:1120
  (143 other events, 1725.5 us)
Sparse Core Ops, SparseCore 0:
  11.5 88.4 all-gather.2
  249.2 50.7 reduce-scatter.3
  321.9 52.9 all-gather.4
  530.9 50.8 reduce-scatter.5
  607.6 51.4 reduce-scatter.7

commit v3 on v2

--- a/solution.py
+++ b/solution.py
@@ -504,9 +504,14 @@
     return pltpu.CompilerParams(dimension_semantics=("arbitrary",), vmem_limit_bytes=VMEM_BYTES)
 
 
-def project_kernel(pieces, *refs):
-    gain_ref, weights, outs = refs[pieces], refs[pieces + 1:pieces + 6], refs[-6:]
-    x = whole(refs[:pieces]).astype(f32)
+def project_kernel(sizes, *refs):
+    parts, refs = split_pieces(refs, sizes)
+    gain_ref, weights, outs, held = refs[0], refs[1:6], refs[-7:-1], refs[-1]
+    if len(sizes) > 1:
+        pick(len(sizes), parts, held)
+        x = held[...].astype(f32)
+    else:
+        x = whole(parts[0]).astype(f32)
     scale = lax.rsqrt(jnp.mean(x * x, axis=-1, keepdims=True) + epsilon)
     normed = (x * scale * gain_ref[...]).astype(bf16)
     outs[5][...] = normed
@@ -514,24 +519,25 @@
         out[...] = dot(normed, weight[...]).astype(out.dtype)
 
 
-def project(pieces, at, total, gain, weights, held):
-    rows, depth = sum(one.shape[0] for one in pieces), pieces[0].shape[1]
-    first, count = at // rows, len(pieces)
+def project(parts, first, total, gain, weights, held, *others):
+    rows, depth = sum(one.shape[0] for one in parts[0]), parts[0][0].shape[1]
+    flat, sizes = [one for part in parts for one in part], [len(part) for part in parts]
     shapes = [jax.ShapeDtypeStruct((total, w.shape[1]), f32 if i == 4 else bf16) for i, w in enumerate(weights)]
     shapes.append(jax.ShapeDtypeStruct((total, depth), bf16))
     return pl.pallas_call(
-        partial(project_kernel, count),
-        grid=(1,),
-        in_specs=[once(one.shape) for one in pieces]
+        partial(project_kernel, sizes),
+        grid=(len(parts),),
+        in_specs=[once(one.shape) for one in flat]
         + [once(gain.shape)]
         + [once(w.shape) for w in weights]
-        + [pl.BlockSpec(memory_space=pl.ANY)] * len(held),
-        out_specs=[pl.BlockSpec((rows, s.shape[1]), lambda i: (first, 0)) for s in shapes],
+        + [pl.BlockSpec(memory_space=pl.ANY)] * (len(held) + len(others)),
+        out_specs=[pl.BlockSpec((rows, s.shape[1]), lambda i: (first + i, 0)) for s in shapes],
         out_shape=shapes,
-        input_output_aliases={count + 6 + i: i for i in range(len(held))},
+        scratch_shapes=[pltpu.VMEM((rows, depth), bf16)],
+        input_output_aliases={len(flat) + 6 + i: i for i in range(len(held))},
         compiler_params=params(),
         cost_estimate=SMALL,
-    )(*pieces, gain, *weights, *held)
+    )(*flat, gain, *weights, *held, *others)
 
 
 def pick(count, refs, held):
@@ -542,16 +548,16 @@
             held[...] = whole(refs[which]) if isinstance(refs[which], (list, tuple)) else refs[which][...]
 
 
-def middle_kernel(sizes, rank_ref, *refs):
+def middle_kernel(sizes, *refs):
     count = len(sizes)
     x_refs, refs = split_pieces(refs, sizes)
     g_refs = refs[:count]
-    weight_ref, gain_ref, normed_ref, own_ref, scr, x_scr = refs[count:]
+    own_weight, far_weight, gain_ref, normed_ref, own_ref, scr, x_scr = refs[count:]
     pick(count, x_refs, x_scr)
     gated = jnp.concatenate([one[...] for one in g_refs], axis=1)
     width = gated.shape[1] // count
     for a, b in column_cuts(scr.shape[1]):
-        weight = [weight_ref[:, rank_ref[0] ^ m, :, a:b].reshape(width, b - a) for m in range(count)]
+        weight = [own_weight[:, a:b]] + [far_weight[:, m, :, a:b].reshape(width, b - a) for m in range(count - 1)]
         scr[:, a:b] = dot(gated, jnp.concatenate(weight, axis=0)) + x_scr[:, a:b].astype(f32)
     middle = scr[...]
     scale = lax.rsqrt(jnp.mean(middle * middle, axis=-1, keepdims=True) + epsilon)
@@ -562,26 +568,23 @@
         own_ref[...] = middle
 
 
-def middle_rows(rank, x_parts, gated_parts, weight, gain):
+def middle_rows(x_parts, gated_parts, own_weight, far_weight, gain):
     count = len(x_parts)
     rows, depth = x_parts[0][0].shape
     width = gated_parts[0].shape[1]
     flat = [one for part in x_parts for one in part]
     return pl.pallas_call(
         partial(middle_kernel, [len(part) for part in x_parts]),
-        grid_spec=pltpu.PrefetchScalarGridSpec(
-            num_scalar_prefetch=1,
-            grid=(count,),
-            in_specs=[once(one.shape) for one in flat]
-            + [pl.BlockSpec((rows, width), lambda i, s, at=at: (i ^ at, 0)) for at in range(count)]
-            + [once(weight.shape), once(gain.shape)],
-            out_specs=[pl.BlockSpec((rows, depth), lambda i, s: (i, 0)), once((rows, depth))],
-            scratch_shapes=[pltpu.VMEM((rows, depth), f32), pltpu.VMEM((rows, depth), bf16)],
-        ),
+        grid=(count,),
+        in_specs=[once(one.shape) for one in flat]
+        + [pl.BlockSpec((rows, width), lambda i, at=at: (i ^ at, 0)) for at in range(count)]
+        + [once(own_weight.shape), once(far_weight.shape), once(gain.shape)],
+        out_specs=[pl.BlockSpec((rows, depth), lambda i: (i, 0)), once((rows, depth))],
         out_shape=[jax.ShapeDtypeStruct((count * rows, depth), bf16), jax.ShapeDtypeStruct((rows, depth), f32)],
+        scratch_shapes=[pltpu.VMEM((rows, depth), f32), pltpu.VMEM((rows, depth), bf16)],
         compiler_params=params(),
         cost_estimate=SMALL,
-    )(rank, *flat, *gated_parts, weight, gain)
+    )(*flat, *gated_parts, own_weight, far_weight, gain)
 
 
 def gated_grad_kernel(rank_ref, rows_ref, weight_ref, *refs):
@@ -1137,11 +1140,13 @@
     return part[0] if len(part) == 1 else jnp.concatenate(part, axis=0)
 
 
-def gather_weight(weight):
-    places, count = lax.axis_size("dp"), lax.axis_size("tp")
+def gather_weight(weight, before, last):
+    places = lax.axis_size("dp")
     rows = weight.shape[0] // places
     piece = lax.dynamic_slice_in_dim(weight, lax.axis_index("dp") * rows, rows, axis=0)
-    return lax.all_gather(piece, ("dp", "tp"), axis=0, tiled=True).reshape(places, count, rows, weight.shape[1])
+    piece = after(piece, before)
+    parts = after([swap(piece, "tp", mask) for mask in range(1, lax.axis_size("tp"))], last)
+    return lax.all_gather(jnp.stack(parts, axis=0), "dp", axis=0)
 
 
 def sum_over(values, axis):
@@ -1195,20 +1200,21 @@
     in_weights = (query_weight, key_weight, value_weight, out_gate_weight, scalar_weight)
     in_gain, mid_gain = attn_norm_gain[None], mlp_norm_gain[None]
     across = lambda one: swap(one, "dp", 1)
-    weight_full = gather_weight(output_weight)
-    held = project([tokens[0]], 0, total, in_gain, in_weights, [])
+    early = [taps, rates, biases, starts, info]
+    held = project([[tokens[0]]], 0, total, in_gain, in_weights, [], *early)
     token_parts = gather_rows(tokens[0], held[-1])
-    for which in range(1, count):
-        if len(token_parts[which]) > 1:
-            token_parts[which] = after(token_parts[which], held[-1])
-        held = project(token_parts[which], which * rows, total, in_gain, in_weights, held)
+    held = project(token_parts[1:3], 1, total, in_gain, in_weights, held)
+    if count == 4:
+        token_parts[-1] = after(token_parts[-1], held[-1])
+    held = project(token_parts[3:], 3, total, in_gain, in_weights, held)
+    far_weight = gather_weight(output_weight, token_parts[-1][-1], held[-1])
     query_proj, key_proj, value_proj, gate_proj, scalar_proj, normed_in = held
     gated, *kept = mixer_forward(
         count, starts, query_proj, key_proj, value_proj, gate_proj, scalar_proj, taps, rates, biases, head_norm_gain[None]
     )
     gated_parts = [joined(one) for one in gather_rows(gated)]
     cot_mine = after(out_cotangent[0], gated_parts[-1])
-    normed_mid, middle = middle_rows(rank[None], token_parts, gated_parts, weight_full, mid_gain)
+    normed_mid, middle = middle_rows(token_parts, gated_parts, output_weight, far_weight, mid_gain)
 
     cot_parts = [[cot_mine]] + [[swap(cot_mine, "tp", mask)] for mask in range(1, count)]
     gates, ups, hidden = hidden_units(normed_mid, mlp_gate_weight, mlp_up_weight)
@@ -1283,11 +1289,13 @@
         up_other = across(after(up_grad, gate_other))
         sources["gate"] = (outer_half(info, True, [([normed_mid], gate_grad), ([mid_other], gate_other)], up_other),)
         step = ticks(sources["gate"][0])
-        sources["up"] = (outer_half(info, True, [([normed_mid], up_grad), ([mid_other], up_other)], step),)
-        mid_normed_grad = after(mid_normed_grad, sources["up"][0])
+        mid_normed_grad = after(mid_normed_grad, step)
         middle_grad, attn_low, gain_mid = norm_grad([mid_normed_grad], middle, out_cotangent[0], mid_gain)
         attn_all = lax.all_gather(attn_low, "tp", axis=0, tiled=True)
-        step = ticks(attn_low)
+        sources["up"] = (outer_half(info, True, [([normed_mid], up_grad), ([mid_other], up_other)], attn_low),)
+        result_partial = result_rows(count, rank[None], hidden, mlp_down_weight, sources["up"][0])
+        result_sum = lax.psum_scatter(result_partial, "tp", scatter_dimension=0, tiled=True)
+        step = ticks(result_partial)
         step = settle(step)
         step = ticks(step)
         gated_grad = gated_grads(count, rank[None], attn_all, output_weight, step)
@@ -1298,15 +1306,17 @@
         step = land(flat_low)
         step = ticks(step)
         one_send, two_send = head_outer(info, False, count, attn_all, gated, normed_in, flat_low, scalar_low, units, step)
-        one_other = across(one_send)
         one_keep, two_keep = head_outer(info, True, count, attn_all, gated, normed_in, flat_low, scalar_low, units, one_send)
-        one_other = after(one_other, one_keep)
-        two_other = across(after(two_send, one_other))
-        step = settle(one_other)
-        sources["one"], sources["two"] = (one_keep, one_other), (two_keep, after(two_other, step))
-        step = tick(even, step)
-        in_partial = input_grads(count, rank[None], flat_low, scalar_low, in_weights, step)
-        step = tick(odd, in_partial)
+        step = land(one_keep)
+        one_other = across(after(one_send, step))
+        step = settle(step)
+        sources["one"] = one_keep, after(one_other, step)
+        two_other = across(after(two_send, sources["one"][1]))
+        step = tick(even, sources["one"][1])
+        sources["two"] = two_keep, after(two_other, step)
+        step = tick(odd, step)
+        in_partial = input_grads(count, rank[None], flat_low, scalar_low, in_weights, step, result_sum)
+        step = land(in_partial)
         in_normed_grad = lax.psum_scatter(after(in_partial, step), "tp", scatter_dimension=0, tiled=True)
         step = settle(step)
         hops = [("tp", 1 << i) for i in range(count.bit_length() - 1)] + [("dp", 1 << i) for i in range(lax.axis_size("dp").bit_length() - 1)]
@@ -1314,13 +1324,12 @@
         while len(odd.results) < len(odd.chunks):
             for line in (even, odd):
                 step = settle(step)
-                step = tick(line, step)
+                step = tick(line, step) if small is None else tick(line, step, small)
                 if line is even and even.step == 8:
                     in_normed_grad = after(in_normed_grad, step)
                     _, input_grad, gain_in = norm_grad([in_normed_grad], tokens[0], middle_grad, in_gain)
+                    result = small_call(total_kernel, jax.ShapeDtypeStruct((rows, width), bf16), middle, result_sum)
                     small = jnp.concatenate([gain_in[0], gain_mid[0], misc[2]])
-                    result_partial = result_rows(count, rank[None], hidden, mlp_down_weight, input_grad)
-                    result_sum = lax.psum_scatter(result_partial, "tp", scatter_dimension=0, tiled=True)
                 elif small is not None and hops:
                     axis, mask = hops.pop(0)
                     small = small + after(swap(small, axis, mask), step)
@@ -1328,7 +1337,6 @@
                         small = jnp.concatenate([small, grad_taps.reshape(-1), misc[0, :heads], misc[1, :heads]])
         while waiting:
             step = settle(step)
-        result = small_call(total_kernel, jax.ShapeDtypeStruct((rows, width), bf16), middle, result_sum)
         grad_output, grad_query, grad_key, grad_value, grad_gate, scalar_sum = placed["heads"]
         scalar_sum = scalar_sum[:, :2 * heads]
         grad_down, grad_mlp_gate, grad_mlp_up = placed["down"], placed["gate"], placed["up"]

time: 820 us -> 774 us (0.944)
  waiting for transfers between devices: 143 us -> 101 us
    ppermute x24, waiting for transfers between devices: 46.9 us -> 24.8 us  [send(): lax.ppermute(left, 'dp', hops(leftward))]
    ppermute x24, waiting for transfers between devices: 37.1 us -> 16.5 us  [send(): lax.ppermute(right, 'dp', hops(rightward))]
    ppermute x42 -> x45, starting transfers between devices: 46.4 us -> 40.3 us  [swap(): return lax.ppermute(values, axis, xor_pairs(lax.axis_size(axis), mask))]
    ppermute x42 -> x45, waiting for transfers between devices: 59.1 us -> 54.5 us  [swap(): return lax.ppermute(values, axis, xor_pairs(lax.axis_size(axis), mask))]
    pallas_call x4 -> x3, Pallas kernels: 29.5 us -> 25.4 us  [project(): pl.pallas_call(partial(project_kernel, sizes), grid=(len(parts),), in_spe...]
    unnamed x148 -> x160, local copies, waits for them, and re-layouts: 36.7 us -> 35.4 us
  transfers between devices with their start and end apart: 95 -> 98, of which waited for: 32 -> 21; matrix products, arithmetic and copies ran while one was open for 2% -> 3% of each run, Pallas kernels for 47% -> 54%
where the time goes in v3:
time: 774 us; the launch traced here: 763 us
  Pallas kernels  436 us (56%)
  starting transfers between devices  152 us (20%)
  waiting for transfers between devices  101 us (13%)
  local copies, waits for them, and re-layouts  48.3 us (6%)
  between operations  16.8 us (2%)
  other arithmetic  9.29 us (1%)
    pallas_call x24, Pallas kernels, advance(): pl.pallas_call(partial(line_step_kernel, len(now), len(later)), grid_spec...  97.4 us
    ppermute x24, starting transfers between devices, send(): lax.ppermute(right, 'dp', hops(rightward))  80.8 us
    ppermute x45, waiting for transfers between devices, swap(): return lax.ppermute(values, axis, xor_pairs(lax.axis_size(axis), mask))  54.5 us
    pallas_call x12, Pallas kernels, place(): pl.pallas_call(partial(place_kernel, turned), grid_spec=pltpu.PrefetchSca...  45.2 us
    pallas_call x4, Pallas kernels, outer_half(): pl.pallas_call(partial(outer_kernel, [len(lefts) for lefts, _ in sides]),...  40.9 us
    ppermute x45, starting transfers between devices, swap(): return lax.ppermute(values, axis, xor_pairs(lax.axis_size(axis), mask))  40.3 us
    unnamed x160, local copies, waits for them, and re-layouts  35.4 us
    pallas_call x1, Pallas kernels, mixer_backward(): pl.pallas_call(partial(backward_kernel, tiles, heads), grid_spec=pltpu.Pr...  33.9 us
  transfers between devices with their start and end apart: 98, of which 21 were waited for; matrix products, arithmetic and copies ran while one was open for 3% of the time, Pallas kernels for 54%

profile of v3, /device:TPU:1, one launch (start us, length us, event | category | flops | bytes accessed | tf_op | source)
XLA Modules:
  0.0 763.5 jit_solution(9854223034773700656)
XLA Ops:
  19.6 7.3 shard_map.305
  40.0 10.8 %shard_map.308 = (bf16[1024,512]{1,0:T(8,128)(2,1)}, bf16[1024,512]{1,0:T(8,128)(2,1)}, bf16[1024,512]{1,0:T(8,128)(2,1)}, bf16[1024,512]{1,0:T(8,128)(2,1)}, f3...) custom-call(bf16[256,2048]{1,0:T(8,128)(2,1)} %get-tuple-element.216, ...), custom_call_target="tpu_custom_call", output_to_operand_aliasing={{0}: (8, {}), {1}: (9, {}), {2}: (10, {}), {3}: (11, {}), {... | custom-call | tf_op jit(solution)/shard_map/pallas_call | solution.py:527
  54.4 7.3 shard_map.310
  66.3 24.5 %shard_map.311 = (bf16[1024,512]{1,0:T(8,128)(2,1)}, bf16[1024,512]{1,0:T(8,128)(2,1)}, bf16[1024,512]{1,0:T(8,128)(2,1)}, bf16[1024,512]{1,0:T(8,128)(2,1)}, bf...) custom-call(s32[3]{0:T(128)} %pad_add_fusion.refs_10_.starts_ref, ...), custom_call_target="tpu_custom_call" | custom-call | tf_op jit(solution)/shard_map/pallas_call | solution.py:233
  92.3 19.6 %collective-permute-done.4.refs_0_ = bf16[1024,512]{1,0:T(8,128)(2,1)S(1)} collective-permute-done((bf16[1024,512]{1,0:T(8,128)(2,1)}, bf16[1024,512]{1,0:T(8,128)(2,1)S(1)}, u32[]{:S(2)}, u32[]{:S(2)}) %collective-permute-start.4) | collective-permute-done | bytes 1048608 | tf_op jit(solution)/shard_map/ppermute | solution.py:1123
  119.1 5.8 collective-permute-done.6
  134.6 17.8 %shard_map.316 = (bf16[1024,2048]{1,0:T(8,128)(2,1)}, f32[256,2048]{1,0:T(8,128)}) custom-call(bf16[256,2048]{1,0:T(8,128)(2,1)} %bitcast.40, bf16[256,2048]{1,0:T(8,128)(2,1)} %get-tuple-element.216.across_ref.refs_0_.refs_1_, bf16[256,2048]{1,0:T(8,128)(2,1)} %get-tuple-element.217.down_ref.refs_1_.refs_2_, ...), custom_call_target="tpu_custom_call" | custom-call | tf_op jit(solution)/shard_map/pallas_call | solution.py:576
  152.4 19.6 %shard_map.317 = (bf16[1024,1408]{1,0:T(8,128)(2,1)}, bf16[1024,1408]{1,0:T(8,128)(2,1)}, bf16[1024,1408]{1,0:T(8,128)(2,1)}) custom-call(bf16[1024,2048]{1,0:T(8,128)(2,1)} %get-tuple-element.248.x_ref.refs_0_, bf16[2048,1408]{1,0:T(8,128)(2,1)} %refs_6_.5, bf16[2048,1408]{1,0:T(8,128)(2,1)} %refs_7_.1), custom_call_target="tpu_custom_call" | custom-call | tf_op jit(solution)/shard_map/pallas_call | solution.py:631
  177.5 8.1 %shard_map.320.refs_5_ = bf16[1024,1408]{1,0:T(8,128)(2,1)} custom-call(s32[4]{0:T(128)} %pad_add_fusion.1.refs_11_.info_ref, bf16[256,2048]{1,0:T(8,128)(2,1)} %shard_map.318.refs_0_, bf16[256,2048]{1,0:T(8,128)(2,1)} %copy-done.11, bf16[256,2048]{1,0:T(8,128)(2,1)} %copy-done.12, bf16[256,2048]{1,0:T(8,128)(2,1)} %shard_map.319.refs_3_, ...), custom_call_target="tpu_custom_call" | custom-call | tf_op jit(solution)/shard_map/pallas_call | solution.py:670
  186.6 8.4 %shard_map.321.refs_0_ = bf16[1024,1408]{1,0:T(8,128)(2,1)} custom-call(s32[4]{0:T(128)} %pad_add_fusion.1.refs_11_.info_ref, bf16[256,2048]{1,0:T(8,128)(2,1)} %shard_map.318.refs_0_, bf16[256,2048]{1,0:T(8,128)(2,1)} %copy-done.11, bf16[256,2048]{1,0:T(8,128)(2,1)} %copy-done.12, bf16[256,2048]{1,0:T(8,128)(2,1)} %shard_map.319.refs_3_, ...), custom_call_target="tpu_custom_call" | custom-call | tf_op jit(solution)/shard_map/pallas_call | solution.py:670
  208.2 30.8 %shard_map.324 = (bf16[1024,1408]{1,0:T(8,128)(2,1)}, bf16[1024,1408]{1,0:T(8,128)(2,1)}, bf16[1024,2048]{1,0:T(8,128)(2,1)}) custom-call(s32[1]{0:T(128)} %bitcast.5.rank_ref, bf16[256,2048]{1,0:T(8,128)(2,1)} %shard_map.318.refs_0_, bf16[256,2048]{1,0:T(8,128)(2,1)} %copy-done.11, bf16[256,2048]{1,0:T(8,128)(2,1)} %copy-done.12, ...), custom_call_target="tpu_custom_call" | custom-call | tf_op jit(solution)/shard_map/pallas_call | solution.py:716
  265.8 12.4 %shard_map.333.refs_2_.refs_7_.refs_0_ = bf16[1024,1408]{1,0:T(8,128)(2,1)} custom-call(s32[4]{0:T(128)} %pad_add_fusion.1.refs_11_.info_ref, bf16[1024,2048]{1,0:T(8,128)(2,1)} %get-tuple-element.248.x_ref.refs_0_, bf16[1024,1408]{1,0:T(8,128)(2,1)} %get-tuple-element.253.refs_1_, bf16[1024,2048]{1,0:T(8,128)(2,1)} %shard_map.325.refs_2_, ...), custom_call_target="tpu_custom_call" | custom-call | tf_op jit(solution)/shard_map/pallas_call | solution.py:670
  278.2 10.7 %collective-permute-done.24.refs_5_ = bf16[256,1408]{1,0:T(8,128)(2,1)} collective-permute-done((bf16[256,1408]{1,0:T(8,128)(2,1)}, bf16[256,1408]{1,0:T(8,128)(2,1)}, u32[]{:S(2)}, u32[]{:S(2)}) %collective-permute-start.24) | collective-permute-done | bytes 720928 | tf_op jit(solution)/shard_map/ppermute | solution.py:988
  314.7 12.0 %shard_map.338.refs_0_.refs_1_ = bf16[1024,1408]{1,0:T(8,128)(2,1)} custom-call(s32[4]{0:T(128)} %pad_add_fusion.1.refs_11_.info_ref, bf16[1024,2048]{1,0:T(8,128)(2,1)} %get-tuple-element.248.x_ref.refs_0_, bf16[1024,1408]{1,0:T(8,128)(2,1)} %get-tuple-element.252.refs_1_, bf16[1024,2048]{1,0:T(8,128)(2,1)} %shard_map.325.refs_2_, ...), custom_call_target="tpu_custom_call" | custom-call | tf_op jit(solution)/shard_map/pallas_call | solution.py:670
  326.6 11.1 %shard_map.339.refs_5_ = bf16[1024,2048]{1,0:T(8,128)(2,1)} custom-call(s32[1]{0:T(128)} %bitcast.5.rank_ref, bf16[1024,1408]{1,0:T(8,128)(2,1)} %get-tuple-element.249.refs_1_.refs_4_.hidden_ref, bf16[1408,2048]{1,0:T(8,128)(2,1)} %weight_ref.2, bf16[1024,1408]{1,0:T(8,128)(2,1)} %shard_map.338.refs_0_.refs_1_), custom_call_target="tpu_custom_call" | custom-call | tf_op jit(solution)/shard_map/pallas_call | solution.py:768
  343.3 6.0 collective-permute-start.32
  392.1 6.6 shard_map.346.gg_ref
  398.7 33.9 %shard_map.347 = (bf16[1024,2048]{1,0:T(8,128)(2,1)}, bf16[1024,128]{1,0:T(8,128)(2,1)}, f32[12,512]{1,0:T(8,128)}, f32[8,128]{1,0:T(8,128)}) custom-call(s32[3]{0:T(128)} %pad_add_fusion.refs_10_.starts_ref, bf16[1024,512]{1,0:T(8,128)(2,1)} %shard_map.346.gg_ref, bf16[1024,512]{1,0:T(8,128)(2,1)} %get-tuple-element.281.mixed_ref, ...), custom_call_target="tpu_custom_call" | custom-call | tf_op jit(solution)/shard_map/pallas_call | solution.py:465
  453.0 11.8 %shard_map.352 = (bf16[1024,1408]{1,0:T(8,128)(2,1)}, bf16[1024,1408]{1,0:T(8,128)(2,1)}) custom-call(s32[4]{0:T(128)} %pad_add_fusion.1.refs_11_.info_ref, bf16[1024,2048]{1,0:T(8,128)(2,1)} %all-gather.4.cloned.1.call-done.rows_ref.refs_0_.refs_1_.refs_2_.refs_3_, bf16[1024,2048]{1,0:T(8,128)(2,1)} %all-gather.4.cloned.1.call-done.rows_ref.refs_0_.refs_1_.refs_2_.refs_3_, ...), custom_call_target="tpu_custom_call" | custom-call | tf_op jit(solution)/shard_map/pallas_call | solution.py:916
  464.8 11.6 %shard_map.353 = (bf16[1024,1408]{1,0:T(8,128)(2,1)}, bf16[1024,1408]{1,0:T(8,128)(2,1)}) custom-call(s32[4]{0:T(128)} %pad_add_fusion.1.refs_11_.info_ref, bf16[1024,2048]{1,0:T(8,128)(2,1)} %all-gather.4.cloned.1.call-done.rows_ref.refs_0_.refs_1_.refs_2_.refs_3_, bf16[1024,2048]{1,0:T(8,128)(2,1)} %all-gather.4.cloned.1.call-done.rows_ref.refs_0_.refs_1_.refs_2_.refs_3_, ...), custom_call_target="tpu_custom_call" | custom-call | tf_op jit(solution)/shard_map/pallas_call | solution.py:916
  481.8 6.1 collective-permute-done.44.other_ref
  515.4 15.5 %shard_map.363.refs_2_.refs_0_ = bf16[1024,2048]{1,0:T(8,128)(2,1)} custom-call(s32[1]{0:T(128)} %bitcast.5.rank_ref, bf16[1024,2048]{1,0:T(8,128)(2,1)} %get-tuple-element.291.refs_2_.refs_6_.grad_ref, bf16[1024,128]{1,0:T(8,128)(2,1)} %get-tuple-element.292.refs_7_.scalar_ref, bf16[2048,512]{1,0:T(8,128)(2,1)} %refs_0_.1, bf16[2048,512]{1,0:T(8,128)(2,1)} %refs_1_.1, ...), custom_call_target="tpu_custom_call" | custom-call | tf_op jit(solution)/shard_map/pallas_call | solution.py:744
  657.5 6.3 collective-permute-done.68.refs_0_
  714.7 7.1 collective-permute-done.80.refs_5_
  (469 shorter events, 435.6 us)
Async XLA Ops:
  7.2 127.4 %all-gather.6.cloned.1.call-start = ((), (), s32[]{:S(2)}) async-start(), calls=%async_computation.7 | async-start | bytes 7077888 | tf_op jit(solution)/shard_map/all_gather | solution.py:1149
  66.1 231.2 %reduce-scatter.4.cloned.1.call-start = ((), (), s32[]{:S(2)}) async-start(), calls=%async_computation.3 | async-start | bytes 5242880 | tf_op jit(solution)/shard_map/reduce_scatter | solution.py:1285
  126.4 45.6 %collective-permute-start.13 = (bf16[256,2048]{1,0:T(8,128)(2,1)}, bf16[256,2048]{1,0:T(8,128)(2,1)S(1)}, u32[]{:S(2)}, u32[]{:S(2)}) collective-permute-start(bf16[256,2048]{1,0:T(8,128)(2,1)} %shard_map.318.refs_0_), channel_id=1, source_target_pairs={{0,24},{8,16},{16,8},{24,0},{1,25},{9,17},{17,9},{25,1},{2,26},{10... | collective-permute-start | bytes 3145736 | tf_op jit(solution)/shard_map/ppermute | solution.py:1123
  129.3 43.6 %collective-permute-start.11 = (bf16[256,2048]{1,0:T(8,128)(2,1)}, bf16[256,2048]{1,0:T(8,128)(2,1)S(1)}, u32[]{:S(2)}, u32[]{:S(2)}) collective-permute-start(bf16[256,2048]{1,0:T(8,128)(2,1)} %shard_map.318.refs_0_), channel_id=1, source_target_pairs={{0,8},{8,0},{16,24},{24,16},{1,9},{9,1},{17,25},{25,17},{2,10},{10... | collective-permute-start | bytes 3145736 | tf_op jit(solution)/shard_map/ppermute | solution.py:1123
  129.7 46.9 %collective-permute-start.12 = (bf16[256,2048]{1,0:T(8,128)(2,1)}, bf16[256,2048]{1,0:T(8,128)(2,1)S(1)}, u32[]{:S(2)}, u32[]{:S(2)}) collective-permute-start(bf16[256,2048]{1,0:T(8,128)(2,1)} %shard_map.318.refs_0_), channel_id=1, source_target_pairs={{0,16},{8,24},{16,0},{24,8},{1,17},{9,25},{17,1},{25,9},{2,18},{10... | collective-permute-start | bytes 3145736 | tf_op jit(solution)/shard_map/ppermute | solution.py:1123
  199.4 39.6 %collective-permute-start.19 = (bf16[256,1408]{1,0:T(8,128)(2,1)}, bf16[256,1408]{1,0:T(8,128)(2,1)S(1)}, u32[]{:S(2)}, u32[]{:S(2)}) collective-permute-start(bf16[256,1408]{1,0:T(8,128)(2,1)} %shard_map.322.refs_2_.refs_3_), channel_id=1, source_target_pairs={{0,2},{1,3},{8,10},{9,11},{16,18},{17,19},{24,26},{25,27}} | collective-permute-start | bytes 2162696 | tf_op jit(solution)/shard_map/ppermute | solution.py:988
  202.6 36.4 %collective-permute-start.20 = (bf16[256,1408]{1,0:T(8,128)(2,1)}, bf16[256,1408]{1,0:T(8,128)(2,1)S(1)}, u32[]{:S(2)}, u32[]{:S(2)}) collective-permute-start(bf16[256,1408]{1,0:T(8,128)(2,1)} %shard_map.322.refs_2_.refs_3_), channel_id=1, source_target_pairs={{6,4},{7,5},{14,12},{15,13},{22,20},{23,21},{30,28},{31,29}} | collective-permute-start | bytes 2162696 | tf_op jit(solution)/shard_map/ppermute | solution.py:988
  206.1 34.0 %collective-permute-start.17 = (bf16[256,1408]{1,0:T(8,128)(2,1)}, bf16[256,1408]{1,0:T(8,128)(2,1)S(1)}, u32[]{:S(2)}, u32[]{:S(2)}) collective-permute-start(bf16[256,1408]{1,0:T(8,128)(2,1)} %shard_map.323.refs_9_.refs_2_.refs_3_), channel_id=1, source_target_pairs={{0,2},{1,3},{8,10},{9,11},{16,18},{17,19},{24,26},{25,27}} | collective-permute-start | bytes 2162696 | tf_op jit(solution)/shard_map/ppermute | solution.py:988
  241.2 150.9 %all-gather.4.cloned.1.call-start = ((), (), s32[]{:S(2)}) async-start(), calls=%async_computation.5 | async-start | bytes 5242880 | tf_op jit(solution)/shard_map/all_gather | solution.py:1294
  256.2 36.8 %collective-permute-start.22 = (bf16[256,1408]{1,0:T(8,128)(2,1)}, bf16[256,1408]{1,0:T(8,128)(2,1)}, u32[]{:S(2)}, u32[]{:S(2)}) collective-permute-start(bf16[256,1408]{1,0:T(8,128)(2,1)} %get-tuple-element.261.refs_3_), channel_id=1, source_target_pairs={{0,2},{1,3},{2,4},{3,5},{8,10},{9,11},{10,12},{11,13},{16,18},{17,... | collective-permute-start | bytes 2162696 | tf_op jit(solution)/shard_map/ppermute | solution.py:988
  302.6 212.8 %reduce-scatter.6.cloned.1.call-start = ((), (), s32[]{:S(2)}) async-start(), calls=%async_computation.4 | async-start | bytes 5242880 | tf_op jit(solution)/shard_map/reduce_scatter | solution.py:1297
  302.7 35.0 %collective-permute-start.28 = (bf16[256,1408]{1,0:T(8,128)(2,1)}, bf16[256,1408]{1,0:T(8,128)(2,1)}, u32[]{:S(2)}, u32[]{:S(2)}) collective-permute-start(bf16[256,1408]{1,0:T(8,128)(2,1)} %get-tuple-element.270.refs_1_), channel_id=1, source_target_pairs={{0,2},{1,3},{2,4},{3,5},{4,6},{5,7},{8,10},{9,11},{10,12},{11,13},... | collective-permute-start | bytes 2162696 | tf_op jit(solution)/shard_map/ppermute | solution.py:988
  309.3 41.3 %collective-permute-start.26 = (bf16[256,1408]{1,0:T(8,128)(2,1)S(1)}, bf16[256,1408]{1,0:T(8,128)(2,1)S(1)}, u32[]{:S(2)}, u32[]{:S(2)}) collective-permute-start(bf16[256,1408]{1,0:T(8,128)(2,1)S(1)} %copy-done.50), channel_id=1, source_target_pairs={{0,2},{1,3},{2,4},{3,5},{4,6},{5,7},{8,10},{9,11},{10,12},{11,13},... | collective-permute-start | bytes 2162696 | tf_op jit(solution)/shard_map/ppermute | solution.py:988
  313.4 37.3 %collective-permute-start.27 = (bf16[256,1408]{1,0:T(8,128)(2,1)S(1)}, bf16[256,1408]{1,0:T(8,128)(2,1)S(1)}, u32[]{:S(2)}, u32[]{:S(2)}) collective-permute-start(bf16[256,1408]{1,0:T(8,128)(2,1)S(1)} %copy-done.51), channel_id=1, source_target_pairs={{6,4},{7,5},{4,2},{5,3},{2,0},{3,1},{14,12},{15,13},{12,10},{13,11... | collective-permute-start | bytes 2162696 | tf_op jit(solution)/shard_map/ppermute | solution.py:988
  361.5 227.8 %reduce-scatter.8.cloned.1.call-start = ((), (), s32[]{:S(2)}) async-start(), calls=%async_computation.6 | async-start | bytes 5242880 | tf_op jit(solution)/shard_map/reduce_scatter | solution.py:1320
  372.9 59.7 %collective-permute-start.37 = (bf16[256,1408]{1,0:T(8,128)(2,1)}, bf16[256,1408]{1,0:T(8,128)(2,1)S(1)}, u32[]{:S(2)}, u32[]{:S(2)}) collective-permute-start(bf16[256,1408]{1,0:T(8,128)(2,1)} %get-tuple-element.295.refs_1_), channel_id=1, source_target_pairs={{0,2},{1,3},{2,4},{3,5},{4,6},{5,7},{8,10},{9,11},{10,12},{11,13},... | collective-permute-start | bytes 2162696 | tf_op jit(solution)/shard_map/ppermute | solution.py:988
  374.7 57.9 %collective-permute-start.38 = (bf16[256,1408]{1,0:T(8,128)(2,1)}, bf16[256,1408]{1,0:T(8,128)(2,1)S(1)}, u32[]{:S(2)}, u32[]{:S(2)}) collective-permute-start(bf16[256,1408]{1,0:T(8,128)(2,1)} %get-tuple-element.296.refs_2_), channel_id=1, source_target_pairs={{6,4},{7,5},{4,2},{5,3},{2,0},{3,1},{14,12},{15,13},{12,10},{13,11... | collective-permute-start | bytes 2162696 | tf_op jit(solution)/shard_map/ppermute | solution.py:988
  389.3 44.5 %collective-permute-start.35 = (bf16[256,1408]{1,0:T(8,128)(2,1)}, bf16[256,1408]{1,0:T(8,128)(2,1)S(1)}, u32[]{:S(2)}, u32[]{:S(2)}) collective-permute-start(bf16[256,1408]{1,0:T(8,128)(2,1)} %get-tuple-element.293.refs_1_), channel_id=1, source_target_pairs={{0,2},{1,3},{2,4},{3,5},{4,6},{5,7},{8,10},{9,11},{10,12},{11,13},... | collective-permute-start | bytes 2162696 | tf_op jit(solution)/shard_map/ppermute | solution.py:988
  390.8 43.0 %collective-permute-start.36 = (bf16[256,1408]{1,0:T(8,128)(2,1)}, bf16[256,1408]{1,0:T(8,128)(2,1)S(1)}, u32[]{:S(2)}, u32[]{:S(2)}) collective-permute-start(bf16[256,1408]{1,0:T(8,128)(2,1)} %get-tuple-element.294.refs_2_), channel_id=1, source_target_pairs={{6,4},{7,5},{4,2},{5,3},{2,0},{3,1},{14,12},{15,13},{12,10},{13,11... | collective-permute-start | bytes 2162696 | tf_op jit(solution)/shard_map/ppermute | solution.py:988
  438.5 37.9 %collective-permute-start.41 = (bf16[256,1408]{1,0:T(8,128)(2,1)}, bf16[256,1408]{1,0:T(8,128)(2,1)S(1)}, u32[]{:S(2)}, u32[]{:S(2)}) collective-permute-start(bf16[256,1408]{1,0:T(8,128)(2,1)} %get-tuple-element.308.refs_3_), channel_id=1, source_target_pairs={{0,2},{1,3},{2,4},{3,5},{4,6},{5,7},{8,10},{9,11},{10,12},{11,13},... | collective-permute-start | bytes 2162696 | tf_op jit(solution)/shard_map/ppermute | solution.py:988
  442.5 33.9 %collective-permute-start.42 = (bf16[256,1408]{1,0:T(8,128)(2,1)}, bf16[256,1408]{1,0:T(8,128)(2,1)S(1)}, u32[]{:S(2)}, u32[]{:S(2)}) collective-permute-start(bf16[256,1408]{1,0:T(8,128)(2,1)} %get-tuple-element.309.refs_4_), channel_id=1, source_target_pairs={{6,4},{7,5},{4,2},{5,3},{2,0},{3,1},{14,12},{15,13},{12,10},{13,11... | collective-permute-start | bytes 2162696 | tf_op jit(solution)/shard_map/ppermute | solution.py:988
  497.8 33.1 %collective-permute-start.48 = (bf16[256,1408]{1,0:T(8,128)(2,1)}, bf16[256,1408]{1,0:T(8,128)(2,1)}, u32[]{:S(2)}, u32[]{:S(2)}) collective-permute-start(bf16[256,1408]{1,0:T(8,128)(2,1)} %get-tuple-element.321.refs_2_), channel_id=1, source_target_pairs={{0,2},{1,3},{2,4},{3,5},{4,6},{5,7},{8,10},{9,11},{10,12},{11,13},... | collective-permute-start | bytes 2162696 | tf_op jit(solution)/shard_map/ppermute | solution.py:988
  560.3 34.3 %collective-permute-start.63 = (bf16[256,1408]{1,0:T(8,128)(2,1)S(1)}, bf16[256,1408]{1,0:T(8,128)(2,1)}, u32[]{:S(2)}, u32[]{:S(2)}) collective-permute-start(bf16[256,1408]{1,0:T(8,128)(2,1)S(1)} %copy-done.40), channel_id=1, source_target_pairs={{0,1},{1,0},{2,3},{3,2},{4,5},{5,4},{6,7},{7,6},{8,9},{9,8},{10,11... | collective-permute-start | bytes 2162696 | tf_op jit(solution)/shard_map/ppermute | solution.py:1123
  594.6 33.1 %collective-permute-start.67 = (bf16[256,1408]{1,0:T(8,128)(2,1)S(1)}, bf16[256,1408]{1,0:T(8,128)(2,1)S(1)}, u32[]{:S(2)}, u32[]{:S(2)}) collective-permute-start(bf16[256,1408]{1,0:T(8,128)(2,1)S(1)} %copy-done.35), channel_id=1, source_target_pairs={{0,1},{1,0},{2,3},{3,2},{4,5},{5,4},{6,7},{7,6},{8,9},{9,8},{10,11... | collective-permute-start | bytes 2162696 | tf_op jit(solution)/shard_map/ppermute | solution.py:1123
  (152 other events, 1864.0 us)
Sparse Core Ops, SparseCore 0:
  66.2 68.3 all-gather.5
  241.3 51.4 reduce-scatter.3
  302.7 52.6 all-gather.3
  361.6 51.9 reduce-scatter.5
  538.6 50.5 reduce-scatter.7

commit v4 on v3

--- a/solution.py
+++ b/solution.py
@@ -1286,7 +1286,7 @@
         gate_other = across(gate_grad)
         step = ticks(step)
         gate_other = after(gate_other, step)
-        up_other = across(after(up_grad, gate_other))
+        up_other = across(up_grad)
         sources["gate"] = (outer_half(info, True, [([normed_mid], gate_grad), ([mid_other], gate_other)], up_other),)
         step = ticks(sources["gate"][0])
         mid_normed_grad = after(mid_normed_grad, step)

time: 774 us -> 773 us (level)
  starting transfers between devices: 152 us -> 161 us
    reduce_scatter x1, waiting for transfers between devices: 0.02 us -> 10.3 us  [body(): lax.psum_scatter(after(mid_partial, step), 'tp', scatter_dimension=0, til...]
    ppermute x24, waiting for transfers between devices: 16.5 us -> 8.01 us  [send(): lax.ppermute(right, 'dp', hops(rightward))]
    ppermute x24, starting transfers between devices: 80.8 us -> 89.2 us  [send(): lax.ppermute(right, 'dp', hops(rightward))]
    unnamed x160 -> x157, local copies, waits for them, and re-layouts: 35.4 us -> 28.4 us
where the time goes in v4:
time: 773 us; the launch traced here: 767 us
  Pallas kernels  436 us (56%)
  starting transfers between devices  161 us (21%)
  waiting for transfers between devices  103 us (13%)
  local copies, waits for them, and re-layouts  41.3 us (5%)
  between operations  16.8 us (2%)
  other arithmetic  9.33 us (1%)
    pallas_call x24, Pallas kernels, advance(): pl.pallas_call(partial(line_step_kernel, len(now), len(later)), grid_spec...  97.2 us
    ppermute x24, starting transfers between devices, send(): lax.ppermute(right, 'dp', hops(rightward))  89.2 us
    ppermute x45, waiting for transfers between devices, swap(): return lax.ppermute(values, axis, xor_pairs(lax.axis_size(axis), mask))  54.9 us
    pallas_call x12, Pallas kernels, place(): pl.pallas_call(partial(place_kernel, turned), grid_spec=pltpu.PrefetchSca...  45.1 us
    pallas_call x4, Pallas kernels, outer_half(): pl.pallas_call(partial(outer_kernel, [len(lefts) for lefts, _ in sides]),...  41.2 us
    ppermute x45, starting transfers between devices, swap(): return lax.ppermute(values, axis, xor_pairs(lax.axis_size(axis), mask))  40.7 us
    pallas_call x1, Pallas kernels, mixer_backward(): pl.pallas_call(partial(backward_kernel, tiles, heads), grid_spec=pltpu.Pr...  34.6 us
    ppermute x24, starting transfers between devices, send(): lax.ppermute(left, 'dp', hops(leftward))  31 us
  transfers between devices with their start and end apart: 98, of which 21 were waited for; matrix products, arithmetic and copies ran while one was open for 3% of the time, Pallas kernels for 54%

profile of v4, /device:TPU:1, one launch (start us, length us, event | category | flops | bytes accessed | tf_op | source)
XLA Modules:
  0.0 767.4 jit_solution(2758079768647592766)
XLA Ops:
  19.6 7.3 shard_map.305
  40.0 10.8 %shard_map.308 = (bf16[1024,512]{1,0:T(8,128)(2,1)}, bf16[1024,512]{1,0:T(8,128)(2,1)}, bf16[1024,512]{1,0:T(8,128)(2,1)}, bf16[1024,512]{1,0:T(8,128)(2,1)}, f3...) custom-call(bf16[256,2048]{1,0:T(8,128)(2,1)} %get-tuple-element.216, ...), custom_call_target="tpu_custom_call", output_to_operand_aliasing={{0}: (8, {}), {1}: (9, {}), {2}: (10, {}), {3}: (11, {}), {... | custom-call | tf_op jit(solution)/shard_map/pallas_call | solution.py:527
  54.5 7.3 shard_map.310
  66.3 24.5 %shard_map.311 = (bf16[1024,512]{1,0:T(8,128)(2,1)}, bf16[1024,512]{1,0:T(8,128)(2,1)}, bf16[1024,512]{1,0:T(8,128)(2,1)}, bf16[1024,512]{1,0:T(8,128)(2,1)}, bf...) custom-call(s32[3]{0:T(128)} %pad_add_fusion.refs_10_.starts_ref, ...), custom_call_target="tpu_custom_call" | custom-call | tf_op jit(solution)/shard_map/pallas_call | solution.py:233
  92.3 19.5 %collective-permute-done.4.refs_0_ = bf16[1024,512]{1,0:T(8,128)(2,1)S(1)} collective-permute-done((bf16[1024,512]{1,0:T(8,128)(2,1)}, bf16[1024,512]{1,0:T(8,128)(2,1)S(1)}, u32[]{:S(2)}, u32[]{:S(2)}) %collective-permute-start.4) | collective-permute-done | bytes 1048608 | tf_op jit(solution)/shard_map/ppermute | solution.py:1123
  119.1 5.8 collective-permute-done.6
  134.6 17.8 %shard_map.316 = (bf16[1024,2048]{1,0:T(8,128)(2,1)}, f32[256,2048]{1,0:T(8,128)}) custom-call(bf16[256,2048]{1,0:T(8,128)(2,1)} %bitcast.40, bf16[256,2048]{1,0:T(8,128)(2,1)} %get-tuple-element.216.across_ref.refs_0_.refs_1_, bf16[256,2048]{1,0:T(8,128)(2,1)} %get-tuple-element.217.down_ref.refs_1_.refs_2_, ...), custom_call_target="tpu_custom_call" | custom-call | tf_op jit(solution)/shard_map/pallas_call | solution.py:576
  152.4 19.6 %shard_map.317 = (bf16[1024,1408]{1,0:T(8,128)(2,1)}, bf16[1024,1408]{1,0:T(8,128)(2,1)}, bf16[1024,1408]{1,0:T(8,128)(2,1)}) custom-call(bf16[1024,2048]{1,0:T(8,128)(2,1)} %get-tuple-element.248.x_ref.refs_0_, bf16[2048,1408]{1,0:T(8,128)(2,1)} %refs_6_.5, bf16[2048,1408]{1,0:T(8,128)(2,1)} %refs_7_.1), custom_call_target="tpu_custom_call" | custom-call | tf_op jit(solution)/shard_map/pallas_call | solution.py:631
  177.6 8.2 %shard_map.320.refs_5_ = bf16[1024,1408]{1,0:T(8,128)(2,1)} custom-call(s32[4]{0:T(128)} %pad_add_fusion.1.refs_11_.info_ref, bf16[256,2048]{1,0:T(8,128)(2,1)} %shard_map.318.refs_0_, bf16[256,2048]{1,0:T(8,128)(2,1)} %copy-done.10, bf16[256,2048]{1,0:T(8,128)(2,1)} %copy-done.11, bf16[256,2048]{1,0:T(8,128)(2,1)} %shard_map.319.refs_3_, ...), custom_call_target="tpu_custom_call" | custom-call | tf_op jit(solution)/shard_map/pallas_call | solution.py:670
  186.6 8.4 %shard_map.321.refs_0_ = bf16[1024,1408]{1,0:T(8,128)(2,1)} custom-call(s32[4]{0:T(128)} %pad_add_fusion.1.refs_11_.info_ref, bf16[256,2048]{1,0:T(8,128)(2,1)} %shard_map.318.refs_0_, bf16[256,2048]{1,0:T(8,128)(2,1)} %copy-done.10, bf16[256,2048]{1,0:T(8,128)(2,1)} %copy-done.11, bf16[256,2048]{1,0:T(8,128)(2,1)} %shard_map.319.refs_3_, ...), custom_call_target="tpu_custom_call" | custom-call | tf_op jit(solution)/shard_map/pallas_call | solution.py:670
  208.2 30.8 %shard_map.324 = (bf16[1024,1408]{1,0:T(8,128)(2,1)}, bf16[1024,1408]{1,0:T(8,128)(2,1)}, bf16[1024,2048]{1,0:T(8,128)(2,1)}) custom-call(s32[1]{0:T(128)} %bitcast.5.rank_ref, bf16[256,2048]{1,0:T(8,128)(2,1)} %shard_map.318.refs_0_, bf16[256,2048]{1,0:T(8,128)(2,1)} %copy-done.10, bf16[256,2048]{1,0:T(8,128)(2,1)} %copy-done.11, ...), custom_call_target="tpu_custom_call" | custom-call | tf_op jit(solution)/shard_map/pallas_call | solution.py:716
  252.9 11.4 %collective-permute-start.24 = (bf16[256,1408]{1,0:T(8,128)(2,1)}, bf16[256,1408]{1,0:T(8,128)(2,1)}, u32[]{:S(2)}, u32[]{:S(2)}) collective-permute-start(bf16[256,1408]{1,0:T(8,128)(2,1)} %get-tuple-element.263.refs_3_), channel_id=1, source_target_pairs={{0,2},{1,3},{2,4},{3,5},{8,10},{9,11},{10,12},{11,13},{16,18},{17,... | collective-permute-start | bytes 2162696 | tf_op jit(solution)/shard_map/ppermute | solution.py:988
  267.5 12.6 %shard_map.332.refs_2_.refs_7_.refs_0_ = bf16[1024,1408]{1,0:T(8,128)(2,1)} custom-call(s32[4]{0:T(128)} %pad_add_fusion.1.refs_11_.info_ref, bf16[1024,2048]{1,0:T(8,128)(2,1)} %get-tuple-element.248.x_ref.refs_0_, bf16[1024,1408]{1,0:T(8,128)(2,1)} %get-tuple-element.256.refs_1_, bf16[1024,2048]{1,0:T(8,128)(2,1)} %shard_map.325.refs_2_, ...), custom_call_target="tpu_custom_call" | custom-call | tf_op jit(solution)/shard_map/pallas_call | solution.py:670
  291.3 10.3 %reduce-scatter.4.cloned.1.call-done.refs_0_ = bf16[256,2048]{1,0:T(8,128)(2,1)} async-done(((bf16[1024,2048]{1,0:T(8,128)(2,1)}), bf16[256,2048]{1,0:T(8,128)(2,1)}) %reduce-scatter.4.cloned.1.call-update) | async-done | bytes 1048592 | tf_op jit(solution)/shard_map/reduce_scatter | solution.py:1285
  317.6 12.0 %shard_map.337.refs_0_.refs_1_ = bf16[1024,1408]{1,0:T(8,128)(2,1)} custom-call(s32[4]{0:T(128)} %pad_add_fusion.1.refs_11_.info_ref, bf16[1024,2048]{1,0:T(8,128)(2,1)} %get-tuple-element.248.x_ref.refs_0_, bf16[1024,1408]{1,0:T(8,128)(2,1)} %get-tuple-element.252.refs_1_, bf16[1024,2048]{1,0:T(8,128)(2,1)} %shard_map.325.refs_2_, ...), custom_call_target="tpu_custom_call" | custom-call | tf_op jit(solution)/shard_map/pallas_call | solution.py:670
  329.6 11.1 %shard_map.338.refs_5_ = bf16[1024,2048]{1,0:T(8,128)(2,1)} custom-call(s32[1]{0:T(128)} %bitcast.5.rank_ref, bf16[1024,1408]{1,0:T(8,128)(2,1)} %get-tuple-element.249.refs_1_.refs_4_.hidden_ref, bf16[1408,2048]{1,0:T(8,128)(2,1)} %weight_ref.2, bf16[1024,1408]{1,0:T(8,128)(2,1)} %shard_map.337.refs_0_.refs_1_), custom_call_target="tpu_custom_call" | custom-call | tf_op jit(solution)/shard_map/pallas_call | solution.py:768
  394.6 6.5 shard_map.345.gg_ref
  401.0 34.6 %shard_map.346 = (bf16[1024,2048]{1,0:T(8,128)(2,1)}, bf16[1024,128]{1,0:T(8,128)(2,1)}, f32[12,512]{1,0:T(8,128)}, f32[8,128]{1,0:T(8,128)}) custom-call(s32[3]{0:T(128)} %pad_add_fusion.refs_10_.starts_ref, bf16[1024,512]{1,0:T(8,128)(2,1)} %shard_map.345.gg_ref, bf16[1024,512]{1,0:T(8,128)(2,1)} %get-tuple-element.281.mixed_ref, ...), custom_call_target="tpu_custom_call" | custom-call | tf_op jit(solution)/shard_map/pallas_call | solution.py:465
  455.7 11.8 %shard_map.351 = (bf16[1024,1408]{1,0:T(8,128)(2,1)}, bf16[1024,1408]{1,0:T(8,128)(2,1)}) custom-call(s32[4]{0:T(128)} %pad_add_fusion.1.refs_11_.info_ref, bf16[1024,2048]{1,0:T(8,128)(2,1)} %all-gather.4.cloned.1.call-done.rows_ref.refs_0_.refs_1_.refs_2_.refs_3_, bf16[1024,2048]{1,0:T(8,128)(2,1)} %all-gather.4.cloned.1.call-done.rows_ref.refs_0_.refs_1_.refs_2_.refs_3_, ...), custom_call_target="tpu_custom_call" | custom-call | tf_op jit(solution)/shard_map/pallas_call | solution.py:916
  467.6 11.6 %shard_map.352 = (bf16[1024,1408]{1,0:T(8,128)(2,1)}, bf16[1024,1408]{1,0:T(8,128)(2,1)}) custom-call(s32[4]{0:T(128)} %pad_add_fusion.1.refs_11_.info_ref, bf16[1024,2048]{1,0:T(8,128)(2,1)} %all-gather.4.cloned.1.call-done.rows_ref.refs_0_.refs_1_.refs_2_.refs_3_, bf16[1024,2048]{1,0:T(8,128)(2,1)} %all-gather.4.cloned.1.call-done.rows_ref.refs_0_.refs_1_.refs_2_.refs_3_, ...), custom_call_target="tpu_custom_call" | custom-call | tf_op jit(solution)/shard_map/pallas_call | solution.py:916
  484.0 6.1 collective-permute-done.44.other_ref
  517.7 15.5 %shard_map.362.refs_2_.refs_0_ = bf16[1024,2048]{1,0:T(8,128)(2,1)} custom-call(s32[1]{0:T(128)} %bitcast.5.rank_ref, bf16[1024,2048]{1,0:T(8,128)(2,1)} %get-tuple-element.291.refs_2_.refs_6_.grad_ref, bf16[1024,128]{1,0:T(8,128)(2,1)} %get-tuple-element.292.refs_7_.scalar_ref, bf16[2048,512]{1,0:T(8,128)(2,1)} %refs_0_.1, bf16[2048,512]{1,0:T(8,128)(2,1)} %refs_1_.1, ...), custom_call_target="tpu_custom_call" | custom-call | tf_op jit(solution)/shard_map/pallas_call | solution.py:744
  661.6 6.4 collective-permute-done.68.refs_0_
  718.6 7.1 collective-permute-done.80.refs_5_
  (465 shorter events, 433.8 us)
Async XLA Ops:
  7.2 127.4 %all-gather.6.cloned.1.call-start = ((), (), s32[]{:S(2)}) async-start(), calls=%async_computation.7 | async-start | bytes 7077888 | tf_op jit(solution)/shard_map/all_gather | solution.py:1149
  66.1 235.5 %reduce-scatter.4.cloned.1.call-start = ((), (), s32[]{:S(2)}) async-start(), calls=%async_computation.3 | async-start | bytes 5242880 | tf_op jit(solution)/shard_map/reduce_scatter | solution.py:1285
  126.4 45.6 %collective-permute-start.13 = (bf16[256,2048]{1,0:T(8,128)(2,1)}, bf16[256,2048]{1,0:T(8,128)(2,1)S(1)}, u32[]{:S(2)}, u32[]{:S(2)}) collective-permute-start(bf16[256,2048]{1,0:T(8,128)(2,1)} %shard_map.318.refs_0_), channel_id=1, source_target_pairs={{0,24},{8,16},{16,8},{24,0},{1,25},{9,17},{17,9},{25,1},{2,26},{10... | collective-permute-start | bytes 3145736 | tf_op jit(solution)/shard_map/ppermute | solution.py:1123
  129.4 43.6 %collective-permute-start.11 = (bf16[256,2048]{1,0:T(8,128)(2,1)}, bf16[256,2048]{1,0:T(8,128)(2,1)S(1)}, u32[]{:S(2)}, u32[]{:S(2)}) collective-permute-start(bf16[256,2048]{1,0:T(8,128)(2,1)} %shard_map.318.refs_0_), channel_id=1, source_target_pairs={{0,8},{8,0},{16,24},{24,16},{1,9},{9,1},{17,25},{25,17},{2,10},{10... | collective-permute-start | bytes 3145736 | tf_op jit(solution)/shard_map/ppermute | solution.py:1123
  129.7 46.9 %collective-permute-start.12 = (bf16[256,2048]{1,0:T(8,128)(2,1)}, bf16[256,2048]{1,0:T(8,128)(2,1)S(1)}, u32[]{:S(2)}, u32[]{:S(2)}) collective-permute-start(bf16[256,2048]{1,0:T(8,128)(2,1)} %shard_map.318.refs_0_), channel_id=1, source_target_pairs={{0,16},{8,24},{16,0},{24,8},{1,17},{9,25},{17,1},{25,9},{2,18},{10... | collective-permute-start | bytes 3145736 | tf_op jit(solution)/shard_map/ppermute | solution.py:1123
  199.4 39.6 %collective-permute-start.19 = (bf16[256,1408]{1,0:T(8,128)(2,1)}, bf16[256,1408]{1,0:T(8,128)(2,1)S(1)}, u32[]{:S(2)}, u32[]{:S(2)}) collective-permute-start(bf16[256,1408]{1,0:T(8,128)(2,1)} %shard_map.322.refs_2_.refs_3_), channel_id=1, source_target_pairs={{0,2},{1,3},{8,10},{9,11},{16,18},{17,19},{24,26},{25,27}} | collective-permute-start | bytes 2162696 | tf_op jit(solution)/shard_map/ppermute | solution.py:988
  202.6 36.4 %collective-permute-start.20 = (bf16[256,1408]{1,0:T(8,128)(2,1)}, bf16[256,1408]{1,0:T(8,128)(2,1)S(1)}, u32[]{:S(2)}, u32[]{:S(2)}) collective-permute-start(bf16[256,1408]{1,0:T(8,128)(2,1)} %shard_map.322.refs_2_.refs_3_), channel_id=1, source_target_pairs={{6,4},{7,5},{14,12},{15,13},{22,20},{23,21},{30,28},{31,29}} | collective-permute-start | bytes 2162696 | tf_op jit(solution)/shard_map/ppermute | solution.py:988
  206.1 33.9 %collective-permute-start.17 = (bf16[256,1408]{1,0:T(8,128)(2,1)}, bf16[256,1408]{1,0:T(8,128)(2,1)S(1)}, u32[]{:S(2)}, u32[]{:S(2)}) collective-permute-start(bf16[256,1408]{1,0:T(8,128)(2,1)} %shard_map.323.refs_9_.refs_2_.refs_3_), channel_id=1, source_target_pairs={{0,2},{1,3},{8,10},{9,11},{16,18},{17,19},{24,26},{25,27}} | collective-permute-start | bytes 2162696 | tf_op jit(solution)/shard_map/ppermute | solution.py:988
  241.2 153.3 %all-gather.4.cloned.1.call-start = ((), (), s32[]{:S(2)}) async-start(), calls=%async_computation.5 | async-start | bytes 5242880 | tf_op jit(solution)/shard_map/all_gather | solution.py:1294
  250.7 36.4 %collective-permute-start.22 = (bf16[256,1408]{1,0:T(8,128)(2,1)}, bf16[256,1408]{1,0:T(8,128)(2,1)}, u32[]{:S(2)}, u32[]{:S(2)}) collective-permute-start(bf16[256,1408]{1,0:T(8,128)(2,1)} %get-tuple-element.261.refs_3_), channel_id=1, source_target_pairs={{0,2},{1,3},{2,4},{3,5},{8,10},{9,11},{10,12},{11,13},{16,18},{17,... | collective-permute-start | bytes 2162696 | tf_op jit(solution)/shard_map/ppermute | solution.py:988
  306.8 210.9 %reduce-scatter.6.cloned.1.call-start = ((), (), s32[]{:S(2)}) async-start(), calls=%async_computation.4 | async-start | bytes 5242880 | tf_op jit(solution)/shard_map/reduce_scatter | solution.py:1297
  306.8 33.8 %collective-permute-start.28 = (bf16[256,1408]{1,0:T(8,128)(2,1)}, bf16[256,1408]{1,0:T(8,128)(2,1)}, u32[]{:S(2)}, u32[]{:S(2)}) collective-permute-start(bf16[256,1408]{1,0:T(8,128)(2,1)} %get-tuple-element.270.refs_1_), channel_id=1, source_target_pairs={{0,2},{1,3},{2,4},{3,5},{4,6},{5,7},{8,10},{9,11},{10,12},{11,13},... | collective-permute-start | bytes 2162696 | tf_op jit(solution)/shard_map/ppermute | solution.py:988
  312.2 40.7 %collective-permute-start.26 = (bf16[256,1408]{1,0:T(8,128)(2,1)S(1)}, bf16[256,1408]{1,0:T(8,128)(2,1)S(1)}, u32[]{:S(2)}, u32[]{:S(2)}) collective-permute-start(bf16[256,1408]{1,0:T(8,128)(2,1)S(1)} %copy-done.49), channel_id=1, source_target_pairs={{0,2},{1,3},{2,4},{3,5},{4,6},{5,7},{8,10},{9,11},{10,12},{11,13},... | collective-permute-start | bytes 2162696 | tf_op jit(solution)/shard_map/ppermute | solution.py:988
  316.3 36.7 %collective-permute-start.27 = (bf16[256,1408]{1,0:T(8,128)(2,1)S(1)}, bf16[256,1408]{1,0:T(8,128)(2,1)S(1)}, u32[]{:S(2)}, u32[]{:S(2)}) collective-permute-start(bf16[256,1408]{1,0:T(8,128)(2,1)S(1)} %copy-done.50), channel_id=1, source_target_pairs={{6,4},{7,5},{4,2},{5,3},{2,0},{3,1},{14,12},{15,13},{12,10},{13,11... | collective-permute-start | bytes 2162696 | tf_op jit(solution)/shard_map/ppermute | solution.py:988
  363.9 228.8 %reduce-scatter.8.cloned.1.call-start = ((), (), s32[]{:S(2)}) async-start(), calls=%async_computation.6 | async-start | bytes 5242880 | tf_op jit(solution)/shard_map/reduce_scatter | solution.py:1320
  375.2 60.4 %collective-permute-start.37 = (bf16[256,1408]{1,0:T(8,128)(2,1)}, bf16[256,1408]{1,0:T(8,128)(2,1)S(1)}, u32[]{:S(2)}, u32[]{:S(2)}) collective-permute-start(bf16[256,1408]{1,0:T(8,128)(2,1)} %get-tuple-element.295.refs_1_), channel_id=1, source_target_pairs={{0,2},{1,3},{2,4},{3,5},{4,6},{5,7},{8,10},{9,11},{10,12},{11,13},... | collective-permute-start | bytes 2162696 | tf_op jit(solution)/shard_map/ppermute | solution.py:988
  377.6 58.0 %collective-permute-start.38 = (bf16[256,1408]{1,0:T(8,128)(2,1)}, bf16[256,1408]{1,0:T(8,128)(2,1)S(1)}, u32[]{:S(2)}, u32[]{:S(2)}) collective-permute-start(bf16[256,1408]{1,0:T(8,128)(2,1)} %get-tuple-element.296.refs_2_), channel_id=1, source_target_pairs={{6,4},{7,5},{4,2},{5,3},{2,0},{3,1},{14,12},{15,13},{12,10},{13,11... | collective-permute-start | bytes 2162696 | tf_op jit(solution)/shard_map/ppermute | solution.py:988
  391.6 45.1 %collective-permute-start.35 = (bf16[256,1408]{1,0:T(8,128)(2,1)}, bf16[256,1408]{1,0:T(8,128)(2,1)S(1)}, u32[]{:S(2)}, u32[]{:S(2)}) collective-permute-start(bf16[256,1408]{1,0:T(8,128)(2,1)} %get-tuple-element.293.refs_1_), channel_id=1, source_target_pairs={{0,2},{1,3},{2,4},{3,5},{4,6},{5,7},{8,10},{9,11},{10,12},{11,13},... | collective-permute-start | bytes 2162696 | tf_op jit(solution)/shard_map/ppermute | solution.py:988
  393.2 43.5 %collective-permute-start.36 = (bf16[256,1408]{1,0:T(8,128)(2,1)}, bf16[256,1408]{1,0:T(8,128)(2,1)S(1)}, u32[]{:S(2)}, u32[]{:S(2)}) collective-permute-start(bf16[256,1408]{1,0:T(8,128)(2,1)} %get-tuple-element.294.refs_2_), channel_id=1, source_target_pairs={{6,4},{7,5},{4,2},{5,3},{2,0},{3,1},{14,12},{15,13},{12,10},{13,11... | collective-permute-start | bytes 2162696 | tf_op jit(solution)/shard_map/ppermute | solution.py:988
  441.5 37.7 %collective-permute-start.41 = (bf16[256,1408]{1,0:T(8,128)(2,1)}, bf16[256,1408]{1,0:T(8,128)(2,1)S(1)}, u32[]{:S(2)}, u32[]{:S(2)}) collective-permute-start(bf16[256,1408]{1,0:T(8,128)(2,1)} %get-tuple-element.308.refs_3_), channel_id=1, source_target_pairs={{0,2},{1,3},{2,4},{3,5},{4,6},{5,7},{8,10},{9,11},{10,12},{11,13},... | collective-permute-start | bytes 2162696 | tf_op jit(solution)/shard_map/ppermute | solution.py:988
  445.3 33.9 %collective-permute-start.42 = (bf16[256,1408]{1,0:T(8,128)(2,1)}, bf16[256,1408]{1,0:T(8,128)(2,1)S(1)}, u32[]{:S(2)}, u32[]{:S(2)}) collective-permute-start(bf16[256,1408]{1,0:T(8,128)(2,1)} %get-tuple-element.309.refs_4_), channel_id=1, source_target_pairs={{6,4},{7,5},{4,2},{5,3},{2,0},{3,1},{14,12},{15,13},{12,10},{13,11... | collective-permute-start | bytes 2162696 | tf_op jit(solution)/shard_map/ppermute | solution.py:988
  563.9 34.0 %collective-permute-start.63 = (bf16[256,1408]{1,0:T(8,128)(2,1)S(1)}, bf16[256,1408]{1,0:T(8,128)(2,1)}, u32[]{:S(2)}, u32[]{:S(2)}) collective-permute-start(bf16[256,1408]{1,0:T(8,128)(2,1)S(1)} %copy-done.39), channel_id=1, source_target_pairs={{0,1},{1,0},{2,3},{3,2},{4,5},{5,4},{6,7},{7,6},{8,9},{9,8},{10,11... | collective-permute-start | bytes 2162696 | tf_op jit(solution)/shard_map/ppermute | solution.py:1123
  597.9 33.7 %collective-permute-start.67 = (bf16[256,1408]{1,0:T(8,128)(2,1)S(1)}, bf16[256,1408]{1,0:T(8,128)(2,1)S(1)}, u32[]{:S(2)}, u32[]{:S(2)}) collective-permute-start(bf16[256,1408]{1,0:T(8,128)(2,1)S(1)} %copy-done.34), channel_id=1, source_target_pairs={{0,1},{1,0},{2,3},{3,2},{4,5},{5,4},{6,7},{7,6},{8,9},{9,8},{10,11... | collective-permute-start | bytes 2162696 | tf_op jit(solution)/shard_map/ppermute | solution.py:1123
  599.7 33.2 %collective-permute-start.71 = (bf16[256,1408]{1,0:T(8,128)(2,1)}, bf16[256,1408]{1,0:T(8,128)(2,1)}, u32[]{:S(2)}, u32[]{:S(2)}) collective-permute-start(bf16[256,1408]{1,0:T(8,128)(2,1)} %get-tuple-element.336.refs_1_.mine_ref), channel_id=1, source_target_pairs={{0,1},{1,0},{2,3},{3,2},{4,5},{5,4},{6,7},{7,6},{8,9},{9,8},{10,11... | collective-permute-start | bytes 2162696 | tf_op jit(solution)/shard_map/ppermute | solution.py:1123
  (151 other events, 1899.2 us)
Sparse Core Ops, SparseCore 0:
  66.2 68.3 all-gather.5
  241.3 60.2 reduce-scatter.3
  306.9 52.6 all-gather.3
  364.0 53.1 reduce-scatter.5
  540.8 51.3 reduce-scatter.7
